TPU v7x, 1024 devices: a whole 4x4x32 slice. The times are simulated.
1024 devices in a mesh: gx: 128 (over z, x), gy: 8 (over y, core).
Axes of the slice: x: 4, y: 4, z: 32, core: 2. Of those that a mesh axis runs over, the one named last changes fastest.
Arguments:
- adjoint_state: float32 [65536, 1536], P(('gx', 'gy')), may hold values from -6 to 6
- geometry: float32 [65536, 1536], P(('gx', 'gy')), may hold values from 0.5 to 2
- inv_mass: float32 [65536, 512], P(('gx', 'gy')), may hold values from 0.5 to 2
- profile_weight: float32 [65536, 512], P(('gx', 'gy')), may hold values from 0.2 to 10, as said below
- bin_index: int32 [65536, 512], P(('gx', 'gy')), may hold values from 0 to 127
- local_pairs: int32 [40960, 2], P(('gx', 'gy')), may hold values from 0 to 383, as said below
- remote_faces: int32 [10240, 24], P(('gx', 'gy')), may hold values from 0 to 383, as said below
Outputs:
- final_state: float32 [65536, 1536], P(('gx', 'gy'))
- profile_gradient: float32 [3, 128], replicated
Inputs may be any that keep to these rules, and one draw needn't show every extreme that they name: `local_pairs`: ids are local face ids 6 e + f of the device's own elements. A device's 40 pairs and its 10 x 24 slots name distinct faces. `remote_faces`: row r of a device's block lists faces shared with its partner at level r; slot k meets the partner's slot k of the same row. Ids are local face ids, distinct from each other and from the device's pair faces. `profile_weight`: weights are positive.
All inputs are finite; a program needn't handle non-finite values.
Results may differ from a plain program's by a relative error of at most 0.0003.
Values sent between devices are 32-bit elements; how exact they have to be, the bound alone decides.
No kernel may reach another device: no remote copies, remote signals or barrier semaphores. Data moves between devices by JAX's collectives and lax.ppermute only.
A program may use at most 32 MiB of HBM per device.

v0:
```python
import math

import jax
import jax.numpy as jnp
from jax import lax
from jax.sharding import PartitionSpec as P

NBIN = 128
STEPS = 2


precise = lax.Precision.HIGHEST
step_size = 0.00015


def from_partner(value, axis, distance):
    mask = 2**distance
    pairs = [(source, source ^ mask) for source in range(lax.axis_size(axis))]
    return lax.ppermute(value, axis, pairs)


def cheb_matrix():
    points = jnp.arange(8)
    nodes = jnp.cos(math.pi * points.astype(jnp.float32) / 7.0)
    weights = jnp.where((points == 0) | (points == 7), 2.0, 1.0).astype(jnp.float32)
    parity = jnp.where((points[:, None] + points[None, :]) % 2 == 0, 1.0, -1.0).astype(jnp.float32)
    spacing = nodes[:, None] - nodes[None, :]
    diagonal_mask = points[:, None] == points[None, :]
    divisor = jnp.where(diagonal_mask, 1.0, spacing)
    offdiag = jnp.where(diagonal_mask, 0.0, weights[:, None] / weights[None, :] * parity / divisor)
    return offdiag - jnp.diag(jnp.sum(offdiag, axis=1))


def lane_operators(derivative):
    eye_eight = jnp.eye(8, dtype=jnp.float32)
    last_matrix = jnp.kron(jnp.eye(16, dtype=jnp.float32), derivative.T)
    middle_matrix = jnp.kron(jnp.kron(jnp.eye(2, dtype=jnp.float32), derivative.T), eye_eight)
    lane_forward = jnp.concatenate([last_matrix, middle_matrix], axis=1)
    lane_back = jnp.concatenate([last_matrix.T, middle_matrix.T], axis=0)
    depth_matrix = jnp.kron(derivative.T, jnp.eye(64, dtype=jnp.float32))
    return (lane_forward, lane_back, depth_matrix)


def face_table():
    within = jnp.arange(64, dtype=jnp.int32)
    upper = within // 8
    lower = within % 8
    targets = jnp.concatenate(
        [
            within,
            448 + within,
            upper * 64 + lower,
            upper * 64 + 56 + lower,
            upper * 64 + lower * 8,
            upper * 64 + lower * 8 + 7,
        ]
    )
    return (jnp.arange(512, dtype=jnp.int32)[:, None] == targets[None, :]).astype(jnp.float32)


def stiffness(flat, geometry, operators):
    lane_forward, lane_back, depth_matrix = operators
    count = geometry.shape[0]
    lane_grads = jnp.dot(
        flat.reshape(count * 12, 128),
        lane_forward,
        precision=precise,
        preferred_element_type=jnp.float32,
    ).reshape(count, 3, 4, 256)
    metric_last = geometry[:, 1024:].reshape(count, 4, 128)
    metric_middle = geometry[:, 512:1024].reshape(count, 4, 128)
    lane_metric = jnp.concatenate([metric_last, metric_middle], axis=-1)
    lane_scaled = (lane_grads * lane_metric[:, None]).reshape(count * 12, 256)
    lane_part = jnp.dot(
        lane_scaled, lane_back, precision=precise, preferred_element_type=jnp.float32
    )
    depth_grads = jnp.dot(
        flat, depth_matrix, precision=precise, preferred_element_type=jnp.float32
    ).reshape(count, 3, 512)
    depth_scaled = (depth_grads * geometry[:, None, :512]).reshape(count * 3, 512)
    depth_part = jnp.dot(
        depth_scaled, depth_matrix.T, precision=precise, preferred_element_type=jnp.float32
    )
    return depth_part + lane_part.reshape(count * 3, 512)


def binned(state, profile_weight, bin_index):
    count = profile_weight.shape[0]
    weighted = (profile_weight[:, None, :] * state.reshape(count, 3, 512)).transpose(1, 0, 2)
    weighted = weighted.reshape(3, count * 512)
    labels = bin_index.reshape(1, count * 512)
    upper_count = NBIN // 16
    upper_mask = (jnp.arange(upper_count, dtype=jnp.int32)[:, None] == labels // 16).astype(
        jnp.float32
    )
    lower_mask = (jnp.arange(16, dtype=jnp.int32)[:, None] == labels % 16).astype(jnp.float32)
    left = (weighted[:, None, :] * upper_mask[None]).reshape(3 * upper_count, count * 512)
    summed = lax.dot_general(
        left,
        lower_mask,
        (((1,), (1,)), ((), ())),
        precision=precise,
        preferred_element_type=jnp.float32,
    )
    return summed.reshape(3, NBIN)


def route_panels(outgoing, gx_bits, gy_bits):
    pieces = []
    for bit_index in range(gx_bits):
        pieces.append(from_partner(outgoing[bit_index], "gx", bit_index))
    for bit_index in range(gy_bits):
        pieces.append(from_partner(outgoing[gx_bits + bit_index], "gy", bit_index))
    return jnp.stack(pieces)


def on_device(
    adjoint_state, geometry, inv_mass, profile_weight, bin_index, local_pairs, remote_faces
):
    derivative = cheb_matrix()
    operators = lane_operators(derivative)
    selector = face_table()
    count = adjoint_state.shape[0]
    levels, slots = remote_faces.shape
    gx_bits = lax.axis_size("gx").bit_length() - 1
    gy_bits = lax.axis_size("gy").bit_length() - 1
    current = adjoint_state.reshape(count * 3, 512)
    gradient = jnp.zeros((3, NBIN), jnp.float32)
    for section in range(STEPS):
        stiff = stiffness(current, geometry, operators)
        face_values = jnp.dot(
            stiff, selector, precision=precise, preferred_element_type=jnp.float32
        )
        panels = face_values.reshape(count, 3, 6, 64).transpose(0, 2, 1, 3).reshape(count * 6, 192)
        outgoing = panels[remote_faces].reshape(levels, slots * 192)
        received = route_panels(outgoing, gx_bits, gy_bits)
        assembly = jnp.zeros_like(panels)
        assembly = assembly.at[local_pairs[:, 0]].add(panels[local_pairs[:, 1]])
        assembly = assembly.at[local_pairs[:, 1]].add(panels[local_pairs[:, 0]])
        assembly = assembly.at[remote_faces.reshape(-1)].add(received.reshape(levels * slots, 192))
        returned = assembly.reshape(count, 6, 3, 64).transpose(0, 2, 1, 3).reshape(count * 3, 384)
        assembled = stiff + jnp.dot(
            returned, selector.T, precision=precise, preferred_element_type=jnp.float32
        )
        update = inv_mass[:, None, :] * assembled.reshape(count, 3, 512)
        current = current - step_size * update.reshape(count * 3, 512)
        gradient = gradient + lax.psum(binned(current, profile_weight, bin_index), ("gx", "gy"))
    scaling = 1.0 / math.sqrt(count * lax.axis_size("gx") * lax.axis_size("gy") * 512 / NBIN)
    return (current.reshape(count, 3 * 512), gradient * scaling)


def solution(mesh):
    in_specs = (
        P(("gx", "gy"), None),
        P(("gx", "gy"), None),
        P(("gx", "gy"), None),
        P(("gx", "gy"), None),
        P(("gx", "gy"), None),
        P(("gx", "gy"), None),
        P(("gx", "gy"), None),
    )
    out_specs = (P(("gx", "gy"), None), P())
    return jax.shard_map(
        on_device, mesh=mesh, in_specs=in_specs, out_specs=out_specs, check_vma=False
    )
```

profile of v0, /device:TPU:1, one launch (start us, length us, event | category | flops | bytes accessed | tf_op | source)
XLA Modules:
  0.0 365.4 jit_solution(12814397023828478436)
XLA Ops:
  25.3 2.3 copy.19
  37.5 3.9 %collective-permute-start = (f32[4608]{0:T(1024)}, f32[4608]{0:T(1024)}, u32[]{:S(2)}, u32[]{:S(2)}) collective-permute-start(f32[4608]{0:T(1024)} %squeeze.68), channel_id=1, source_target_pairs={{0,8},{8,0},{16,24},{24,16},{32,40},{40,32},{48,56},{56,48},{64,72... | collective-permute-start | bytes 55304 | tf_op jit(solution)/shard_map/ppermute | solution.py:19
  42.8 4.4 %collective-permute-start.1 = (f32[4608]{0:T(1024)}, f32[4608]{0:T(1024)}, u32[]{:S(2)}, u32[]{:S(2)}) collective-permute-start(f32[4608]{0:T(1024)} %squeeze.69), channel_id=1, source_target_pairs={{0,16},{8,24},{16,0},{24,8},{32,48},{40,56},{48,32},{56,40},{64,80... | collective-permute-start | bytes 55304 | tf_op jit(solution)/shard_map/ppermute | solution.py:19
  48.6 3.5 collective-permute-start.2
  53.6 4.9 %collective-permute-start.3 = (f32[4608]{0:T(1024)}, f32[4608]{0:T(1024)}, u32[]{:S(2)}, u32[]{:S(2)}) collective-permute-start(f32[4608]{0:T(1024)} %squeeze.71), channel_id=1, source_target_pairs={{0,64},{8,72},{16,80},{24,88},{32,96},{40,104},{48,112},{56,120},{... | collective-permute-start | bytes 55304 | tf_op jit(solution)/shard_map/ppermute | solution.py:19
  59.9 8.8 %collective-permute-start.4 = (f32[4608]{0:T(1024)}, f32[4608]{0:T(1024)}, u32[]{:S(2)}, u32[]{:S(2)}) collective-permute-start(f32[4608]{0:T(1024)} %squeeze.72), channel_id=1, source_target_pairs={{0,128},{8,136},{16,144},{24,152},{32,160},{40,168},{48,176},{56,1... | collective-permute-start | bytes 55304 | tf_op jit(solution)/shard_map/ppermute | solution.py:19
  77.1 15.4 %collective-permute-start.5 = (f32[4608]{0:T(1024)}, f32[4608]{0:T(1024)}, u32[]{:S(2)}, u32[]{:S(2)}) collective-permute-start(f32[4608]{0:T(1024)} %squeeze.73), channel_id=1, source_target_pairs={{0,256},{8,264},{16,272},{24,280},{32,288},{40,296},{48,304},{56,3... | collective-permute-start | bytes 55304 | tf_op jit(solution)/shard_map/ppermute | solution.py:19
  92.5 11.6 %collective-permute-start.6 = (f32[4608]{0:T(1024)}, f32[4608]{0:T(1024)}, u32[]{:S(2)}, u32[]{:S(2)}) collective-permute-start(f32[4608]{0:T(1024)} %squeeze.74), channel_id=1, source_target_pairs={{0,512},{8,520},{16,528},{24,536},{32,544},{40,552},{48,560},{56,5... | collective-permute-start | bytes 55304 | tf_op jit(solution)/shard_map/ppermute | solution.py:19
  104.1 4.5 %collective-permute-start.7 = (f32[4608]{0:T(1024)}, f32[4608]{0:T(1024)}, u32[]{:S(2)}, u32[]{:S(2)}) collective-permute-start(f32[4608]{0:T(1024)} %squeeze.75), channel_id=1, source_target_pairs={{0,1},{1,0},{2,3},{3,2},{4,5},{5,4},{6,7},{7,6},{8,9},{9,8},{10,11... | collective-permute-start | bytes 55304 | tf_op jit(solution)/shard_map/ppermute | solution.py:19
  108.7 3.2 collective-permute-start.8
  111.9 4.5 %collective-permute-start.9 = (f32[4608]{0:T(1024)}, f32[4608]{0:T(1024)}, u32[]{:S(2)}, u32[]{:S(2)}) collective-permute-start(f32[4608]{0:T(1024)} %squeeze.77), channel_id=1, source_target_pairs={{0,4},{1,5},{2,6},{3,7},{4,0},{5,1},{6,2},{7,3},{8,12},{9,13},{10,... | collective-permute-start | bytes 55304 | tf_op jit(solution)/shard_map/ppermute | solution.py:19
  135.3 2.1 reshape.628
  152.3 3.3 collective-permute-start.11
  155.6 2.6 collective-permute-start.12
  158.3 3.1 collective-permute-start.13
  161.5 5.2 %collective-permute-start.14 = (f32[4608]{0:T(1024)S(1)}, f32[4608]{0:T(1024)S(1)}, u32[]{:S(2)}, u32[]{:S(2)}) collective-permute-start(f32[4608]{0:T(1024)S(1)} %squeeze.82), channel_id=1, source_target_pairs={{0,128},{8,136},{16,144},{24,152},{32,160},{40,168},{48,176},{56,1... | collective-permute-start | bytes 55304 | tf_op jit(solution)/shard_map/ppermute | solution.py:19
  167.2 8.2 %collective-permute-start.15 = (f32[4608]{0:T(1024)S(1)}, f32[4608]{0:T(1024)S(1)}, u32[]{:S(2)}, u32[]{:S(2)}) collective-permute-start(f32[4608]{0:T(1024)S(1)} %squeeze.83), channel_id=1, source_target_pairs={{0,256},{8,264},{16,272},{24,280},{32,288},{40,296},{48,304},{56,3... | collective-permute-start | bytes 55304 | tf_op jit(solution)/shard_map/ppermute | solution.py:19
  175.4 3.7 %collective-permute-start.16 = (f32[4608]{0:T(1024)S(1)}, f32[4608]{0:T(1024)S(1)}, u32[]{:S(2)}, u32[]{:S(2)}) collective-permute-start(f32[4608]{0:T(1024)S(1)} %squeeze.84), channel_id=1, source_target_pairs={{0,512},{8,520},{16,528},{24,536},{32,544},{40,552},{48,560},{56,5... | collective-permute-start | bytes 55304 | tf_op jit(solution)/shard_map/ppermute | solution.py:19
  179.1 3.9 %collective-permute-start.17 = (f32[4608]{0:T(1024)S(1)}, f32[4608]{0:T(1024)S(1)}, u32[]{:S(2)}, u32[]{:S(2)}) collective-permute-start(f32[4608]{0:T(1024)S(1)} %squeeze.85), channel_id=1, source_target_pairs={{0,1},{1,0},{2,3},{3,2},{4,5},{5,4},{6,7},{7,6},{8,9},{9,8},{10,11... | collective-permute-start | bytes 55304 | tf_op jit(solution)/shard_map/ppermute | solution.py:19
  182.9 3.6 collective-permute-start.18
  186.6 5.8 %collective-permute-start.19 = (f32[4608]{0:T(1024)S(1)}, f32[4608]{0:T(1024)S(1)}, u32[]{:S(2)}, u32[]{:S(2)}) collective-permute-start(f32[4608]{0:T(1024)S(1)} %squeeze.87), channel_id=1, source_target_pairs={{0,4},{1,5},{2,6},{3,7},{4,0},{5,1},{6,2},{7,3},{8,12},{9,13},{10,... | collective-permute-start | bytes 55304 | tf_op jit(solution)/shard_map/ppermute | solution.py:19
  196.2 2.4 collective-permute-done.16
  207.8 2.2 fusion.18
  210.2 154.6 %psum.16 = f32[3,128]{1,0:T(4,128)S(1)} all-reduce(f32[3,128]{1,0:T(4,128)S(1)} %reshape.782), channel_id=1, replica_groups=mesh['gx'=128,'gy'=8] {'gx','gy'}, use_global_device_ids=true, to_apply=%region_7.8 | all-reduce | flops 384 | bytes 3072 | tf_op jit(solution)/shard_map/psum | solution.py:147
  (200 shorter events, 96.1 us)
Async XLA Ops:
  3.4 14.0 %copy-start.3 = (f32[192,512]{1,0:T(8,128)}, f32[192,512]{1,0:T(8,128)S(1)}, u32[]{:S(2)}) copy-start(f32[192,512]{1,0:T(8,128)S(1)} %reshape.619) | copy-start | bytes 1179652
  22.0 7.7 %copy-start.19 = (s32[10,24]{1,0:T(8,128)S(1)}, s32[10,24]{1,0:T(8,128)}, u32[]{:S(2)}) copy-start(s32[10,24]{1,0:T(8,128)} %param.13) | copy-start | bytes 2884
  37.5 39.6 %collective-permute-start = (f32[4608]{0:T(1024)}, f32[4608]{0:T(1024)}, u32[]{:S(2)}, u32[]{:S(2)}) collective-permute-start(f32[4608]{0:T(1024)} %squeeze.68), channel_id=1, source_target_pairs={{0,8},{8,0},{16,24},{24,16},{32,40},{40,32},{48,56},{56,48},{64,72... | collective-permute-start | bytes 55304 | tf_op jit(solution)/shard_map/ppermute | solution.py:19
  42.8 49.7 %collective-permute-start.1 = (f32[4608]{0:T(1024)}, f32[4608]{0:T(1024)}, u32[]{:S(2)}, u32[]{:S(2)}) collective-permute-start(f32[4608]{0:T(1024)} %squeeze.69), channel_id=1, source_target_pairs={{0,16},{8,24},{16,0},{24,8},{32,48},{40,56},{48,32},{56,40},{64,80... | collective-permute-start | bytes 55304 | tf_op jit(solution)/shard_map/ppermute | solution.py:19
  48.6 55.5 %collective-permute-start.2 = (f32[4608]{0:T(1024)}, f32[4608]{0:T(1024)}, u32[]{:S(2)}, u32[]{:S(2)}) collective-permute-start(f32[4608]{0:T(1024)} %squeeze.70), channel_id=1, source_target_pairs={{0,32},{8,40},{16,48},{24,56},{32,0},{40,8},{48,16},{56,24},{64,96... | collective-permute-start | bytes 55304 | tf_op jit(solution)/shard_map/ppermute | solution.py:19
  53.6 55.1 %collective-permute-start.3 = (f32[4608]{0:T(1024)}, f32[4608]{0:T(1024)}, u32[]{:S(2)}, u32[]{:S(2)}) collective-permute-start(f32[4608]{0:T(1024)} %squeeze.71), channel_id=1, source_target_pairs={{0,64},{8,72},{16,80},{24,88},{32,96},{40,104},{48,112},{56,120},{... | collective-permute-start | bytes 55304 | tf_op jit(solution)/shard_map/ppermute | solution.py:19
  59.9 52.0 %collective-permute-start.4 = (f32[4608]{0:T(1024)}, f32[4608]{0:T(1024)}, u32[]{:S(2)}, u32[]{:S(2)}) collective-permute-start(f32[4608]{0:T(1024)} %squeeze.72), channel_id=1, source_target_pairs={{0,128},{8,136},{16,144},{24,152},{32,160},{40,168},{48,176},{56,1... | collective-permute-start | bytes 55304 | tf_op jit(solution)/shard_map/ppermute | solution.py:19
  77.1 50.7 %collective-permute-start.5 = (f32[4608]{0:T(1024)}, f32[4608]{0:T(1024)}, u32[]{:S(2)}, u32[]{:S(2)}) collective-permute-start(f32[4608]{0:T(1024)} %squeeze.73), channel_id=1, source_target_pairs={{0,256},{8,264},{16,272},{24,280},{32,288},{40,296},{48,304},{56,3... | collective-permute-start | bytes 55304 | tf_op jit(solution)/shard_map/ppermute | solution.py:19
  92.5 36.0 %collective-permute-start.6 = (f32[4608]{0:T(1024)}, f32[4608]{0:T(1024)}, u32[]{:S(2)}, u32[]{:S(2)}) collective-permute-start(f32[4608]{0:T(1024)} %squeeze.74), channel_id=1, source_target_pairs={{0,512},{8,520},{16,528},{24,536},{32,544},{40,552},{48,560},{56,5... | collective-permute-start | bytes 55304 | tf_op jit(solution)/shard_map/ppermute | solution.py:19
  104.1 25.2 %collective-permute-start.7 = (f32[4608]{0:T(1024)}, f32[4608]{0:T(1024)}, u32[]{:S(2)}, u32[]{:S(2)}) collective-permute-start(f32[4608]{0:T(1024)} %squeeze.75), channel_id=1, source_target_pairs={{0,1},{1,0},{2,3},{3,2},{4,5},{5,4},{6,7},{7,6},{8,9},{9,8},{10,11... | collective-permute-start | bytes 55304 | tf_op jit(solution)/shard_map/ppermute | solution.py:19
  108.7 21.4 %collective-permute-start.8 = (f32[4608]{0:T(1024)}, f32[4608]{0:T(1024)}, u32[]{:S(2)}, u32[]{:S(2)}) collective-permute-start(f32[4608]{0:T(1024)} %squeeze.76), channel_id=1, source_target_pairs={{0,2},{1,3},{2,0},{3,1},{4,6},{5,7},{6,4},{7,5},{8,10},{9,11},{10,... | collective-permute-start | bytes 55304 | tf_op jit(solution)/shard_map/ppermute | solution.py:19
  111.9 18.9 %collective-permute-start.9 = (f32[4608]{0:T(1024)}, f32[4608]{0:T(1024)}, u32[]{:S(2)}, u32[]{:S(2)}) collective-permute-start(f32[4608]{0:T(1024)} %squeeze.77), channel_id=1, source_target_pairs={{0,4},{1,5},{2,6},{3,7},{4,0},{5,1},{6,2},{7,3},{8,12},{9,13},{10,... | collective-permute-start | bytes 55304 | tf_op jit(solution)/shard_map/ppermute | solution.py:19
  119.8 17.6 %copy-start.1 = (f32[192,512]{1,0:T(8,128)}, f32[192,512]{1,0:T(8,128)S(1)}, u32[]{:S(2)}) copy-start(f32[192,512]{1,0:T(8,128)S(1)} %mul.257) | copy-start | bytes 1179652
  148.8 17.9 %copy-start.15 = (s32[8,4,8,128]{3,1,2,0:T(4,128)S(1)}, s32[8,4,8,128]{3,1,2,0:T(4,128)}, u32[]{:S(2)}) copy-start(s32[8,4,8,128]{3,1,2,0:T(4,128)} %copy.33) | copy-start | bytes 393220
  150.3 16.9 %collective-permute-start.10 = (f32[4608]{0:T(1024)S(1)}, f32[4608]{0:T(1024)S(1)}, u32[]{:S(2)}, u32[]{:S(2)}) collective-permute-start(f32[4608]{0:T(1024)S(1)} %squeeze.78), channel_id=1, source_target_pairs={{0,8},{8,0},{16,24},{24,16},{32,40},{40,32},{48,56},{56,48},{64,72... | collective-permute-start | bytes 55304 | tf_op jit(solution)/shard_map/ppermute | solution.py:19
  152.3 23.1 %collective-permute-start.11 = (f32[4608]{0:T(1024)S(1)}, f32[4608]{0:T(1024)S(1)}, u32[]{:S(2)}, u32[]{:S(2)}) collective-permute-start(f32[4608]{0:T(1024)S(1)} %squeeze.79), channel_id=1, source_target_pairs={{0,16},{8,24},{16,0},{24,8},{32,48},{40,56},{48,32},{56,40},{64,80... | collective-permute-start | bytes 55304 | tf_op jit(solution)/shard_map/ppermute | solution.py:19
  155.6 23.4 %collective-permute-start.12 = (f32[4608]{0:T(1024)S(1)}, f32[4608]{0:T(1024)S(1)}, u32[]{:S(2)}, u32[]{:S(2)}) collective-permute-start(f32[4608]{0:T(1024)S(1)} %squeeze.80), channel_id=1, source_target_pairs={{0,32},{8,40},{16,48},{24,56},{32,0},{40,8},{48,16},{56,24},{64,96... | collective-permute-start | bytes 55304 | tf_op jit(solution)/shard_map/ppermute | solution.py:19
  158.3 24.6 %collective-permute-start.13 = (f32[4608]{0:T(1024)S(1)}, f32[4608]{0:T(1024)S(1)}, u32[]{:S(2)}, u32[]{:S(2)}) collective-permute-start(f32[4608]{0:T(1024)S(1)} %squeeze.81), channel_id=1, source_target_pairs={{0,64},{8,72},{16,80},{24,88},{32,96},{40,104},{48,112},{56,120},{... | collective-permute-start | bytes 55304 | tf_op jit(solution)/shard_map/ppermute | solution.py:19
  161.5 25.1 %collective-permute-start.14 = (f32[4608]{0:T(1024)S(1)}, f32[4608]{0:T(1024)S(1)}, u32[]{:S(2)}, u32[]{:S(2)}) collective-permute-start(f32[4608]{0:T(1024)S(1)} %squeeze.82), channel_id=1, source_target_pairs={{0,128},{8,136},{16,144},{24,152},{32,160},{40,168},{48,176},{56,1... | collective-permute-start | bytes 55304 | tf_op jit(solution)/shard_map/ppermute | solution.py:19
  167.2 29.0 %collective-permute-start.15 = (f32[4608]{0:T(1024)S(1)}, f32[4608]{0:T(1024)S(1)}, u32[]{:S(2)}, u32[]{:S(2)}) collective-permute-start(f32[4608]{0:T(1024)S(1)} %squeeze.83), channel_id=1, source_target_pairs={{0,256},{8,264},{16,272},{24,280},{32,288},{40,296},{48,304},{56,3... | collective-permute-start | bytes 55304 | tf_op jit(solution)/shard_map/ppermute | solution.py:19
  175.4 23.2 %collective-permute-start.16 = (f32[4608]{0:T(1024)S(1)}, f32[4608]{0:T(1024)S(1)}, u32[]{:S(2)}, u32[]{:S(2)}) collective-permute-start(f32[4608]{0:T(1024)S(1)} %squeeze.84), channel_id=1, source_target_pairs={{0,512},{8,520},{16,528},{24,536},{32,544},{40,552},{48,560},{56,5... | collective-permute-start | bytes 55304 | tf_op jit(solution)/shard_map/ppermute | solution.py:19
  179.1 19.6 %collective-permute-start.17 = (f32[4608]{0:T(1024)S(1)}, f32[4608]{0:T(1024)S(1)}, u32[]{:S(2)}, u32[]{:S(2)}) collective-permute-start(f32[4608]{0:T(1024)S(1)} %squeeze.85), channel_id=1, source_target_pairs={{0,1},{1,0},{2,3},{3,2},{4,5},{5,4},{6,7},{7,6},{8,9},{9,8},{10,11... | collective-permute-start | bytes 55304 | tf_op jit(solution)/shard_map/ppermute | solution.py:19
  182.9 15.7 %collective-permute-start.18 = (f32[4608]{0:T(1024)S(1)}, f32[4608]{0:T(1024)S(1)}, u32[]{:S(2)}, u32[]{:S(2)}) collective-permute-start(f32[4608]{0:T(1024)S(1)} %squeeze.86), channel_id=1, source_target_pairs={{0,2},{1,3},{2,0},{3,1},{4,6},{5,7},{6,4},{7,5},{8,10},{9,11},{10,... | collective-permute-start | bytes 55304 | tf_op jit(solution)/shard_map/ppermute | solution.py:19
  186.6 12.1 %collective-permute-start.19 = (f32[4608]{0:T(1024)S(1)}, f32[4608]{0:T(1024)S(1)}, u32[]{:S(2)}, u32[]{:S(2)}) collective-permute-start(f32[4608]{0:T(1024)S(1)} %squeeze.87), channel_id=1, source_target_pairs={{0,4},{1,5},{2,6},{3,7},{4,0},{5,1},{6,2},{7,3},{8,12},{9,13},{10,... | collective-permute-start | bytes 55304 | tf_op jit(solution)/shard_map/ppermute | solution.py:19
  (18 other events, 59.1 us)
where the time goes:
time: 368 us; the launch traced here: 365 us
  blocking collectives  155 us (42%)
  starting transfers between devices  106 us (29%)
  local copies, waits for them, and re-layouts  63.7 us (17%)
  matrix products  19.5 us (5%)
  other arithmetic  17.6 us (5%)
    psum x1, blocking collectives, on_device(): lax.psum(binned(current, profile_weight, bin_index), ('gx', 'gy'))  155 us
    ppermute x20, starting transfers between devices, from_partner(): return lax.ppermute(value, axis, pairs)  106 us
    squeeze x14, local copies, waits for them, and re-layouts, route_panels(): pieces.append(from_partner(outgoing[bit_index], 'gx', bit_index))  10.4 us
    another operation x22, local copies, waits for them, and re-layouts, route_panels(): return jnp.stack(pieces)  8.13 us
  transfers between devices with their start and end apart: 20, of which 1 were waited for; matrix products, arithmetic and copies ran while one was open for 9% of the time, Pallas kernels for 0%

commit v1 on v0

v1 whole, which is shorter than its diff:
```python
import functools
import math

import jax
import jax.numpy as jnp
import numpy as np
from jax import lax
from jax.experimental import pallas as pl
from jax.experimental.pallas import tpu as pltpu
from jax.sharding import Mesh
from jax.sharding import PartitionSpec as P

NBIN = 128
STEP = 0.00015
E = 64
K = 24
F32 = jnp.float32
BF16 = jnp.bfloat16
VM = pltpu.VMEM


def cheb():
    m = np.arange(8)
    x = np.cos(np.pi * m / 7.0)
    c = np.where((m == 0) | (m == 7), 2.0, 1.0)
    sign = np.where((m[:, None] + m[None, :]) % 2 == 0, 1.0, -1.0)
    same = m[:, None] == m[None, :]
    gap = np.where(same, 1.0, x[:, None] - x[None, :])
    off = np.where(same, 0.0, c[:, None] / c[None, :] * sign / gap)
    return off - np.diag(off.sum(axis=1))


def split_const(a):
    hi = a.astype(np.float32).astype(jnp.bfloat16)
    lo = (a - hi.astype(np.float64)).astype(np.float32).astype(jnp.bfloat16)
    return hi, lo


def constants():
    d = cheb()
    last = np.kron(np.eye(16), d.T)
    middle = np.kron(np.kron(np.eye(2), d.T), np.eye(8))
    fh, fl = split_const(np.concatenate([last, middle], axis=1))
    forward = np.concatenate([fh, fh, fl], axis=0)
    bh, bl = split_const(np.concatenate([last.T, middle.T], axis=0))
    back = np.concatenate([bh, bl], axis=1)
    rows = []
    for mat in (d, d.T):
        for cross in (0, 1):
            for out in range(4):
                for src in range(4):
                    low = mat[2 * out, 2 * src + cross]
                    high = mat[2 * out + 1, 2 * src + 1 - cross]
                    rows.append(np.repeat([low, high], 64))
    coef = np.stack(rows).astype(np.float32)
    p = np.arange(64)
    u, l = p // 8, p % 8
    targets = np.concatenate(
        [p, 448 + p, u * 64 + l, u * 64 + 56 + l, u * 64 + l * 8, u * 64 + l * 8 + 7]
    )
    sel = np.arange(512)[:, None] == targets[None, :]
    sel = sel.astype(np.float32).astype(jnp.bfloat16)
    return forward, back, coef, sel, np.ascontiguousarray(sel.T)


def split(x):
    hi = x.astype(BF16)
    return hi, (x - hi.astype(F32)).astype(BF16)


def dot(a, b):
    return lax.dot_general(a, b, (((1,), (0,)), ((), ())), preferred_element_type=F32)


def thrice(x):
    return jnp.concatenate([x, x, x], axis=0)


def stiffness(x, geo, fwd, back, coef):
    quads = [x[:, 128 * q : 128 * q + 128] for q in range(4)]
    rows = jnp.concatenate(quads, axis=0)
    hi, lo = split(rows)
    grads = dot(jnp.concatenate([hi, lo], axis=1), fwd[0:256, :]) + dot(hi, fwd[256:384, :])
    scaled = []
    for q in range(4):
        metric = jnp.concatenate(
            [
                geo[:, 1024 + 128 * q : 1152 + 128 * q],
                geo[:, 512 + 128 * q : 640 + 128 * q],
            ],
            axis=1,
        )
        scaled.append(grads[192 * q : 192 * q + 192] * thrice(metric))
    hi, lo = split(jnp.concatenate(scaled, axis=0))
    both = dot(hi, back[...])
    lanes = both[:, :128] + both[:, 128:] + dot(lo, back[:, 0:128])
    out = []
    for part in range(6):
        lo_row = 32 * part
        e0 = lo_row % 64
        xs = [q[lo_row : lo_row + 32] for q in quads]
        rolled = [pltpu.roll(v, 64, 1) for v in xs]
        mids = []
        for o in range(4):
            acc = None
            for s in range(4):
                r = 4 * o + s
                term = coef[r : r + 1, :] * xs[s] + coef[16 + r : 17 + r, :] * rolled[s]
                acc = term if acc is None else acc + term
            mids.append(acc * geo[e0 : e0 + 32, 128 * o : 128 * o + 128])
        rolled = [pltpu.roll(v, 64, 1) for v in mids]
        cols = []
        for o in range(4):
            base = 192 * o + lo_row
            acc = lanes[base : base + 32]
            for s in range(4):
                r = 32 + 4 * o + s
                acc = acc + coef[r : r + 1, :] * mids[s] + coef[16 + r : 17 + r, :] * rolled[s]
            cols.append(acc)
        out.append(jnp.concatenate(cols, axis=1))
    return jnp.concatenate(out, axis=0)


def store_panels(stiff, extra, sel, pm):
    hi, lo = split(stiff)
    stack = [hi, lo]
    if extra is not None:
        weight, bins = extra
        stack += [*split(weight), bins.astype(BF16)]
    got = dot(jnp.concatenate(stack, axis=0), sel[...])
    face = got[0:192] + got[192:384]
    if extra is not None:
        wface = got[384:448] + got[448:512]
        bface = got[512:576]
    zero = jnp.zeros((E, 64), F32)
    for f in range(6):
        cut = slice(64 * f, 64 * f + 64)
        c0, c1, c2 = (face[64 * c : 64 * c + 64, cut] for c in range(3))
        third = zero if extra is None else wface[:, cut]
        pm[0][pl.ds(f, E, stride=6), :] = jnp.concatenate([c0, c1], axis=1)
        pm[1][pl.ds(f, E, stride=6), :] = jnp.concatenate([c2, third], axis=1)
        if extra is not None:
            pm[2][pl.ds(f, E, stride=6), :] = jnp.concatenate([bface[:, cut], zero], axis=1)


def send_rows(remote, me, levels, pm, out_near, out_far):
    for r, (kind, where) in enumerate(levels):
        for k in range(K):
            face = remote[r, k]
            for i, block in enumerate(pm):
                row, lanes = block[pl.ds(face, 1), :], slice(128 * i, 128 * i + 128)
                if kind == "near":
                    out_near[me[0] ^ where, k : k + 1, lanes] = row
                else:
                    out_far[where][k : k + 1, lanes] = row


def take_rows(remote, me, levels, near, far, asm):
    for r, (kind, where) in enumerate(levels):
        for k in range(K):
            face = remote[r, k]
            for i, block in enumerate(asm):
                lanes = slice(128 * i, 128 * i + 128)
                if kind == "near":
                    row = near[me[0] ^ where, k : k + 1, lanes]
                else:
                    row = far[where][k : k + 1, lanes]
                block[pl.ds(face, 1), :] = row


def pair_rows(pairs, pm, asm):
    for i in range(pairs.shape[0]):
        a, b = pairs[i, 0], pairs[i, 1]
        for source, block in zip(pm, asm):
            block[pl.ds(b, 1), :] = source[pl.ds(a, 1), :]
            block[pl.ds(a, 1), :] = source[pl.ds(b, 1), :]


def lift(asm, selt):
    faces = []
    for f in range(6):
        one = asm[0][pl.ds(f, E, stride=6), :]
        two = asm[1][pl.ds(f, E, stride=6), :]
        faces.append(jnp.concatenate([one[:, 0:64], one[:, 64:128], two[:, 0:64]], axis=0))
    hi, lo = split(jnp.concatenate(faces, axis=1))
    got = dot(jnp.concatenate([hi, lo], axis=0), selt[...])
    return got[0:192] + got[192:384]


def bin_dot(ws, bins):
    groups = bins.shape[0] // 8
    left, right = [], []
    for g in range(groups):
        cut = slice(8 * g, 8 * g + 8)
        b = bins[cut]
        upper, lower = b >> 5, b & 31
        masks = [upper == u for u in range(4)]
        rows = [jnp.where(m, w[cut], 0.0) for w in ws for m in masks]
        left.append(jnp.concatenate(rows, axis=0))
        ones = [jnp.where(lower == v, 1.0, 0.0) for v in range(32)]
        right.append(jnp.concatenate(ones, axis=0).astype(BF16))
    hi, lo = split(jnp.concatenate(left, axis=1))
    return lax.dot_general(
        jnp.concatenate([hi, lo], axis=0),
        jnp.concatenate(right, axis=1),
        (((1,), (1,)), ((), ())),
        preferred_element_type=F32,
    )


def bin_finish(acc):
    row = lax.broadcasted_iota(jnp.int32, (192, 256), 0)
    col = lax.broadcasted_iota(jnp.int32, (192, 256), 1)
    acc = jnp.where((row & 7) == (col & 7), acc, 0.0)
    summed = jnp.sum(acc.reshape(24, 8, 256), axis=1)
    r = lax.broadcasted_iota(jnp.int32, (256, 128), 0)
    c = lax.broadcasted_iota(jnp.int32, (256, 128), 1)
    put = jnp.where((r >> 3) + 64 == c, 1.0, 0.0)
    summed = summed[0:12] + summed[12:24]
    return jnp.dot(summed, put, precision=lax.Precision.HIGHEST, preferred_element_type=F32)


def first_kernel(levels, me, remote, pairs, state, geo, mass, weight, bins, fwd, back, coef, sel, *outs):
    stiff_out, asm0, asm1, out_near, *rest = outs
    out_far, pm = rest[:-3], rest[-3:]
    x = jnp.concatenate([state[:, 512 * c : 512 * c + 512] for c in range(3)], axis=0)
    stiff = stiffness(x, geo, fwd, back, coef)
    stiff_out[...] = stiff
    shares = (-STEP) * weight[...] * mass[...]
    store_panels(stiff, (shares, bins[...].astype(F32)), sel, pm)
    send_rows(remote, me, levels, pm, out_near, out_far)
    asm0[...] = jnp.zeros_like(asm0)
    asm1[...] = jnp.zeros_like(asm1)
    pair_rows(pairs, pm, (asm0, asm1))


def middle_kernel(levels, n_far, me, remote, pairs, *refs):
    near, far = refs[0], refs[1 : 1 + n_far]
    rest = refs[1 + n_far :]
    state, stiff1, asm0, asm1, geo, mass, weight, bins, fwd, back, coef, sel, selt = rest[:13]
    part_out, out_near = rest[13], rest[14]
    out_far = rest[15 : 15 + n_far]
    asm, pm = rest[15 + n_far : 17 + n_far], rest[17 + n_far :]
    asm[0][...] = asm0[...]
    asm[1][...] = asm1[...]
    take_rows(remote, me, levels, near, far, asm)
    scale = thrice(STEP * mass[...])
    x = jnp.concatenate([state[:, 512 * c : 512 * c + 512] for c in range(3)], axis=0)
    x = x - scale * (stiff1[...] + lift(asm, selt))
    stiff = stiffness(x, geo, fwd, back, coef)
    store_panels(stiff, None, sel, pm)
    send_rows(remote, me, levels, pm, out_near, out_far)
    asm[0][...] = jnp.zeros_like(asm0)
    asm[1][...] = jnp.zeros_like(asm1)
    pair_rows(pairs, pm, asm)
    part = x - scale * (stiff + lift(asm, selt))
    part_out[...] = part
    total = x + part
    w = weight[...]
    acc = bin_dot([w * total[64 * c : 64 * c + 64] for c in range(3)], bins[...])
    lane = lax.broadcasted_iota(jnp.int32, (K, 128), 1)
    for r, (kind, where) in enumerate(levels):
        if kind == "near":
            j = me[0] ^ where
            got, sent = (lambda a, b: near[j, :, a:b]), (lambda a, b: out_near[j, :, a:b])
        else:
            got = lambda a, b, ref=far[where]: ref[:, a:b]
            sent = lambda a, b, ref=out_far[where]: ref[:, a:b]
        high, bin_low = got(128, 256), got(256, 384)
        share = jnp.where(lane < 64, pltpu.roll(high, 64, 1), high)
        label = jnp.where(lane < 64, bin_low, pltpu.roll(bin_low, 64, 1)).astype(jnp.int32)
        first = sent(0, 128) * share
        second = jnp.where(lane < 64, sent(128, 256) * share, 0.0)
        fields = [jnp.where(lane < 64, first, 0.0), jnp.where(lane < 64, 0.0, first), second]
        acc = acc + bin_dot(fields, label)
    sums = bin_finish(acc)
    for j in range(out_near.shape[0]):
        out_near[j, 0:12, 192:256] = sums[:, 64:128]


def merge_kernel(copies, near, out):
    sums = jnp.sum(near[:, :, :], axis=0)
    row = lax.broadcasted_iota(jnp.int32, (K, 128), 0)
    col = lax.broadcasted_iota(jnp.int32, (K, 128), 1)
    r = lax.broadcasted_iota(jnp.int32, (128, 128), 0)
    c = lax.broadcasted_iota(jnp.int32, (128, 128), 1)
    spread = jnp.where((r >= 64) & (r < 96) & ((c & 31) == r - 64), 1.0, 0.0)
    sums = jnp.where((row < 12) & (col >= 64) & (col < 96), sums, 0.0)
    full = jnp.dot(sums, spread, precision=lax.Precision.HIGHEST, preferred_element_type=F32)
    full = jnp.where((row & 3) == (col >> 5), full, 0.0)
    done = jnp.concatenate([jnp.sum(full[4 * i : 4 * i + 4], axis=0, keepdims=True) for i in range(3)], axis=0)
    for j in range(copies):
        out[j] = done


def last_kernel(levels, n_far, me, remote, *refs):
    near, far = refs[0], refs[1 : 1 + n_far]
    part, mass, selt, out, *asm = refs[1 + n_far :]
    for block in asm:
        block[...] = jnp.zeros_like(block)
    take_rows(remote, me, levels, near, far, asm)
    moved = part[...] - thrice(STEP * mass[...]) * lift(asm, selt)
    for c in range(3):
        out[:, 512 * c : 512 * c + 512] = moved[64 * c : 64 * c + 64]


SMEM = pl.BlockSpec(memory_space=pltpu.SMEM)
VMEM = pl.BlockSpec(memory_space=pltpu.VMEM)
PARAMS = pltpu.CompilerParams(vmem_limit_bytes=24 * 1024 * 1024)


def on_device(sizes, state, geo, mass, weight, bins, pairs, remote):
    nz, nx, ny, nc = sizes
    group = ("x", "y", "c")
    n_near = nx * ny * nc
    log = lambda n: n.bit_length() - 1
    levels = [("near", ny * nc * 2**b) for b in range(log(nx))]
    levels += [("far", b) for b in range(log(nz))]
    levels += [("near", 2**b) for b in range(log(ny * nc))]
    n_far = log(nz)
    fwd, back, coef, sel, selt = (jnp.asarray(a) for a in constants())
    me = lax.axis_index(group).astype(jnp.int32).reshape(1)
    shape = jax.ShapeDtypeStruct

    def exchange(near, far):
        got_far = [None] * n_far
        for b in reversed(range(n_far)):
            got_far[b] = lax.ppermute(far[b], "z", [(s, s ^ 2**b) for s in range(nz)])
        return lax.all_to_all(near, group, 0, 0, tiled=True), got_far

    stiff1, asm0, asm1, near, *far = pl.pallas_call(
        functools.partial(first_kernel, levels),
        out_shape=[shape((192, 512), F32), shape((384, 128), F32), shape((384, 128), F32)]
        + [shape((n_near, K, 384), F32)] + [shape((K, 384), F32)] * n_far,
        in_specs=[SMEM] * 3 + [VMEM] * 9,
        out_specs=[VMEM] * (4 + n_far),
        scratch_shapes=[VM((384, 128), F32)] * 3,
        compiler_params=PARAMS,
        name="first",
    )(me, remote, pairs, state, geo, mass, weight, bins, fwd, back, coef, sel)
    near, far = exchange(near, far)
    part, near, *far = pl.pallas_call(
        functools.partial(middle_kernel, levels, n_far),
        out_shape=[shape((192, 512), F32), shape((n_near, K, 256), F32)] + [shape((K, 256), F32)] * n_far,
        in_specs=[SMEM] * 3 + [VMEM] * (14 + n_far),
        out_specs=[VMEM] * (2 + n_far),
        scratch_shapes=[VM((384, 128), F32)] * 4,
        compiler_params=PARAMS,
        name="middle",
    )(me, remote, pairs, near, *far, state, stiff1, asm0, asm1, geo, mass, weight, bins, fwd, back, coef, sel, selt)
    near, far = exchange(near, far)
    sums = pl.pallas_call(
        functools.partial(merge_kernel, nz),
        out_shape=shape((nz, 3, 128), F32),
        grid=(1,),
        in_specs=[pl.BlockSpec((n_near, K, 128), lambda i: (0, 0, 1))],
        out_specs=pl.BlockSpec((nz, 3, 128), lambda i: (0, 0, 0)),
        compiler_params=PARAMS,
        name="merge",
    )(near)
    sums = lax.all_to_all(sums, "z", 0, 0, tiled=True)
    final = pl.pallas_call(
        functools.partial(last_kernel, levels, n_far),
        out_shape=shape((E, 1536), F32),
        in_specs=[SMEM] * 2 + [VMEM] * (4 + n_far),
        out_specs=VMEM,
        scratch_shapes=[VM((384, 128), F32)] * 2,
        compiler_params=PARAMS,
        name="last",
    )(me, remote, near, *far, part, mass, selt)
    points = nz * n_near * E * 512
    return final, jnp.sum(sums, axis=0) * (1.0 / math.sqrt(points / NBIN))


def solution(mesh):
    gx, gy = mesh.shape["gx"], mesh.shape["gy"]
    nx = 4 if gx >= 16 else 2
    sizes = (gx // nx, nx, gy // 2, 2)
    names = ("z", "x", "y", "c")
    inner = Mesh(mesh.devices.reshape(sizes), names)
    rows = P(names, None)
    return jax.shard_map(
        functools.partial(on_device, sizes),
        mesh=inner,
        in_specs=(rows,) * 7,
        out_specs=(rows, P()),
        check_vma=False,
    )
```

time: 368 us -> 191 us (0.52)
  blocking collectives: 155 us -> 23.7 us
  local copies, waits for them, and re-layouts: 63.7 us -> 26.8 us
  waiting for transfers between devices: 2.44 us -> 27.9 us
  matrix products: 19.5 us -> 0 us
  other arithmetic: 17.6 us -> 0.63 us
  Pallas kernels: 0 us -> 12.6 us
  starting transfers between devices: 106 us -> 95 us
    psum x1 -> x0, blocking collectives: 155 us -> none  [on_device(): lax.psum(binned(current, profile_weight, bin_index), ('gx', 'gy'))]
    ppermute x20 -> x10, starting transfers between devices: 106 us -> 65.4 us  [exchange(): got_far[b] = lax.ppermute(far[b], 'z', [(s, s ^ 2 ** b) for s in range(nz)])]
    all_to_all x0 -> x2, starting transfers between devices: none -> 29.5 us  [the longest x1 17.9 us: exchange(): return (lax.all_to_all(near, group, 0, 0, tiled=True), got_far)]
    ppermute x20 -> x10, waiting for transfers between devices: 2.44 us -> 27.9 us  [exchange(): got_far[b] = lax.ppermute(far[b], 'z', [(s, s ^ 2 ** b) for s in range(nz)])]
    all_to_all x0 -> x1, blocking collectives: none -> 23.7 us  [exchange(): return (lax.all_to_all(near, group, 0, 0, tiled=True), got_far)]
    unnamed x48 -> x101, local copies, waits for them, and re-layouts: 3.34 us -> 26.8 us
    dot_general x14 -> x0, matrix products: 19.5 us -> none  [the longest x2 4.29 us: binned(): lax.dot_general(left, lower_mask, (((1,), (1,)), ((), ())), precision=pre...]
    squeeze x20 -> x0, local copies, waits for them, and re-layouts: 14.9 us -> none  [the longest x14 10.4 us: route_panels(): pieces.append(from_partner(outgoing[bit_index], 'gx', bit_index))]
  transfers between devices with their start and end apart: 20 -> 12, of which waited for: 1 -> 3; matrix products, arithmetic and copies ran while one was open for 9% -> 0% of each run, Pallas kernels for 0% -> 1%
where the time goes in v1:
time: 191 us; the launch traced here: 188 us
  starting transfers between devices  95 us (50%)
  waiting for transfers between devices  27.9 us (15%)
  local copies, waits for them, and re-layouts  26.8 us (14%)
  blocking collectives  23.7 us (12%)
  Pallas kernels  12.6 us (7%)
    ppermute x10, starting transfers between devices, exchange(): got_far[b] = lax.ppermute(far[b], 'z', [(s, s ^ 2 ** b) for s in range(nz)])  65.4 us
    ppermute x10, waiting for transfers between devices, exchange(): got_far[b] = lax.ppermute(far[b], 'z', [(s, s ^ 2 ** b) for s in range(nz)])  27.9 us
    unnamed x101, local copies, waits for them, and re-layouts  26.8 us
    all_to_all x1, blocking collectives, exchange(): return (lax.all_to_all(near, group, 0, 0, tiled=True), got_far)  23.7 us
    all_to_all x1, starting transfers between devices, exchange(): return (lax.all_to_all(near, group, 0, 0, tiled=True), got_far)  17.9 us
    all_to_all x1, starting transfers between devices, on_device(): sums = lax.all_to_all(sums, 'z', 0, 0, tiled=True)  11.6 us
    pallas_call x1, Pallas kernels, on_device(): pl.pallas_call(functools.partial(middle_kernel, levels, n_far), out_shape...  6.56 us
  transfers between devices with their start and end apart: 12, of which 3 were waited for; matrix products, arithmetic and copies ran while one was open for 0% of the time, Pallas kernels for 1%

profile of v1, /device:TPU:1, one launch (start us, length us, event | category | flops | bytes accessed | tf_op | source)
XLA Modules:
  0.0 187.6 jit_solution(10722212539594616227)
XLA Ops:
  1.4 1.0 copy-done.1
  2.4 1.0 copy-done.3
  3.4 1.0 copy-done.5
  10.4 3.1 %first.1 = (f32[192,512]{1,0:T(8,128)S(1)}, f32[384,128]{1,0:T(8,128)S(1)}, f32[384,128]{1,0:T(8,128)S(1)}, f32[32,24,384]{2,1,0:T(8,128)S(1)}, f32[24,384]{1,0:...) custom-call(s32[1]{0:T(128)} %bitcast.me, ...), custom_call_target="tpu_custom_call" | custom-call | tf_op jit(solution)/shard_map/first/pallas_call | solution.py:331
  13.5 1.1 copy-done.9
  19.8 17.9 %all-to-all-start = ((f32[32,24,384]{2,1,0:T(8,128)}), f32[32,24,384]{2,1,0:T(8,128)S(1)}, u32[]{:S(2)}, u32[]{:S(2)}) async-start(f32[32,24,384]{2,1,0:T(8,128)} %copy-done.9), calls=%async_computation | async-start | bytes 2359296 | tf_op jit(solution)/shard_map/all_to_all | solution.py:329
  37.7 1.9 %collective-permute-start = (f32[24,384]{1,0:T(8,128)}, f32[24,384]{1,0:T(8,128)S(1)}, u32[]{:S(2)}, u32[]{:S(2)}) collective-permute-start(f32[24,384]{1,0:T(8,128)} %copy-done.44), channel_id=1, source_target_pairs={{0,32},{32,0},{64,96},{96,64},{128,160},{160,128},{192,224},{224,1... | collective-permute-start | bytes 110600 | tf_op jit(solution)/shard_map/ppermute | solution.py:328
  39.6 1.9 %collective-permute-start.1 = (f32[24,384]{1,0:T(8,128)}, f32[24,384]{1,0:T(8,128)S(1)}, u32[]{:S(2)}, u32[]{:S(2)}) collective-permute-start(f32[24,384]{1,0:T(8,128)} %copy-done.43), channel_id=1, source_target_pairs={{0,64},{32,96},{64,0},{96,32},{128,192},{160,224},{192,128},{224,1... | collective-permute-start | bytes 110600 | tf_op jit(solution)/shard_map/ppermute | solution.py:328
  41.5 4.3 %collective-permute-start.2 = (f32[24,384]{1,0:T(8,128)}, f32[24,384]{1,0:T(8,128)S(1)}, u32[]{:S(2)}, u32[]{:S(2)}) collective-permute-start(f32[24,384]{1,0:T(8,128)} %copy-done.42), channel_id=1, source_target_pairs={{0,128},{32,160},{64,192},{96,224},{128,0},{160,32},{192,64},{224,... | collective-permute-start | bytes 110600 | tf_op jit(solution)/shard_map/ppermute | solution.py:328
  45.8 15.4 %collective-permute-start.3 = (f32[24,384]{1,0:T(8,128)}, f32[24,384]{1,0:T(8,128)S(1)}, u32[]{:S(2)}, u32[]{:S(2)}) collective-permute-start(f32[24,384]{1,0:T(8,128)} %copy-done.41), channel_id=1, source_target_pairs={{0,256},{32,288},{64,320},{96,352},{128,384},{160,416},{192,448},{... | collective-permute-start | bytes 110600 | tf_op jit(solution)/shard_map/ppermute | solution.py:328
  61.3 11.6 %collective-permute-start.4 = (f32[24,384]{1,0:T(8,128)}, f32[24,384]{1,0:T(8,128)S(1)}, u32[]{:S(2)}, u32[]{:S(2)}) collective-permute-start(f32[24,384]{1,0:T(8,128)} %copy-done.40), channel_id=1, source_target_pairs={{0,512},{32,544},{64,576},{96,608},{128,640},{160,672},{192,704},{... | collective-permute-start | bytes 110600 | tf_op jit(solution)/shard_map/ppermute | solution.py:328
  75.3 9.2 %collective-permute-done.4.refs_5_ = f32[24,384]{1,0:T(8,128)S(1)} collective-permute-done((f32[24,384]{1,0:T(8,128)}, f32[24,384]{1,0:T(8,128)S(1)}, u32[]{:S(2)}, u32[]{:S(2)}) %collective-permute-start.4) | collective-permute-done | bytes 36896 | tf_op jit(solution)/shard_map/ppermute | solution.py:328
  91.9 6.6 %middle.1 = (f32[192,512]{1,0:T(8,128)S(1)}, f32[32,24,256]{2,1,0:T(8,128)S(1)}, f32[24,256]{1,0:T(8,128)S(1)}, f32[24,256]{1,0:T(8,128)S(1)}, f32[24,256]{1,0:T...) custom-call(s32[1]{0:T(128)} %bitcast.me, s32[10,24]{1,0:T(8,128)S(1)} %copy-done.29, s32[40,2]{1,0:T(8,128)S(1)} %copy.15.pairs, ...), custom_call_target="tpu_custom_call" | custom-call | tf_op jit(solution)/shard_map/middle/pallas_call | solution.py:342
  98.5 23.7 %all_to_all.15.refs_0_.near = f32[32,24,256]{2,1,0:T(8,128)S(1)} all-to-all(f32[32,24,256]{2,1,0:T(8,128)S(1)} %get-tuple-element.27), channel_id=1, replica_groups=mesh['z'=32,'x'=4,'y'=4,'c'=2] {'x','y','c'}, dimensions={0} | all-to-all | bytes 1572864 | tf_op jit(solution)/shard_map/all_to_all | solution.py:329
  123.1 11.6 %all-to-all-start.2 = ((f32[32,3,128]{2,1,0:T(4,128)}), f32[32,3,128]{2,1,0:T(4,128)S(1)}, u32[]{:S(2)}, u32[]{:S(2)}) async-start(f32[32,3,128]{2,1,0:T(4,128)} %merge.1), calls=%async_computation.2 | async-start | bytes 131072 | tf_op jit(solution)/shard_map/all_to_all | solution.py:361
  134.7 3.1 %collective-permute-start.5 = (f32[24,256]{1,0:T(8,128)}, f32[24,256]{1,0:T(8,128)S(1)}, u32[]{:S(2)}, u32[]{:S(2)}) collective-permute-start(f32[24,256]{1,0:T(8,128)} %copy-done.49), channel_id=1, source_target_pairs={{0,32},{32,0},{64,96},{96,64},{128,160},{160,128},{192,224},{224,1... | collective-permute-start | bytes 73736 | tf_op jit(solution)/shard_map/ppermute | solution.py:328
  137.9 4.0 %collective-permute-start.6 = (f32[24,256]{1,0:T(8,128)}, f32[24,256]{1,0:T(8,128)S(1)}, u32[]{:S(2)}, u32[]{:S(2)}) collective-permute-start(f32[24,256]{1,0:T(8,128)} %copy-done.48), channel_id=1, source_target_pairs={{0,64},{32,96},{64,0},{96,32},{128,192},{160,224},{192,128},{224,1... | collective-permute-start | bytes 73736 | tf_op jit(solution)/shard_map/ppermute | solution.py:328
  141.9 7.0 %collective-permute-start.7 = (f32[24,256]{1,0:T(8,128)}, f32[24,256]{1,0:T(8,128)S(1)}, u32[]{:S(2)}, u32[]{:S(2)}) collective-permute-start(f32[24,256]{1,0:T(8,128)} %copy-done.47), channel_id=1, source_target_pairs={{0,128},{32,160},{64,192},{96,224},{128,0},{160,32},{192,64},{224,... | collective-permute-start | bytes 73736 | tf_op jit(solution)/shard_map/ppermute | solution.py:328
  148.9 11.8 %collective-permute-start.8 = (f32[24,256]{1,0:T(8,128)}, f32[24,256]{1,0:T(8,128)S(1)}, u32[]{:S(2)}, u32[]{:S(2)}) collective-permute-start(f32[24,256]{1,0:T(8,128)} %copy-done.46), channel_id=1, source_target_pairs={{0,256},{32,288},{64,320},{96,352},{128,384},{160,416},{192,448},{... | collective-permute-start | bytes 73736 | tf_op jit(solution)/shard_map/ppermute | solution.py:328
  160.7 4.4 %collective-permute-start.9 = (f32[24,256]{1,0:T(8,128)}, f32[24,256]{1,0:T(8,128)S(1)}, u32[]{:S(2)}, u32[]{:S(2)}) collective-permute-start(f32[24,256]{1,0:T(8,128)} %copy-done.45), channel_id=1, source_target_pairs={{0,512},{32,544},{64,576},{96,608},{128,640},{160,672},{192,704},{... | collective-permute-start | bytes 73736 | tf_op jit(solution)/shard_map/ppermute | solution.py:328
  165.1 1.4 collective-permute-done.8.refs_4_
  166.5 17.3 %collective-permute-done.9.refs_5_ = f32[24,256]{1,0:T(8,128)S(1)} collective-permute-done((f32[24,256]{1,0:T(8,128)}, f32[24,256]{1,0:T(8,128)S(1)}, u32[]{:S(2)}, u32[]{:S(2)}) %collective-permute-start.9) | collective-permute-done | bytes 24608 | tf_op jit(solution)/shard_map/ppermute | solution.py:328
  183.8 1.0 copy-done.21
  184.8 2.1 %last.1 = f32[64,1536]{1,0:T(8,128)} custom-call(s32[1]{0:T(128)} %bitcast.me, s32[10,24]{1,0:T(8,128)S(1)} %copy-done.29, f32[32,24,256]{2,1,0:T(8,128)S(1)} %all_to_all.15.refs_0_.near, f32[24,256]{1,0:T(8,128)S(1)} %collective-permute-done.5.refs_1_, f32[24,256]{1,0:T(8,128)S(1)} %collective-permute-done.6.refs_2_, ...), custom_call_target="tpu_custom_call" | custom-call | tf_op jit(solution)/shard_map/last/pallas_call | solution.py:362
  (108 shorter events, 23.2 us)
Async XLA Ops:
  19.7 65.4 %copy-start = (bf16[384,512]{1,0:T(8,128)(2,1)S(1)}, bf16[384,512]{1,0:T(8,128)(2,1)}, u32[]{:S(2)}) copy-start(bf16[384,512]{1,0:T(8,128)(2,1)} %constant.33.clone.refs_18_.refs_8_) | copy-start | bytes 1179652
  19.7 65.4 %copy-start.2 = (f32[64,1536]{1,0:T(8,128)S(1)}, f32[64,1536]{1,0:T(8,128)}, u32[]{:S(2)}) copy-start(f32[64,1536]{1,0:T(8,128)} %refs_6_.1) | copy-start | bytes 1179652
  19.7 65.4 %copy-start.4 = (f32[64,1536]{1,0:T(8,128)S(1)}, f32[64,1536]{1,0:T(8,128)}, u32[]{:S(2)}) copy-start(f32[64,1536]{1,0:T(8,128)} %refs_10_.1) | copy-start | bytes 1179652
  19.7 65.4 %copy-start.6 = (bf16[512,384]{1,0:T(8,128)(2,1)S(1)}, bf16[512,384]{1,0:T(8,128)(2,1)}, u32[]{:S(2)}) copy-start(bf16[512,384]{1,0:T(8,128)(2,1)} %constant.32.clone.sel.refs_17_) | copy-start | bytes 1179652
  19.7 65.4 %copy-start.8 = (f32[64,512]{1,0:T(8,128)S(1)}, f32[64,512]{1,0:T(8,128)}, u32[]{:S(2)}) copy-start(f32[64,512]{1,0:T(8,128)} %refs_7_.1) | copy-start | bytes 393220
  19.7 65.4 %copy-start.11 = (bf16[384,256]{1,0:T(8,128)(2,1)S(1)}, bf16[384,256]{1,0:T(8,128)(2,1)}, u32[]{:S(2)}) copy-start(bf16[384,256]{1,0:T(8,128)(2,1)} %constant.29.clone.fwd.refs_14_) | copy-start | bytes 589828
  19.7 65.4 %copy-start.13 = (f32[64,512]{1,0:T(8,128)S(1)}, f32[64,512]{1,0:T(8,128)}, u32[]{:S(2)}) copy-start(f32[64,512]{1,0:T(8,128)} %refs_12_.1) | copy-start | bytes 393220
  19.7 65.4 %copy-start.15 = (s32[64,512]{1,0:T(8,128)S(1)}, s32[64,512]{1,0:T(8,128)}, u32[]{:S(2)}) copy-start(s32[64,512]{1,0:T(8,128)} %refs_13_.1) | copy-start | bytes 393220
  19.7 65.4 %copy-start.17 = (bf16[256,256]{1,0:T(8,128)(2,1)S(1)}, bf16[256,256]{1,0:T(8,128)(2,1)}, u32[]{:S(2)}) copy-start(bf16[256,256]{1,0:T(8,128)(2,1)} %constant.30.clone.back.refs_15_) | copy-start | bytes 393220
  19.8 65.4 %copy-start.27 = (f32[64,128]{1,0:T(8,128)S(1)}, f32[64,128]{1,0:T(8,128)}, u32[]{:S(2)}) copy-start(f32[64,128]{1,0:T(8,128)} %constant.31.clone.coef.refs_16_) | copy-start | bytes 98308
  19.8 65.4 %copy-start.29 = (s32[10,24]{1,0:T(8,128)S(1)}, s32[10,24]{1,0:T(8,128)}, u32[]{:S(2)}) copy-start(s32[10,24]{1,0:T(8,128)} %remote.5) | copy-start | bytes 2884
  19.8 65.3 %all-to-all-start = ((f32[32,24,384]{2,1,0:T(8,128)}), f32[32,24,384]{2,1,0:T(8,128)S(1)}, u32[]{:S(2)}, u32[]{:S(2)}) async-start(f32[32,24,384]{2,1,0:T(8,128)} %copy-done.9), calls=%async_computation | async-start | bytes 2359296 | tf_op jit(solution)/shard_map/all_to_all | solution.py:329
  37.7 35.2 %collective-permute-start = (f32[24,384]{1,0:T(8,128)}, f32[24,384]{1,0:T(8,128)S(1)}, u32[]{:S(2)}, u32[]{:S(2)}) collective-permute-start(f32[24,384]{1,0:T(8,128)} %copy-done.44), channel_id=1, source_target_pairs={{0,32},{32,0},{64,96},{96,64},{128,160},{160,128},{192,224},{224,1... | collective-permute-start | bytes 110600 | tf_op jit(solution)/shard_map/ppermute | solution.py:328
  39.6 33.9 %collective-permute-start.1 = (f32[24,384]{1,0:T(8,128)}, f32[24,384]{1,0:T(8,128)S(1)}, u32[]{:S(2)}, u32[]{:S(2)}) collective-permute-start(f32[24,384]{1,0:T(8,128)} %copy-done.43), channel_id=1, source_target_pairs={{0,64},{32,96},{64,0},{96,32},{128,192},{160,224},{192,128},{224,1... | collective-permute-start | bytes 110600 | tf_op jit(solution)/shard_map/ppermute | solution.py:328
  41.5 32.5 %collective-permute-start.2 = (f32[24,384]{1,0:T(8,128)}, f32[24,384]{1,0:T(8,128)S(1)}, u32[]{:S(2)}, u32[]{:S(2)}) collective-permute-start(f32[24,384]{1,0:T(8,128)} %copy-done.42), channel_id=1, source_target_pairs={{0,128},{32,160},{64,192},{96,224},{128,0},{160,32},{192,64},{224,... | collective-permute-start | bytes 110600 | tf_op jit(solution)/shard_map/ppermute | solution.py:328
  45.8 28.9 %collective-permute-start.3 = (f32[24,384]{1,0:T(8,128)}, f32[24,384]{1,0:T(8,128)S(1)}, u32[]{:S(2)}, u32[]{:S(2)}) collective-permute-start(f32[24,384]{1,0:T(8,128)} %copy-done.41), channel_id=1, source_target_pairs={{0,256},{32,288},{64,320},{96,352},{128,384},{160,416},{192,448},{... | collective-permute-start | bytes 110600 | tf_op jit(solution)/shard_map/ppermute | solution.py:328
  61.3 23.2 %collective-permute-start.4 = (f32[24,384]{1,0:T(8,128)}, f32[24,384]{1,0:T(8,128)S(1)}, u32[]{:S(2)}, u32[]{:S(2)}) collective-permute-start(f32[24,384]{1,0:T(8,128)} %copy-done.40), channel_id=1, source_target_pairs={{0,512},{32,544},{64,576},{96,608},{128,640},{160,672},{192,704},{... | collective-permute-start | bytes 110600 | tf_op jit(solution)/shard_map/ppermute | solution.py:328
  98.5 23.7 %copy-start.20 = (f32[192,512]{1,0:T(8,128)}, f32[192,512]{1,0:T(8,128)S(1)}, u32[]{:S(2)}) copy-start(f32[192,512]{1,0:T(8,128)S(1)} %get-tuple-element.33.refs_6_) | copy-start | bytes 1179652
  123.1 63.9 %all-to-all-start.2 = ((f32[32,3,128]{2,1,0:T(4,128)}), f32[32,3,128]{2,1,0:T(4,128)S(1)}, u32[]{:S(2)}, u32[]{:S(2)}) async-start(f32[32,3,128]{2,1,0:T(4,128)} %merge.1), calls=%async_computation.2 | async-start | bytes 131072 | tf_op jit(solution)/shard_map/all_to_all | solution.py:361
  134.7 30.4 %collective-permute-start.5 = (f32[24,256]{1,0:T(8,128)}, f32[24,256]{1,0:T(8,128)S(1)}, u32[]{:S(2)}, u32[]{:S(2)}) collective-permute-start(f32[24,256]{1,0:T(8,128)} %copy-done.49), channel_id=1, source_target_pairs={{0,32},{32,0},{64,96},{96,64},{128,160},{160,128},{192,224},{224,1... | collective-permute-start | bytes 73736 | tf_op jit(solution)/shard_map/ppermute | solution.py:328
  137.9 27.2 %collective-permute-start.6 = (f32[24,256]{1,0:T(8,128)}, f32[24,256]{1,0:T(8,128)S(1)}, u32[]{:S(2)}, u32[]{:S(2)}) collective-permute-start(f32[24,256]{1,0:T(8,128)} %copy-done.48), channel_id=1, source_target_pairs={{0,64},{32,96},{64,0},{96,32},{128,192},{160,224},{192,128},{224,1... | collective-permute-start | bytes 73736 | tf_op jit(solution)/shard_map/ppermute | solution.py:328
  141.9 23.2 %collective-permute-start.7 = (f32[24,256]{1,0:T(8,128)}, f32[24,256]{1,0:T(8,128)S(1)}, u32[]{:S(2)}, u32[]{:S(2)}) collective-permute-start(f32[24,256]{1,0:T(8,128)} %copy-done.47), channel_id=1, source_target_pairs={{0,128},{32,160},{64,192},{96,224},{128,0},{160,32},{192,64},{224,... | collective-permute-start | bytes 73736 | tf_op jit(solution)/shard_map/ppermute | solution.py:328
  148.9 17.6 %collective-permute-start.8 = (f32[24,256]{1,0:T(8,128)}, f32[24,256]{1,0:T(8,128)S(1)}, u32[]{:S(2)}, u32[]{:S(2)}) collective-permute-start(f32[24,256]{1,0:T(8,128)} %copy-done.46), channel_id=1, source_target_pairs={{0,256},{32,288},{64,320},{96,352},{128,384},{160,416},{192,448},{... | collective-permute-start | bytes 73736 | tf_op jit(solution)/shard_map/ppermute | solution.py:328
  160.7 23.1 %collective-permute-start.9 = (f32[24,256]{1,0:T(8,128)}, f32[24,256]{1,0:T(8,128)S(1)}, u32[]{:S(2)}, u32[]{:S(2)}) collective-permute-start(f32[24,256]{1,0:T(8,128)} %copy-done.45), channel_id=1, source_target_pairs={{0,512},{32,544},{64,576},{96,608},{128,640},{160,672},{192,704},{... | collective-permute-start | bytes 73736 | tf_op jit(solution)/shard_map/ppermute | solution.py:328
  (38 other events, 144.6 us)

commit v2 on v1

--- a/solution.py
+++ b/solution.py
@@ -169,8 +169,8 @@
 
 
 def pair_rows(pairs, pm, asm):
-    for i in range(pairs.shape[0]):
-        a, b = pairs[i, 0], pairs[i, 1]
+    for i in range(pairs.shape[1]):
+        a, b = pairs[0, i], pairs[1, i]
         for source, block in zip(pm, asm):
             block[pl.ds(b, 1), :] = source[pl.ds(a, 1), :]
             block[pl.ds(a, 1), :] = source[pl.ds(b, 1), :]
@@ -278,7 +278,8 @@
         out_near[j, 0:12, 192:256] = sums[:, 64:128]
 
 
-def merge_kernel(copies, near, out):
+def merge_kernel(copies, n_in, near, *refs):
+    out = refs[n_in]
     sums = jnp.sum(near[:, :, :], axis=0)
     row = lax.broadcasted_iota(jnp.int32, (K, 128), 0)
     col = lax.broadcasted_iota(jnp.int32, (K, 128), 1)
@@ -305,8 +306,25 @@
 
 
 SMEM = pl.BlockSpec(memory_space=pltpu.SMEM)
-VMEM = pl.BlockSpec(memory_space=pltpu.VMEM)
-PARAMS = pltpu.CompilerParams(vmem_limit_bytes=24 * 1024 * 1024)
+ANY = pl.BlockSpec(memory_space=pl.ANY)
+PARAMS = pltpu.CompilerParams(vmem_limit_bytes=56 * 1024 * 1024)
+
+
+def whole(a):
+    return pl.BlockSpec(a.shape, lambda i, n=len(a.shape): (0,) * n)
+
+
+def call(kernel, name, scalars, arrays, outs, scratch):
+    return pl.pallas_call(
+        kernel,
+        out_shape=outs,
+        grid=(1,),
+        in_specs=[SMEM] * len(scalars) + [whole(a) for a in arrays],
+        out_specs=[whole(a) for a in outs],
+        scratch_shapes=scratch,
+        compiler_params=PARAMS,
+        name=name,
+    )(*scalars, *arrays)
 
 
 def on_device(sizes, state, geo, mass, weight, bins, pairs, remote):
@@ -314,60 +332,61 @@
     group = ("x", "y", "c")
     n_near = nx * ny * nc
     log = lambda n: n.bit_length() - 1
+    n_far = log(nz)
     levels = [("near", ny * nc * 2**b) for b in range(log(nx))]
-    levels += [("far", b) for b in range(log(nz))]
+    levels += [("far", n_far - 1 - b) for b in range(n_far)]
     levels += [("near", 2**b) for b in range(log(ny * nc))]
-    n_far = log(nz)
     fwd, back, coef, sel, selt = (jnp.asarray(a) for a in constants())
     me = lax.axis_index(group).astype(jnp.int32).reshape(1)
-    shape = jax.ShapeDtypeStruct
-
-    def exchange(near, far):
-        got_far = [None] * n_far
-        for b in reversed(range(n_far)):
-            got_far[b] = lax.ppermute(far[b], "z", [(s, s ^ 2**b) for s in range(nz)])
-        return lax.all_to_all(near, group, 0, 0, tiled=True), got_far
-
-    stiff1, asm0, asm1, near, *far = pl.pallas_call(
+    shape = lambda *dims: jax.ShapeDtypeStruct(dims, F32)
+
+    def swap(far, first=0):
+        masks = [2 ** (n_far - 1 - first - i) for i in range(len(far))]
+        return [lax.ppermute(v, "z", [(s, s ^ m) for s in range(nz)]) for v, m in zip(far, masks)]
+
+    def spread(near):
+        return lax.all_to_all(near, group, 0, 0, tiled=True)
+
+    ops = [fwd, back, coef, sel]
+    stiff1, asm0, asm1, near, *far = call(
         functools.partial(first_kernel, levels),
-        out_shape=[shape((192, 512), F32), shape((384, 128), F32), shape((384, 128), F32)]
-        + [shape((n_near, K, 384), F32)] + [shape((K, 384), F32)] * n_far,
-        in_specs=[SMEM] * 3 + [VMEM] * 9,
-        out_specs=[VMEM] * (4 + n_far),
-        scratch_shapes=[VM((384, 128), F32)] * 3,
-        compiler_params=PARAMS,
-        name="first",
-    )(me, remote, pairs, state, geo, mass, weight, bins, fwd, back, coef, sel)
-    near, far = exchange(near, far)
-    part, near, *far = pl.pallas_call(
+        "first",
+        [me, remote, pairs.T],
+        [state, geo, mass, weight, bins, *ops],
+        [shape(192, 512), shape(384, 128), shape(384, 128), shape(n_near, K, 384)]
+        + [shape(K, 384)] * n_far,
+        [VM((384, 128), F32)] * 3,
+    )
+    near, far = spread(near), swap(far)
+    part, near, *far = call(
         functools.partial(middle_kernel, levels, n_far),
-        out_shape=[shape((192, 512), F32), shape((n_near, K, 256), F32)] + [shape((K, 256), F32)] * n_far,
-        in_specs=[SMEM] * 3 + [VMEM] * (14 + n_far),
-        out_specs=[VMEM] * (2 + n_far),
-        scratch_shapes=[VM((384, 128), F32)] * 4,
-        compiler_params=PARAMS,
-        name="middle",
-    )(me, remote, pairs, near, *far, state, stiff1, asm0, asm1, geo, mass, weight, bins, fwd, back, coef, sel, selt)
-    near, far = exchange(near, far)
-    sums = pl.pallas_call(
-        functools.partial(merge_kernel, nz),
-        out_shape=shape((nz, 3, 128), F32),
+        "middle",
+        [me, remote, pairs.T],
+        [near, *far, state, stiff1, asm0, asm1, geo, mass, weight, bins, *ops, selt],
+        [shape(192, 512), shape(n_near, K, 256)] + [shape(K, 256)] * n_far,
+        [VM((384, 128), F32)] * 4,
+    )
+    near, early, late = spread(near), swap(far[:2]), far[2:]
+    sums, *late = pl.pallas_call(
+        functools.partial(merge_kernel, nz, len(early) + len(late)),
+        out_shape=[shape(nz, 3, 128)] + [shape(K, 256)] * len(late),
         grid=(1,),
-        in_specs=[pl.BlockSpec((n_near, K, 128), lambda i: (0, 0, 1))],
-        out_specs=pl.BlockSpec((nz, 3, 128), lambda i: (0, 0, 0)),
+        in_specs=[pl.BlockSpec((n_near, K, 128), lambda i: (0, 0, 1))] + [ANY] * (len(early) + len(late)),
+        out_specs=[pl.BlockSpec((nz, 3, 128), lambda i: (0, 0, 0))] + [ANY] * len(late),
+        input_output_aliases={1 + len(early) + i: 1 + i for i in range(len(late))},
         compiler_params=PARAMS,
         name="merge",
-    )(near)
+    )(near, *early, *late)
     sums = lax.all_to_all(sums, "z", 0, 0, tiled=True)
-    final = pl.pallas_call(
+    far = early + swap(late, 2)
+    (final,) = call(
         functools.partial(last_kernel, levels, n_far),
-        out_shape=shape((E, 1536), F32),
-        in_specs=[SMEM] * 2 + [VMEM] * (4 + n_far),
-        out_specs=VMEM,
-        scratch_shapes=[VM((384, 128), F32)] * 2,
-        compiler_params=PARAMS,
-        name="last",
-    )(me, remote, near, *far, part, mass, selt)
+        "last",
+        [me, remote],
+        [near, *far, part, mass, selt],
+        [shape(E, 1536)],
+        [VM((384, 128), F32)] * 2,
+    )
     points = nz * n_near * E * 512
     return final, jnp.sum(sums, axis=0) * (1.0 / math.sqrt(points / NBIN))
 

time: 191 us -> 150 us (0.79)
  the two profiles are of different devices: /device:TPU:1 before, /device:TPU:2 now
where the time goes in v2:
time: 150 us
  starting transfers between devices  102 us (68%)
  waiting for transfers between devices  25.8 us (17%)
  Pallas kernels  17.8 us (12%)
  local copies, waits for them, and re-layouts  2.57 us (2%)
    ppermute x10, starting transfers between devices, swap(): lax.ppermute(v, 'z', [(s, s ^ m) for s in range(nz)])  65.3 us
    all_to_all x2, starting transfers between devices, spread(): return lax.all_to_all(near, group, 0, 0, tiled=True)  24.5 us
    ppermute x10, waiting for transfers between devices, swap(): lax.ppermute(v, 'z', [(s, s ^ m) for s in range(nz)])  21.9 us
    pallas_call x3, Pallas kernels, call(): pl.pallas_call(kernel, out_shape=outs, grid=(1,), in_specs=[SMEM] * len(s...  16 us
    all_to_all x1, starting transfers between devices, on_device(): sums = lax.all_to_all(sums, 'z', 0, 0, tiled=True)  12 us
    all_to_all x1, waiting for transfers between devices, on_device(): sums = lax.all_to_all(sums, 'z', 0, 0, tiled=True)  3.94 us
  transfers between devices with their start and end apart: 13, of which 6 were waited for; matrix products, arithmetic and copies ran while one was open for 0% of the time, Pallas kernels for 2%

profile of v2, /device:TPU:2, one launch (start us, length us, event | category | flops | bytes accessed | tf_op | source)
XLA Modules:
  0.0 149.5 jit_solution(12258344086864906522)
XLA Ops:
  0.6 4.4 %first.1 = (f32[192,512]{1,0:T(8,128)}, f32[384,128]{1,0:T(8,128)}, f32[384,128]{1,0:T(8,128)}, f32[32,24,384]{2,1,0:T(8,128)}, f32[24,384]{1,0:T(8,128)}, /*ind...) custom-call(s32[1]{0:T(128)} %bitcast.me, s32[10,24]{1,0:T(8,128)} %remote.5, ...), custom_call_target="tpu_custom_call" | custom-call | tf_op jit(solution)/shard_map/first/pallas_call | solution.py:318
  5.1 17.0 %all-to-all-start = ((f32[32,24,384]{2,1,0:T(8,128)}), f32[32,24,384]{2,1,0:T(8,128)S(1)}, u32[]{:S(2)}, u32[]{:S(2)}) async-start(f32[32,24,384]{2,1,0:T(8,128)} %get-tuple-element.22), calls=%async_computation | async-start | bytes 2359296 | tf_op jit(solution)/shard_map/all_to_all | solution.py:348
  22.1 19.8 %collective-permute-start = (f32[24,384]{1,0:T(8,128)S(1)}, f32[24,384]{1,0:T(8,128)S(1)}, u32[]{:S(2)}, u32[]{:S(2)}) collective-permute-start(f32[24,384]{1,0:T(8,128)S(1)} %copy-done.16), channel_id=1, source_target_pairs={{0,512},{32,544},{64,576},{96,608},{128,640},{160,672},{192,704},{... | collective-permute-start | bytes 110600 | tf_op jit(solution)/shard_map/ppermute | solution.py:345
  41.9 6.1 %collective-permute-start.1 = (f32[24,384]{1,0:T(8,128)S(1)}, f32[24,384]{1,0:T(8,128)S(1)}, u32[]{:S(2)}, u32[]{:S(2)}) collective-permute-start(f32[24,384]{1,0:T(8,128)S(1)} %copy-done.15), channel_id=1, source_target_pairs={{0,256},{32,288},{64,320},{96,352},{128,384},{160,416},{192,448},{... | collective-permute-start | bytes 110600 | tf_op jit(solution)/shard_map/ppermute | solution.py:345
  48.0 4.3 %collective-permute-start.2 = (f32[24,384]{1,0:T(8,128)S(1)}, f32[24,384]{1,0:T(8,128)S(1)}, u32[]{:S(2)}, u32[]{:S(2)}) collective-permute-start(f32[24,384]{1,0:T(8,128)S(1)} %copy-done.14), channel_id=1, source_target_pairs={{0,128},{32,160},{64,192},{96,224},{128,0},{160,32},{192,64},{224,... | collective-permute-start | bytes 110600 | tf_op jit(solution)/shard_map/ppermute | solution.py:345
  52.3 3.4 %collective-permute-start.3 = (f32[24,384]{1,0:T(8,128)S(1)}, f32[24,384]{1,0:T(8,128)S(1)}, u32[]{:S(2)}, u32[]{:S(2)}) collective-permute-start(f32[24,384]{1,0:T(8,128)S(1)} %copy-done.13), channel_id=1, source_target_pairs={{0,64},{32,96},{64,0},{96,32},{128,192},{160,224},{192,128},{224,1... | collective-permute-start | bytes 110600 | tf_op jit(solution)/shard_map/ppermute | solution.py:345
  55.7 2.9 %collective-permute-start.4 = (f32[24,384]{1,0:T(8,128)S(1)}, f32[24,384]{1,0:T(8,128)S(1)}, u32[]{:S(2)}, u32[]{:S(2)}) collective-permute-start(f32[24,384]{1,0:T(8,128)S(1)} %copy-done.12), channel_id=1, source_target_pairs={{0,32},{32,0},{64,96},{96,64},{128,160},{160,128},{192,224},{224,1... | collective-permute-start | bytes 110600 | tf_op jit(solution)/shard_map/ppermute | solution.py:345
  58.7 2.8 %collective-permute-done.1.refs_2_ = f32[24,384]{1,0:T(8,128)S(1)} collective-permute-done((f32[24,384]{1,0:T(8,128)S(1)}, f32[24,384]{1,0:T(8,128)S(1)}, u32[]{:S(2)}, u32[]{:S(2)}) %collective-permute-start.1) | collective-permute-done | bytes 36896 | tf_op jit(solution)/shard_map/ppermute | solution.py:345
  62.9 8.6 %middle.1 = (f32[192,512]{1,0:T(8,128)}, f32[32,24,256]{2,1,0:T(8,128)}, f32[24,256]{1,0:T(8,128)}, f32[24,256]{1,0:T(8,128)}, f32[24,256]{1,0:T(8,128)}, /*index=5*/f32[24,256]{1,0:T(8,128)}, f32[24,256]{1,0:T(8,128)}) custom-call(s32[1]{0:T(128)} %bitcast.me, s32[10,24]{1,0:T(8,128)} %remote.5, s32[2,40]{1,0:T(2,128)} %bitcast.3, ...), custom_call_target="tpu_custom_call" | custom-call | tf_op jit(solution)/shard_map/middle/pallas_call | solution.py:318
  71.5 7.5 %all-to-all-start.1 = ((f32[32,24,256]{2,1,0:T(8,128)}), f32[32,24,256]{2,1,0:T(8,128)S(1)}, u32[]{:S(2)}, u32[]{:S(2)}) async-start(f32[32,24,256]{2,1,0:T(8,128)} %get-tuple-element.31), calls=%async_computation.1 | async-start | bytes 1572864 | tf_op jit(solution)/shard_map/all_to_all | solution.py:348
  79.1 11.1 %collective-permute-start.5 = (f32[24,256]{1,0:T(8,128)S(1)}, f32[24,256]{1,0:T(8,128)S(1)}, u32[]{:S(2)}, u32[]{:S(2)}) collective-permute-start(f32[24,256]{1,0:T(8,128)S(1)} %copy-done.18), channel_id=1, source_target_pairs={{0,512},{32,544},{64,576},{96,608},{128,640},{160,672},{192,704},{... | collective-permute-start | bytes 73736 | tf_op jit(solution)/shard_map/ppermute | solution.py:345
  90.2 2.4 %collective-permute-start.6 = (f32[24,256]{1,0:T(8,128)S(1)}, f32[24,256]{1,0:T(8,128)S(1)}, u32[]{:S(2)}, u32[]{:S(2)}) collective-permute-start(f32[24,256]{1,0:T(8,128)S(1)} %copy-done.17), channel_id=1, source_target_pairs={{0,256},{32,288},{64,320},{96,352},{128,384},{160,416},{192,448},{... | collective-permute-start | bytes 73736 | tf_op jit(solution)/shard_map/ppermute | solution.py:345
  92.7 10.5 %collective-permute-done.5.refs_0_.refs_1_ = f32[24,256]{1,0:T(8,128)S(1)} collective-permute-done((f32[24,256]{1,0:T(8,128)S(1)}, f32[24,256]{1,0:T(8,128)S(1)}, u32[]{:S(2)}, u32[]{:S(2)}) %collective-permute-start.5) | collective-permute-done | bytes 24608 | tf_op jit(solution)/shard_map/ppermute | solution.py:345
  103.1 5.7 %collective-permute-done.6.refs_1_.refs_2_ = f32[24,256]{1,0:T(8,128)S(1)} collective-permute-done((f32[24,256]{1,0:T(8,128)S(1)}, f32[24,256]{1,0:T(8,128)S(1)}, u32[]{:S(2)}, u32[]{:S(2)}) %collective-permute-start.6) | collective-permute-done | bytes 24608 | tf_op jit(solution)/shard_map/ppermute | solution.py:345
  109.7 1.8 %merge.1 = (f32[32,3,128]{2,1,0:T(4,128)}, f32[24,256]{1,0:T(8,128)}, f32[24,256]{1,0:T(8,128)}, f32[24,256]{1,0:T(8,128)}) custom-call(f32[32,24,256]{2,1,0:T(8,128)} %copy-done, f32[24,256]{1,0:T(8,128)} %copy-done.2, f32[24,256]{1,0:T(8,128)} %copy-done.3, ...), custom_call_target="tpu_custom_call", output_to_operand_aliasing={{1}: (3, {}), {2}: (4, {}), {3}: (5, {})} | custom-call | tf_op jit(solution)/shard_map/merge/pallas_call | solution.py:370
  111.5 12.0 %all-to-all-start.2 = ((f32[32,3,128]{2,1,0:T(4,128)}), f32[32,3,128]{2,1,0:T(4,128)S(1)}, u32[]{:S(2)}, u32[]{:S(2)}) async-start(f32[32,3,128]{2,1,0:T(4,128)} %get-tuple-element.41), calls=%async_computation.2 | async-start | bytes 131072 | tf_op jit(solution)/shard_map/all_to_all | solution.py:380
  123.5 7.6 %collective-permute-start.7 = (f32[24,256]{1,0:T(8,128)}, f32[24,256]{1,0:T(8,128)S(1)}, u32[]{:S(2)}, u32[]{:S(2)}) collective-permute-start(f32[24,256]{1,0:T(8,128)} %get-tuple-element.37), channel_id=1, source_target_pairs={{0,128},{32,160},{64,192},{96,224},{128,0},{160,32},{192,64},{224,... | collective-permute-start | bytes 73736 | tf_op jit(solution)/shard_map/ppermute | solution.py:345
  131.1 4.3 %collective-permute-start.8 = (f32[24,256]{1,0:T(8,128)}, f32[24,256]{1,0:T(8,128)S(1)}, u32[]{:S(2)}, u32[]{:S(2)}) collective-permute-start(f32[24,256]{1,0:T(8,128)} %get-tuple-element.38), channel_id=1, source_target_pairs={{0,64},{32,96},{64,0},{96,32},{128,192},{160,224},{192,128},{224,1... | collective-permute-start | bytes 73736 | tf_op jit(solution)/shard_map/ppermute | solution.py:345
  135.4 3.4 %collective-permute-start.9 = (f32[24,256]{1,0:T(8,128)}, f32[24,256]{1,0:T(8,128)S(1)}, u32[]{:S(2)}, u32[]{:S(2)}) collective-permute-start(f32[24,256]{1,0:T(8,128)} %get-tuple-element.39), channel_id=1, source_target_pairs={{0,32},{32,0},{64,96},{96,64},{128,160},{160,128},{192,224},{224,1... | collective-permute-start | bytes 73736 | tf_op jit(solution)/shard_map/ppermute | solution.py:345
  138.8 2.6 %collective-permute-done.9.refs_5_ = f32[24,256]{1,0:T(8,128)S(1)} collective-permute-done((f32[24,256]{1,0:T(8,128)}, f32[24,256]{1,0:T(8,128)S(1)}, u32[]{:S(2)}, u32[]{:S(2)}) %collective-permute-start.9) | collective-permute-done | bytes 24608 | tf_op jit(solution)/shard_map/ppermute | solution.py:345
  141.4 0.6 copy-done.11
  142.0 3.0 %last.1 = f32[64,1536]{1,0:T(8,128)} custom-call(s32[1]{0:T(128)} %bitcast.me, s32[10,24]{1,0:T(8,128)} %remote.5, f32[32,24,256]{2,1,0:T(8,128)} %copy-done, f32[24,256]{1,0:T(8,128)} %copy-done.2, f32[24,256]{1,0:T(8,128)} %copy-done.3, f32[24,256]{1,0:T(8,128)} %copy-done.9, f32[24,256]{1,0:T(8,128)} %copy-done.10, f32[24,256]{1,0:T(8,128)} %copy-done.11, ...), custom_call_target="tpu_custom_call" | custom-call | tf_op jit(solution)/shard_map/last/pallas_call | solution.py:318
  145.0 3.9 %all-to-all-done.2 = f32[32,3,128]{2,1,0:T(4,128)S(1)} async-done(((f32[32,3,128]{2,1,0:T(4,128)}), f32[32,3,128]{2,1,0:T(4,128)S(1)}, u32[]{:S(2)}, u32[]{:S(2)}) %all-to-all-start.2) | async-done | bytes 49184 | tf_op jit(solution)/shard_map/all_to_all | solution.py:380
  149.0 0.6 broadcast_multiply_fusion
  (46 shorter events, 2.4 us)
Async XLA Ops:
  5.0 17.0 %copy-start.16 = (f32[24,384]{1,0:T(8,128)S(1)}, f32[24,384]{1,0:T(8,128)}, u32[]{:S(2)}) copy-start(f32[24,384]{1,0:T(8,128)} %get-tuple-element.23) | copy-start | bytes 110596
  5.1 36.8 %copy-start.15 = (f32[24,384]{1,0:T(8,128)S(1)}, f32[24,384]{1,0:T(8,128)}, u32[]{:S(2)}) copy-start(f32[24,384]{1,0:T(8,128)} %get-tuple-element.24) | copy-start | bytes 110596
  5.1 42.9 %copy-start.14 = (f32[24,384]{1,0:T(8,128)S(1)}, f32[24,384]{1,0:T(8,128)}, u32[]{:S(2)}) copy-start(f32[24,384]{1,0:T(8,128)} %get-tuple-element.25) | copy-start | bytes 110596
  5.1 47.2 %copy-start.13 = (f32[24,384]{1,0:T(8,128)S(1)}, f32[24,384]{1,0:T(8,128)}, u32[]{:S(2)}) copy-start(f32[24,384]{1,0:T(8,128)} %get-tuple-element.26) | copy-start | bytes 110596
  5.1 50.6 %copy-start.12 = (f32[24,384]{1,0:T(8,128)S(1)}, f32[24,384]{1,0:T(8,128)}, u32[]{:S(2)}) copy-start(f32[24,384]{1,0:T(8,128)} %get-tuple-element.27) | copy-start | bytes 110596
  5.1 56.7 %all-to-all-start = ((f32[32,24,384]{2,1,0:T(8,128)}), f32[32,24,384]{2,1,0:T(8,128)S(1)}, u32[]{:S(2)}, u32[]{:S(2)}) async-start(f32[32,24,384]{2,1,0:T(8,128)} %get-tuple-element.22), calls=%async_computation | async-start | bytes 2359296 | tf_op jit(solution)/shard_map/all_to_all | solution.py:348
  22.1 36.6 %collective-permute-start = (f32[24,384]{1,0:T(8,128)S(1)}, f32[24,384]{1,0:T(8,128)S(1)}, u32[]{:S(2)}, u32[]{:S(2)}) collective-permute-start(f32[24,384]{1,0:T(8,128)S(1)} %copy-done.16), channel_id=1, source_target_pairs={{0,512},{32,544},{64,576},{96,608},{128,640},{160,672},{192,704},{... | collective-permute-start | bytes 110600 | tf_op jit(solution)/shard_map/ppermute | solution.py:345
  41.9 19.6 %collective-permute-start.1 = (f32[24,384]{1,0:T(8,128)S(1)}, f32[24,384]{1,0:T(8,128)S(1)}, u32[]{:S(2)}, u32[]{:S(2)}) collective-permute-start(f32[24,384]{1,0:T(8,128)S(1)} %copy-done.15), channel_id=1, source_target_pairs={{0,256},{32,288},{64,320},{96,352},{128,384},{160,416},{192,448},{... | collective-permute-start | bytes 110600 | tf_op jit(solution)/shard_map/ppermute | solution.py:345
  48.0 13.5 %collective-permute-start.2 = (f32[24,384]{1,0:T(8,128)S(1)}, f32[24,384]{1,0:T(8,128)S(1)}, u32[]{:S(2)}, u32[]{:S(2)}) collective-permute-start(f32[24,384]{1,0:T(8,128)S(1)} %copy-done.14), channel_id=1, source_target_pairs={{0,128},{32,160},{64,192},{96,224},{128,0},{160,32},{192,64},{224,... | collective-permute-start | bytes 110600 | tf_op jit(solution)/shard_map/ppermute | solution.py:345
  52.3 9.2 %collective-permute-start.3 = (f32[24,384]{1,0:T(8,128)S(1)}, f32[24,384]{1,0:T(8,128)S(1)}, u32[]{:S(2)}, u32[]{:S(2)}) collective-permute-start(f32[24,384]{1,0:T(8,128)S(1)} %copy-done.13), channel_id=1, source_target_pairs={{0,64},{32,96},{64,0},{96,32},{128,192},{160,224},{192,128},{224,1... | collective-permute-start | bytes 110600 | tf_op jit(solution)/shard_map/ppermute | solution.py:345
  55.7 6.1 %collective-permute-start.4 = (f32[24,384]{1,0:T(8,128)S(1)}, f32[24,384]{1,0:T(8,128)S(1)}, u32[]{:S(2)}, u32[]{:S(2)}) collective-permute-start(f32[24,384]{1,0:T(8,128)S(1)} %copy-done.12), channel_id=1, source_target_pairs={{0,32},{32,0},{64,96},{96,64},{128,160},{160,128},{192,224},{224,1... | collective-permute-start | bytes 110600 | tf_op jit(solution)/shard_map/ppermute | solution.py:345
  58.7 3.2 %copy-start.4 = (f32[24,384]{1,0:T(8,128)}, f32[24,384]{1,0:T(8,128)S(1)}, u32[]{:S(2)}) copy-start(f32[24,384]{1,0:T(8,128)S(1)} %collective-permute-done.refs_1_) | copy-start | bytes 110596
  71.5 7.6 %copy-start.18 = (f32[24,256]{1,0:T(8,128)S(1)}, f32[24,256]{1,0:T(8,128)}, u32[]{:S(2)}) copy-start(f32[24,256]{1,0:T(8,128)} %get-tuple-element.32) | copy-start | bytes 73732
  71.5 18.7 %copy-start.17 = (f32[24,256]{1,0:T(8,128)S(1)}, f32[24,256]{1,0:T(8,128)}, u32[]{:S(2)}) copy-start(f32[24,256]{1,0:T(8,128)} %get-tuple-element.33) | copy-start | bytes 73732
  71.5 37.3 %all-to-all-start.1 = ((f32[32,24,256]{2,1,0:T(8,128)}), f32[32,24,256]{2,1,0:T(8,128)S(1)}, u32[]{:S(2)}, u32[]{:S(2)}) async-start(f32[32,24,256]{2,1,0:T(8,128)} %get-tuple-element.31), calls=%async_computation.1 | async-start | bytes 1572864 | tf_op jit(solution)/shard_map/all_to_all | solution.py:348
  79.1 24.0 %collective-permute-start.5 = (f32[24,256]{1,0:T(8,128)S(1)}, f32[24,256]{1,0:T(8,128)S(1)}, u32[]{:S(2)}, u32[]{:S(2)}) collective-permute-start(f32[24,256]{1,0:T(8,128)S(1)} %copy-done.18), channel_id=1, source_target_pairs={{0,512},{32,544},{64,576},{96,608},{128,640},{160,672},{192,704},{... | collective-permute-start | bytes 73736 | tf_op jit(solution)/shard_map/ppermute | solution.py:345
  90.2 18.6 %collective-permute-start.6 = (f32[24,256]{1,0:T(8,128)S(1)}, f32[24,256]{1,0:T(8,128)S(1)}, u32[]{:S(2)}, u32[]{:S(2)}) collective-permute-start(f32[24,256]{1,0:T(8,128)S(1)} %copy-done.17), channel_id=1, source_target_pairs={{0,256},{32,288},{64,320},{96,352},{128,384},{160,416},{192,448},{... | collective-permute-start | bytes 73736 | tf_op jit(solution)/shard_map/ppermute | solution.py:345
  103.1 5.7 %copy-start.2 = (f32[24,256]{1,0:T(8,128)}, f32[24,256]{1,0:T(8,128)S(1)}, u32[]{:S(2)}) copy-start(f32[24,256]{1,0:T(8,128)S(1)} %collective-permute-done.5.refs_0_.refs_1_) | copy-start | bytes 73732
  111.5 37.4 %all-to-all-start.2 = ((f32[32,3,128]{2,1,0:T(4,128)}), f32[32,3,128]{2,1,0:T(4,128)S(1)}, u32[]{:S(2)}, u32[]{:S(2)}) async-start(f32[32,3,128]{2,1,0:T(4,128)} %get-tuple-element.41), calls=%async_computation.2 | async-start | bytes 131072 | tf_op jit(solution)/shard_map/all_to_all | solution.py:380
  123.5 15.3 %collective-permute-start.7 = (f32[24,256]{1,0:T(8,128)}, f32[24,256]{1,0:T(8,128)S(1)}, u32[]{:S(2)}, u32[]{:S(2)}) collective-permute-start(f32[24,256]{1,0:T(8,128)} %get-tuple-element.37), channel_id=1, source_target_pairs={{0,128},{32,160},{64,192},{96,224},{128,0},{160,32},{192,64},{224,... | collective-permute-start | bytes 73736 | tf_op jit(solution)/shard_map/ppermute | solution.py:345
  131.1 7.7 %collective-permute-start.8 = (f32[24,256]{1,0:T(8,128)}, f32[24,256]{1,0:T(8,128)S(1)}, u32[]{:S(2)}, u32[]{:S(2)}) collective-permute-start(f32[24,256]{1,0:T(8,128)} %get-tuple-element.38), channel_id=1, source_target_pairs={{0,64},{32,96},{64,0},{96,32},{128,192},{160,224},{192,128},{224,1... | collective-permute-start | bytes 73736 | tf_op jit(solution)/shard_map/ppermute | solution.py:345
  135.4 6.0 %collective-permute-start.9 = (f32[24,256]{1,0:T(8,128)}, f32[24,256]{1,0:T(8,128)S(1)}, u32[]{:S(2)}, u32[]{:S(2)}) collective-permute-start(f32[24,256]{1,0:T(8,128)} %get-tuple-element.39), channel_id=1, source_target_pairs={{0,32},{32,0},{64,96},{96,64},{128,160},{160,128},{192,224},{224,1... | collective-permute-start | bytes 73736 | tf_op jit(solution)/shard_map/ppermute | solution.py:345
  138.8 2.6 %copy-start.9 = (f32[24,256]{1,0:T(8,128)}, f32[24,256]{1,0:T(8,128)S(1)}, u32[]{:S(2)}) copy-start(f32[24,256]{1,0:T(8,128)S(1)} %collective-permute-done.7.refs_3_) | copy-start | bytes 73732
  138.8 2.6 %copy-start.10 = (f32[24,256]{1,0:T(8,128)}, f32[24,256]{1,0:T(8,128)S(1)}, u32[]{:S(2)}) copy-start(f32[24,256]{1,0:T(8,128)S(1)} %collective-permute-done.8.refs_4_) | copy-start | bytes 73732
  (8 other events, 5.6 us)

commit v3 on v2

--- a/solution.py
+++ b/solution.py
@@ -366,7 +366,7 @@
         [shape(192, 512), shape(n_near, K, 256)] + [shape(K, 256)] * n_far,
         [VM((384, 128), F32)] * 4,
     )
-    near, early, late = spread(near), swap(far[:2]), far[2:]
+    near, late, early = spread(near), far[:2], swap(far[2:], 2)
     sums, *late = pl.pallas_call(
         functools.partial(merge_kernel, nz, len(early) + len(late)),
         out_shape=[shape(nz, 3, 128)] + [shape(K, 256)] * len(late),
@@ -378,7 +378,7 @@
         name="merge",
     )(near, *early, *late)
     sums = lax.all_to_all(sums, "z", 0, 0, tiled=True)
-    far = early + swap(late, 2)
+    far = swap(late) + early
     (final,) = call(
         functools.partial(last_kernel, levels, n_far),
         "last",

time: 150 us -> 153 us (1.020)
  the two profiles are of different devices: /device:TPU:2 before, /device:TPU:1 now
where the time goes in v3:
time: 153 us; the launch traced here: 152 us
  starting transfers between devices  109 us (71%)
  waiting for transfers between devices  21.3 us (14%)
  Pallas kernels  17.9 us (12%)
  local copies, waits for them, and re-layouts  2.54 us (2%)
    ppermute x10, starting transfers between devices, swap(): lax.ppermute(v, 'z', [(s, s ^ m) for s in range(nz)])  69.5 us
    all_to_all x2, starting transfers between devices, spread(): return lax.all_to_all(near, group, 0, 0, tiled=True)  27.5 us
    ppermute x10, waiting for transfers between devices, swap(): lax.ppermute(v, 'z', [(s, s ^ m) for s in range(nz)])  20 us
    pallas_call x3, Pallas kernels, call(): pl.pallas_call(kernel, out_shape=outs, grid=(1,), in_specs=[SMEM] * len(s...  16.1 us
    all_to_all x1, starting transfers between devices, on_device(): sums = lax.all_to_all(sums, 'z', 0, 0, tiled=True)  12 us
  transfers between devices with their start and end apart: 13, of which 7 were waited for; matrix products, arithmetic and copies ran while one was open for 0% of the time, Pallas kernels for 2%

profile of v3, /device:TPU:1, one launch (start us, length us, event | category | flops | bytes accessed | tf_op | source)
XLA Modules:
  0.0 152.3 jit_solution(2943788475172251945)
XLA Ops:
  0.6 4.4 %first.1 = (f32[192,512]{1,0:T(8,128)}, f32[384,128]{1,0:T(8,128)}, f32[384,128]{1,0:T(8,128)}, f32[32,24,384]{2,1,0:T(8,128)}, f32[24,384]{1,0:T(8,128)}, /*ind...) custom-call(s32[1]{0:T(128)} %bitcast.me, s32[10,24]{1,0:T(8,128)} %remote.5, ...), custom_call_target="tpu_custom_call" | custom-call | tf_op jit(solution)/shard_map/first/pallas_call | solution.py:318
  5.1 17.9 %all-to-all-start = ((f32[32,24,384]{2,1,0:T(8,128)}), f32[32,24,384]{2,1,0:T(8,128)S(1)}, u32[]{:S(2)}, u32[]{:S(2)}) async-start(f32[32,24,384]{2,1,0:T(8,128)} %get-tuple-element.21), calls=%async_computation | async-start | bytes 2359296 | tf_op jit(solution)/shard_map/all_to_all | solution.py:348
  23.0 19.5 %collective-permute-start = (f32[24,384]{1,0:T(8,128)S(1)}, f32[24,384]{1,0:T(8,128)S(1)}, u32[]{:S(2)}, u32[]{:S(2)}) collective-permute-start(f32[24,384]{1,0:T(8,128)S(1)} %copy-done.16), channel_id=1, source_target_pairs={{0,512},{32,544},{64,576},{96,608},{128,640},{160,672},{192,704},{... | collective-permute-start | bytes 110600 | tf_op jit(solution)/shard_map/ppermute | solution.py:345
  42.6 5.8 %collective-permute-start.1 = (f32[24,384]{1,0:T(8,128)S(1)}, f32[24,384]{1,0:T(8,128)S(1)}, u32[]{:S(2)}, u32[]{:S(2)}) collective-permute-start(f32[24,384]{1,0:T(8,128)S(1)} %copy-done.15), channel_id=1, source_target_pairs={{0,256},{32,288},{64,320},{96,352},{128,384},{160,416},{192,448},{... | collective-permute-start | bytes 110600 | tf_op jit(solution)/shard_map/ppermute | solution.py:345
  48.4 4.0 %collective-permute-start.2 = (f32[24,384]{1,0:T(8,128)S(1)}, f32[24,384]{1,0:T(8,128)S(1)}, u32[]{:S(2)}, u32[]{:S(2)}) collective-permute-start(f32[24,384]{1,0:T(8,128)S(1)} %copy-done.14), channel_id=1, source_target_pairs={{0,128},{32,160},{64,192},{96,224},{128,0},{160,32},{192,64},{224,... | collective-permute-start | bytes 110600 | tf_op jit(solution)/shard_map/ppermute | solution.py:345
  52.4 3.1 %collective-permute-start.3 = (f32[24,384]{1,0:T(8,128)S(1)}, f32[24,384]{1,0:T(8,128)S(1)}, u32[]{:S(2)}, u32[]{:S(2)}) collective-permute-start(f32[24,384]{1,0:T(8,128)S(1)} %copy-done.13), channel_id=1, source_target_pairs={{0,64},{32,96},{64,0},{96,32},{128,192},{160,224},{192,128},{224,1... | collective-permute-start | bytes 110600 | tf_op jit(solution)/shard_map/ppermute | solution.py:345
  55.6 2.6 %collective-permute-start.4 = (f32[24,384]{1,0:T(8,128)S(1)}, f32[24,384]{1,0:T(8,128)S(1)}, u32[]{:S(2)}, u32[]{:S(2)}) collective-permute-start(f32[24,384]{1,0:T(8,128)S(1)} %copy-done.12), channel_id=1, source_target_pairs={{0,32},{32,0},{64,96},{96,64},{128,160},{160,128},{192,224},{224,1... | collective-permute-start | bytes 110600 | tf_op jit(solution)/shard_map/ppermute | solution.py:345
  58.3 1.0 collective-permute-done.2.refs_3_
  59.3 1.4 collective-permute-done.4.refs_5_
  61.7 8.7 %middle.1 = (f32[192,512]{1,0:T(8,128)}, f32[32,24,256]{2,1,0:T(8,128)}, f32[24,256]{1,0:T(8,128)}, f32[24,256]{1,0:T(8,128)}, f32[24,256]{1,0:T(8,128)}, /*index=5*/f32[24,256]{1,0:T(8,128)}, f32[24,256]{1,0:T(8,128)}) custom-call(s32[1]{0:T(128)} %bitcast.me, s32[10,24]{1,0:T(8,128)} %remote.5, s32[2,40]{1,0:T(2,128)} %bitcast.3, ...), custom_call_target="tpu_custom_call" | custom-call | tf_op jit(solution)/shard_map/middle/pallas_call | solution.py:318
  70.4 9.6 %all-to-all-start.1 = ((f32[32,24,256]{2,1,0:T(8,128)}), f32[32,24,256]{2,1,0:T(8,128)S(1)}, u32[]{:S(2)}, u32[]{:S(2)}) async-start(f32[32,24,256]{2,1,0:T(8,128)} %get-tuple-element.30), calls=%async_computation.1 | async-start | bytes 1572864 | tf_op jit(solution)/shard_map/all_to_all | solution.py:348
  80.1 4.9 %collective-permute-start.5 = (f32[24,256]{1,0:T(8,128)S(1)}, f32[24,256]{1,0:T(8,128)S(1)}, u32[]{:S(2)}, u32[]{:S(2)}) collective-permute-start(f32[24,256]{1,0:T(8,128)S(1)} %copy-done.19), channel_id=1, source_target_pairs={{0,128},{32,160},{64,192},{96,224},{128,0},{160,32},{192,64},{224,... | collective-permute-start | bytes 73736 | tf_op jit(solution)/shard_map/ppermute | solution.py:345
  85.0 3.1 %collective-permute-start.6 = (f32[24,256]{1,0:T(8,128)S(1)}, f32[24,256]{1,0:T(8,128)S(1)}, u32[]{:S(2)}, u32[]{:S(2)}) collective-permute-start(f32[24,256]{1,0:T(8,128)S(1)} %copy-done.18), channel_id=1, source_target_pairs={{0,64},{32,96},{64,0},{96,32},{128,192},{160,224},{192,128},{224,1... | collective-permute-start | bytes 73736 | tf_op jit(solution)/shard_map/ppermute | solution.py:345
  88.1 2.6 %collective-permute-start.7 = (f32[24,256]{1,0:T(8,128)S(1)}, f32[24,256]{1,0:T(8,128)S(1)}, u32[]{:S(2)}, u32[]{:S(2)}) collective-permute-start(f32[24,256]{1,0:T(8,128)S(1)} %copy-done.17), channel_id=1, source_target_pairs={{0,32},{32,0},{64,96},{96,64},{128,160},{160,128},{192,224},{224,1... | collective-permute-start | bytes 73736 | tf_op jit(solution)/shard_map/ppermute | solution.py:345
  91.0 2.0 %collective-permute-done.7.refs_2_.refs_5_ = f32[24,256]{1,0:T(8,128)S(1)} collective-permute-done((f32[24,256]{1,0:T(8,128)S(1)}, f32[24,256]{1,0:T(8,128)S(1)}, u32[]{:S(2)}, u32[]{:S(2)}) %collective-permute-start.7) | collective-permute-done | bytes 24608 | tf_op jit(solution)/shard_map/ppermute | solution.py:345
  93.0 1.3 all-to-all-done.1.near.refs_0_
  94.3 0.9 copy-done
  95.2 1.8 %merge.1 = (f32[32,3,128]{2,1,0:T(4,128)}, f32[24,256]{1,0:T(8,128)}, f32[24,256]{1,0:T(8,128)}) custom-call(f32[32,24,256]{2,1,0:T(8,128)} %copy-done, f32[24,256]{1,0:T(8,128)} %copy-done.2, f32[24,256]{1,0:T(8,128)} %copy-done.3, f32[24,256]{1,0:T(8,128)} %copy-done.4, ...), custom_call_target="tpu_custom_call", output_to_operand_aliasing={{1}: (4, {}), {2}: (5, {})} | custom-call | tf_op jit(solution)/shard_map/merge/pallas_call | solution.py:370
  97.0 12.0 %all-to-all-start.2 = ((f32[32,3,128]{2,1,0:T(4,128)}), f32[32,3,128]{2,1,0:T(4,128)S(1)}, u32[]{:S(2)}, u32[]{:S(2)}) async-start(f32[32,3,128]{2,1,0:T(4,128)} %get-tuple-element.39), calls=%async_computation.2 | async-start | bytes 131072 | tf_op jit(solution)/shard_map/all_to_all | solution.py:380
  109.0 21.5 %collective-permute-start.8 = (f32[24,256]{1,0:T(8,128)}, f32[24,256]{1,0:T(8,128)S(1)}, u32[]{:S(2)}, u32[]{:S(2)}) collective-permute-start(f32[24,256]{1,0:T(8,128)} %get-tuple-element.36), channel_id=1, source_target_pairs={{0,512},{32,544},{64,576},{96,608},{128,640},{160,672},{192,704},{... | collective-permute-start | bytes 73736 | tf_op jit(solution)/shard_map/ppermute | solution.py:345
  130.5 2.2 %collective-permute-start.9 = (f32[24,256]{1,0:T(8,128)}, f32[24,256]{1,0:T(8,128)S(1)}, u32[]{:S(2)}, u32[]{:S(2)}) collective-permute-start(f32[24,256]{1,0:T(8,128)} %get-tuple-element.37), channel_id=1, source_target_pairs={{0,256},{32,288},{64,320},{96,352},{128,384},{160,416},{192,448},{... | collective-permute-start | bytes 73736 | tf_op jit(solution)/shard_map/ppermute | solution.py:345
  132.7 3.7 %collective-permute-done.8.refs_1_ = f32[24,256]{1,0:T(8,128)S(1)} collective-permute-done((f32[24,256]{1,0:T(8,128)}, f32[24,256]{1,0:T(8,128)S(1)}, u32[]{:S(2)}, u32[]{:S(2)}) %collective-permute-start.8) | collective-permute-done | bytes 24608 | tf_op jit(solution)/shard_map/ppermute | solution.py:345
  136.5 11.7 %collective-permute-done.9.refs_2_ = f32[24,256]{1,0:T(8,128)S(1)} collective-permute-done((f32[24,256]{1,0:T(8,128)}, f32[24,256]{1,0:T(8,128)S(1)}, u32[]{:S(2)}, u32[]{:S(2)}) %collective-permute-start.9) | collective-permute-done | bytes 24608 | tf_op jit(solution)/shard_map/ppermute | solution.py:345
  148.7 3.0 %last.1 = f32[64,1536]{1,0:T(8,128)} custom-call(s32[1]{0:T(128)} %bitcast.me, s32[10,24]{1,0:T(8,128)} %remote.5, f32[32,24,256]{2,1,0:T(8,128)} %copy-done, f32[24,256]{1,0:T(8,128)} %copy-done.10, f32[24,256]{1,0:T(8,128)} %copy-done.11, f32[24,256]{1,0:T(8,128)} %copy-done.2, f32[24,256]{1,0:T(8,128)} %copy-done.3, f32[24,256]{1,0:T(8,128)} %copy-done.4, ...), custom_call_target="tpu_custom_call" | custom-call | tf_op jit(solution)/shard_map/last/pallas_call | solution.py:318
  (48 shorter events, 2.5 us)
Async XLA Ops:
  5.1 17.9 %copy-start.16 = (f32[24,384]{1,0:T(8,128)S(1)}, f32[24,384]{1,0:T(8,128)}, u32[]{:S(2)}) copy-start(f32[24,384]{1,0:T(8,128)} %get-tuple-element.22) | copy-start | bytes 110596
  5.1 37.5 %copy-start.15 = (f32[24,384]{1,0:T(8,128)S(1)}, f32[24,384]{1,0:T(8,128)}, u32[]{:S(2)}) copy-start(f32[24,384]{1,0:T(8,128)} %get-tuple-element.23) | copy-start | bytes 110596
  5.1 43.3 %copy-start.14 = (f32[24,384]{1,0:T(8,128)S(1)}, f32[24,384]{1,0:T(8,128)}, u32[]{:S(2)}) copy-start(f32[24,384]{1,0:T(8,128)} %get-tuple-element.24) | copy-start | bytes 110596
  5.1 47.3 %copy-start.13 = (f32[24,384]{1,0:T(8,128)S(1)}, f32[24,384]{1,0:T(8,128)}, u32[]{:S(2)}) copy-start(f32[24,384]{1,0:T(8,128)} %get-tuple-element.25) | copy-start | bytes 110596
  5.1 50.5 %copy-start.12 = (f32[24,384]{1,0:T(8,128)S(1)}, f32[24,384]{1,0:T(8,128)}, u32[]{:S(2)}) copy-start(f32[24,384]{1,0:T(8,128)} %get-tuple-element.26) | copy-start | bytes 110596
  5.1 55.6 %all-to-all-start = ((f32[32,24,384]{2,1,0:T(8,128)}), f32[32,24,384]{2,1,0:T(8,128)S(1)}, u32[]{:S(2)}, u32[]{:S(2)}) async-start(f32[32,24,384]{2,1,0:T(8,128)} %get-tuple-element.21), calls=%async_computation | async-start | bytes 2359296 | tf_op jit(solution)/shard_map/all_to_all | solution.py:348
  23.0 35.2 %collective-permute-start = (f32[24,384]{1,0:T(8,128)S(1)}, f32[24,384]{1,0:T(8,128)S(1)}, u32[]{:S(2)}, u32[]{:S(2)}) collective-permute-start(f32[24,384]{1,0:T(8,128)S(1)} %copy-done.16), channel_id=1, source_target_pairs={{0,512},{32,544},{64,576},{96,608},{128,640},{160,672},{192,704},{... | collective-permute-start | bytes 110600 | tf_op jit(solution)/shard_map/ppermute | solution.py:345
  42.6 15.7 %collective-permute-start.1 = (f32[24,384]{1,0:T(8,128)S(1)}, f32[24,384]{1,0:T(8,128)S(1)}, u32[]{:S(2)}, u32[]{:S(2)}) collective-permute-start(f32[24,384]{1,0:T(8,128)S(1)} %copy-done.15), channel_id=1, source_target_pairs={{0,256},{32,288},{64,320},{96,352},{128,384},{160,416},{192,448},{... | collective-permute-start | bytes 110600 | tf_op jit(solution)/shard_map/ppermute | solution.py:345
  48.4 10.9 %collective-permute-start.2 = (f32[24,384]{1,0:T(8,128)S(1)}, f32[24,384]{1,0:T(8,128)S(1)}, u32[]{:S(2)}, u32[]{:S(2)}) collective-permute-start(f32[24,384]{1,0:T(8,128)S(1)} %copy-done.14), channel_id=1, source_target_pairs={{0,128},{32,160},{64,192},{96,224},{128,0},{160,32},{192,64},{224,... | collective-permute-start | bytes 110600 | tf_op jit(solution)/shard_map/ppermute | solution.py:345
  52.4 6.8 %collective-permute-start.3 = (f32[24,384]{1,0:T(8,128)S(1)}, f32[24,384]{1,0:T(8,128)S(1)}, u32[]{:S(2)}, u32[]{:S(2)}) collective-permute-start(f32[24,384]{1,0:T(8,128)S(1)} %copy-done.13), channel_id=1, source_target_pairs={{0,64},{32,96},{64,0},{96,32},{128,192},{160,224},{192,128},{224,1... | collective-permute-start | bytes 110600 | tf_op jit(solution)/shard_map/ppermute | solution.py:345
  55.6 5.1 %collective-permute-start.4 = (f32[24,384]{1,0:T(8,128)S(1)}, f32[24,384]{1,0:T(8,128)S(1)}, u32[]{:S(2)}, u32[]{:S(2)}) collective-permute-start(f32[24,384]{1,0:T(8,128)S(1)} %copy-done.12), channel_id=1, source_target_pairs={{0,32},{32,0},{64,96},{96,64},{128,160},{160,128},{192,224},{224,1... | collective-permute-start | bytes 110600 | tf_op jit(solution)/shard_map/ppermute | solution.py:345
  70.4 9.7 %copy-start.19 = (f32[24,256]{1,0:T(8,128)S(1)}, f32[24,256]{1,0:T(8,128)}, u32[]{:S(2)}) copy-start(f32[24,256]{1,0:T(8,128)} %get-tuple-element.31) | copy-start | bytes 73732
  70.4 14.6 %copy-start.18 = (f32[24,256]{1,0:T(8,128)S(1)}, f32[24,256]{1,0:T(8,128)}, u32[]{:S(2)}) copy-start(f32[24,256]{1,0:T(8,128)} %get-tuple-element.32) | copy-start | bytes 73732
  70.4 17.7 %copy-start.17 = (f32[24,256]{1,0:T(8,128)S(1)}, f32[24,256]{1,0:T(8,128)}, u32[]{:S(2)}) copy-start(f32[24,256]{1,0:T(8,128)} %get-tuple-element.33) | copy-start | bytes 73732
  70.4 23.9 %all-to-all-start.1 = ((f32[32,24,256]{2,1,0:T(8,128)}), f32[32,24,256]{2,1,0:T(8,128)S(1)}, u32[]{:S(2)}, u32[]{:S(2)}) async-start(f32[32,24,256]{2,1,0:T(8,128)} %get-tuple-element.30), calls=%async_computation.1 | async-start | bytes 1572864 | tf_op jit(solution)/shard_map/all_to_all | solution.py:348
  80.1 10.7 %collective-permute-start.5 = (f32[24,256]{1,0:T(8,128)S(1)}, f32[24,256]{1,0:T(8,128)S(1)}, u32[]{:S(2)}, u32[]{:S(2)}) collective-permute-start(f32[24,256]{1,0:T(8,128)S(1)} %copy-done.19), channel_id=1, source_target_pairs={{0,128},{32,160},{64,192},{96,224},{128,0},{160,32},{192,64},{224,... | collective-permute-start | bytes 73736 | tf_op jit(solution)/shard_map/ppermute | solution.py:345
  85.0 5.9 %collective-permute-start.6 = (f32[24,256]{1,0:T(8,128)S(1)}, f32[24,256]{1,0:T(8,128)S(1)}, u32[]{:S(2)}, u32[]{:S(2)}) collective-permute-start(f32[24,256]{1,0:T(8,128)S(1)} %copy-done.18), channel_id=1, source_target_pairs={{0,64},{32,96},{64,0},{96,32},{128,192},{160,224},{192,128},{224,1... | collective-permute-start | bytes 73736 | tf_op jit(solution)/shard_map/ppermute | solution.py:345
  88.1 4.9 %collective-permute-start.7 = (f32[24,256]{1,0:T(8,128)S(1)}, f32[24,256]{1,0:T(8,128)S(1)}, u32[]{:S(2)}, u32[]{:S(2)}) collective-permute-start(f32[24,256]{1,0:T(8,128)S(1)} %copy-done.17), channel_id=1, source_target_pairs={{0,32},{32,0},{64,96},{96,64},{128,160},{160,128},{192,224},{224,1... | collective-permute-start | bytes 73736 | tf_op jit(solution)/shard_map/ppermute | solution.py:345
  90.8 3.5 %copy-start.2 = (f32[24,256]{1,0:T(8,128)}, f32[24,256]{1,0:T(8,128)S(1)}, u32[]{:S(2)}) copy-start(f32[24,256]{1,0:T(8,128)S(1)} %collective-permute-done.5.refs_0_.refs_3_) | copy-start | bytes 73732
  91.0 3.4 %copy-start.3 = (f32[24,256]{1,0:T(8,128)}, f32[24,256]{1,0:T(8,128)S(1)}, u32[]{:S(2)}) copy-start(f32[24,256]{1,0:T(8,128)S(1)} %collective-permute-done.6.refs_1_.refs_4_) | copy-start | bytes 73732
  97.0 54.7 %all-to-all-start.2 = ((f32[32,3,128]{2,1,0:T(4,128)}), f32[32,3,128]{2,1,0:T(4,128)S(1)}, u32[]{:S(2)}, u32[]{:S(2)}) async-start(f32[32,3,128]{2,1,0:T(4,128)} %get-tuple-element.39), calls=%async_computation.2 | async-start | bytes 131072 | tf_op jit(solution)/shard_map/all_to_all | solution.py:380
  109.0 27.4 %collective-permute-start.8 = (f32[24,256]{1,0:T(8,128)}, f32[24,256]{1,0:T(8,128)S(1)}, u32[]{:S(2)}, u32[]{:S(2)}) collective-permute-start(f32[24,256]{1,0:T(8,128)} %get-tuple-element.36), channel_id=1, source_target_pairs={{0,512},{32,544},{64,576},{96,608},{128,640},{160,672},{192,704},{... | collective-permute-start | bytes 73736 | tf_op jit(solution)/shard_map/ppermute | solution.py:345
  130.5 17.6 %collective-permute-start.9 = (f32[24,256]{1,0:T(8,128)}, f32[24,256]{1,0:T(8,128)S(1)}, u32[]{:S(2)}, u32[]{:S(2)}) collective-permute-start(f32[24,256]{1,0:T(8,128)} %get-tuple-element.37), channel_id=1, source_target_pairs={{0,256},{32,288},{64,320},{96,352},{128,384},{160,416},{192,448},{... | collective-permute-start | bytes 73736 | tf_op jit(solution)/shard_map/ppermute | solution.py:345
  136.5 11.7 %copy-start.10 = (f32[24,256]{1,0:T(8,128)}, f32[24,256]{1,0:T(8,128)S(1)}, u32[]{:S(2)}) copy-start(f32[24,256]{1,0:T(8,128)S(1)} %collective-permute-done.8.refs_1_) | copy-start | bytes 73732
  (9 other events, 12.3 us)

commit v4 on v3

--- a/solution.py
+++ b/solution.py
@@ -278,7 +278,7 @@
         out_near[j, 0:12, 192:256] = sums[:, 64:128]
 
 
-def merge_kernel(copies, n_in, near, *refs):
+def merge_kernel(n_in, near, *refs):
     out = refs[n_in]
     sums = jnp.sum(near[:, :, :], axis=0)
     row = lax.broadcasted_iota(jnp.int32, (K, 128), 0)
@@ -290,7 +290,7 @@
     full = jnp.dot(sums, spread, precision=lax.Precision.HIGHEST, preferred_element_type=F32)
     full = jnp.where((row & 3) == (col >> 5), full, 0.0)
     done = jnp.concatenate([jnp.sum(full[4 * i : 4 * i + 4], axis=0, keepdims=True) for i in range(3)], axis=0)
-    for j in range(copies):
+    for j in range(out.shape[0]):
         out[j] = done
 
 
@@ -366,19 +366,17 @@
         [shape(192, 512), shape(n_near, K, 256)] + [shape(K, 256)] * n_far,
         [VM((384, 128), F32)] * 4,
     )
-    near, late, early = spread(near), far[:2], swap(far[2:], 2)
-    sums, *late = pl.pallas_call(
-        functools.partial(merge_kernel, nz, len(early) + len(late)),
-        out_shape=[shape(nz, 3, 128)] + [shape(K, 256)] * len(late),
+    near, far = spread(near), swap(far)
+    sums = pl.pallas_call(
+        functools.partial(merge_kernel, n_far),
+        out_shape=shape(nz, 3, 128),
         grid=(1,),
-        in_specs=[pl.BlockSpec((n_near, K, 128), lambda i: (0, 0, 1))] + [ANY] * (len(early) + len(late)),
-        out_specs=[pl.BlockSpec((nz, 3, 128), lambda i: (0, 0, 0))] + [ANY] * len(late),
-        input_output_aliases={1 + len(early) + i: 1 + i for i in range(len(late))},
+        in_specs=[pl.BlockSpec((n_near, K, 128), lambda i: (0, 0, 1))] + [ANY] * n_far,
+        out_specs=pl.BlockSpec((nz, 3, 128), lambda i: (0, 0, 0)),
         compiler_params=PARAMS,
         name="merge",
-    )(near, *early, *late)
+    )(near, *far)
     sums = lax.all_to_all(sums, "z", 0, 0, tiled=True)
-    far = swap(late) + early
     (final,) = call(
         functools.partial(last_kernel, levels, n_far),
         "last",

time: 153 us -> 155 us (1.013)
  the two profiles are of different devices: /device:TPU:1 before, /device:TPU:2 now
where the time goes in v4:
time: 155 us; the launch traced here: 154 us
  starting transfers between devices  106 us (68%)
  waiting for transfers between devices  26.4 us (17%)
  Pallas kernels  17.9 us (12%)
  local copies, waits for them, and re-layouts  2.54 us (2%)
    ppermute x10, starting transfers between devices, swap(): lax.ppermute(v, 'z', [(s, s ^ m) for s in range(nz)])  65.3 us
    all_to_all x2, starting transfers between devices, spread(): return lax.all_to_all(near, group, 0, 0, tiled=True)  24.5 us
    all_to_all x1, waiting for transfers between devices, on_device(): sums = lax.all_to_all(sums, 'z', 0, 0, tiled=True)  21.5 us
    all_to_all x1, starting transfers between devices, on_device(): sums = lax.all_to_all(sums, 'z', 0, 0, tiled=True)  16.1 us
    pallas_call x3, Pallas kernels, call(): pl.pallas_call(kernel, out_shape=outs, grid=(1,), in_specs=[SMEM] * len(s...  16.1 us
    ppermute x10, waiting for transfers between devices, swap(): lax.ppermute(v, 'z', [(s, s ^ m) for s in range(nz)])  4.9 us
  transfers between devices with their start and end apart: 13, of which 5 were waited for; matrix products, arithmetic and copies ran while one was open for 0% of the time, Pallas kernels for 2%

profile of v4, /device:TPU:2, one launch (start us, length us, event | category | flops | bytes accessed | tf_op | source)
XLA Modules:
  0.0 154.3 jit_solution(3220348375774765587)
XLA Ops:
  0.6 4.4 %first.1 = (f32[192,512]{1,0:T(8,128)}, f32[384,128]{1,0:T(8,128)}, f32[384,128]{1,0:T(8,128)}, f32[32,24,384]{2,1,0:T(8,128)}, f32[24,384]{1,0:T(8,128)}, /*ind...) custom-call(s32[1]{0:T(128)} %bitcast.me, s32[10,24]{1,0:T(8,128)} %remote.5, ...), custom_call_target="tpu_custom_call" | custom-call | tf_op jit(solution)/shard_map/first/pallas_call | solution.py:318
  5.1 17.0 %all-to-all-start = ((f32[32,24,384]{2,1,0:T(8,128)}), f32[32,24,384]{2,1,0:T(8,128)S(1)}, u32[]{:S(2)}, u32[]{:S(2)}) async-start(f32[32,24,384]{2,1,0:T(8,128)} %get-tuple-element.18), calls=%async_computation | async-start | bytes 2359296 | tf_op jit(solution)/shard_map/all_to_all | solution.py:348
  22.1 19.8 %collective-permute-start = (f32[24,384]{1,0:T(8,128)S(1)}, f32[24,384]{1,0:T(8,128)S(1)}, u32[]{:S(2)}, u32[]{:S(2)}) collective-permute-start(f32[24,384]{1,0:T(8,128)S(1)} %copy-done.16), channel_id=1, source_target_pairs={{0,512},{32,544},{64,576},{96,608},{128,640},{160,672},{192,704},{... | collective-permute-start | bytes 110600 | tf_op jit(solution)/shard_map/ppermute | solution.py:345
  41.9 6.1 %collective-permute-start.1 = (f32[24,384]{1,0:T(8,128)S(1)}, f32[24,384]{1,0:T(8,128)S(1)}, u32[]{:S(2)}, u32[]{:S(2)}) collective-permute-start(f32[24,384]{1,0:T(8,128)S(1)} %copy-done.15), channel_id=1, source_target_pairs={{0,256},{32,288},{64,320},{96,352},{128,384},{160,416},{192,448},{... | collective-permute-start | bytes 110600 | tf_op jit(solution)/shard_map/ppermute | solution.py:345
  48.0 4.3 %collective-permute-start.2 = (f32[24,384]{1,0:T(8,128)S(1)}, f32[24,384]{1,0:T(8,128)S(1)}, u32[]{:S(2)}, u32[]{:S(2)}) collective-permute-start(f32[24,384]{1,0:T(8,128)S(1)} %copy-done.14), channel_id=1, source_target_pairs={{0,128},{32,160},{64,192},{96,224},{128,0},{160,32},{192,64},{224,... | collective-permute-start | bytes 110600 | tf_op jit(solution)/shard_map/ppermute | solution.py:345
  52.3 3.4 %collective-permute-start.3 = (f32[24,384]{1,0:T(8,128)S(1)}, f32[24,384]{1,0:T(8,128)S(1)}, u32[]{:S(2)}, u32[]{:S(2)}) collective-permute-start(f32[24,384]{1,0:T(8,128)S(1)} %copy-done.13), channel_id=1, source_target_pairs={{0,64},{32,96},{64,0},{96,32},{128,192},{160,224},{192,128},{224,1... | collective-permute-start | bytes 110600 | tf_op jit(solution)/shard_map/ppermute | solution.py:345
  55.7 2.9 %collective-permute-start.4 = (f32[24,384]{1,0:T(8,128)S(1)}, f32[24,384]{1,0:T(8,128)S(1)}, u32[]{:S(2)}, u32[]{:S(2)}) collective-permute-start(f32[24,384]{1,0:T(8,128)S(1)} %copy-done.12), channel_id=1, source_target_pairs={{0,32},{32,0},{64,96},{96,64},{128,160},{160,128},{192,224},{224,1... | collective-permute-start | bytes 110600 | tf_op jit(solution)/shard_map/ppermute | solution.py:345
  58.7 2.8 %collective-permute-done.1.refs_2_ = f32[24,384]{1,0:T(8,128)S(1)} collective-permute-done((f32[24,384]{1,0:T(8,128)S(1)}, f32[24,384]{1,0:T(8,128)S(1)}, u32[]{:S(2)}, u32[]{:S(2)}) %collective-permute-start.1) | collective-permute-done | bytes 36896 | tf_op jit(solution)/shard_map/ppermute | solution.py:345
  62.9 8.7 %middle.1 = (f32[192,512]{1,0:T(8,128)}, f32[32,24,256]{2,1,0:T(8,128)}, f32[24,256]{1,0:T(8,128)}, f32[24,256]{1,0:T(8,128)}, f32[24,256]{1,0:T(8,128)}, /*index=5*/f32[24,256]{1,0:T(8,128)}, f32[24,256]{1,0:T(8,128)}) custom-call(s32[1]{0:T(128)} %bitcast.me, s32[10,24]{1,0:T(8,128)} %remote.5, s32[2,40]{1,0:T(2,128)} %bitcast.3, ...), custom_call_target="tpu_custom_call" | custom-call | tf_op jit(solution)/shard_map/middle/pallas_call | solution.py:318
  71.6 7.5 %all-to-all-start.1 = ((f32[32,24,256]{2,1,0:T(8,128)}), f32[32,24,256]{2,1,0:T(8,128)S(1)}, u32[]{:S(2)}, u32[]{:S(2)}) async-start(f32[32,24,256]{2,1,0:T(8,128)} %get-tuple-element.27), calls=%async_computation.1 | async-start | bytes 1572864 | tf_op jit(solution)/shard_map/all_to_all | solution.py:348
  79.1 11.1 %collective-permute-start.5 = (f32[24,256]{1,0:T(8,128)S(1)}, f32[24,256]{1,0:T(8,128)S(1)}, u32[]{:S(2)}, u32[]{:S(2)}) collective-permute-start(f32[24,256]{1,0:T(8,128)S(1)} %copy-done.21), channel_id=1, source_target_pairs={{0,512},{32,544},{64,576},{96,608},{128,640},{160,672},{192,704},{... | collective-permute-start | bytes 73736 | tf_op jit(solution)/shard_map/ppermute | solution.py:345
  90.3 2.4 %collective-permute-start.6 = (f32[24,256]{1,0:T(8,128)S(1)}, f32[24,256]{1,0:T(8,128)S(1)}, u32[]{:S(2)}, u32[]{:S(2)}) collective-permute-start(f32[24,256]{1,0:T(8,128)S(1)} %copy-done.20), channel_id=1, source_target_pairs={{0,256},{32,288},{64,320},{96,352},{128,384},{160,416},{192,448},{... | collective-permute-start | bytes 73736 | tf_op jit(solution)/shard_map/ppermute | solution.py:345
  92.7 5.5 %collective-permute-start.7 = (f32[24,256]{1,0:T(8,128)S(1)}, f32[24,256]{1,0:T(8,128)S(1)}, u32[]{:S(2)}, u32[]{:S(2)}) collective-permute-start(f32[24,256]{1,0:T(8,128)S(1)} %copy-done.19), channel_id=1, source_target_pairs={{0,128},{32,160},{64,192},{96,224},{128,0},{160,32},{192,64},{224,... | collective-permute-start | bytes 73736 | tf_op jit(solution)/shard_map/ppermute | solution.py:345
  98.3 5.7 %collective-permute-start.8 = (f32[24,256]{1,0:T(8,128)S(1)}, f32[24,256]{1,0:T(8,128)S(1)}, u32[]{:S(2)}, u32[]{:S(2)}) collective-permute-start(f32[24,256]{1,0:T(8,128)S(1)} %copy-done.18), channel_id=1, source_target_pairs={{0,64},{32,96},{64,0},{96,32},{128,192},{160,224},{192,128},{224,1... | collective-permute-start | bytes 73736 | tf_op jit(solution)/shard_map/ppermute | solution.py:345
  103.9 4.1 %collective-permute-start.9 = (f32[24,256]{1,0:T(8,128)S(1)}, f32[24,256]{1,0:T(8,128)S(1)}, u32[]{:S(2)}, u32[]{:S(2)}) collective-permute-start(f32[24,256]{1,0:T(8,128)S(1)} %copy-done.17), channel_id=1, source_target_pairs={{0,32},{32,0},{64,96},{96,64},{128,160},{160,128},{192,224},{224,1... | collective-permute-start | bytes 73736 | tf_op jit(solution)/shard_map/ppermute | solution.py:345
  108.0 0.9 collective-permute-done.6.refs_2_.refs_1_
  108.9 0.8 collective-permute-done.9.refs_5_.refs_4_
  109.8 0.6 copy-done.6
  110.4 0.9 copy-done
  111.3 1.8 %merge.1 = f32[32,3,128]{2,1,0:T(4,128)} custom-call(f32[32,24,256]{2,1,0:T(8,128)} %copy-done, f32[24,256]{1,0:T(8,128)} %copy-done.2, f32[24,256]{1,0:T(8,128)} %copy-done.3, f32[24,256]{1,0:T(8,128)} %copy-done.4, f32[24,256]{1,0:T(8,128)} %copy-done.5, f32[24,256]{1,0:T(8,128)} %copy-done.6), custom_call_target="tpu_custom_call" | custom-call | tf_op jit(solution)/shard_map/merge/pallas_call | solution.py:370
  113.1 16.1 %all-to-all-start.2 = ((f32[32,3,128]{2,1,0:T(4,128)}), f32[32,3,128]{2,1,0:T(4,128)S(1)}, u32[]{:S(2)}, u32[]{:S(2)}) async-start(f32[32,3,128]{2,1,0:T(4,128)} %merge.1), calls=%async_computation.2 | async-start | bytes 131072 | tf_op jit(solution)/shard_map/all_to_all | solution.py:379
  129.2 3.0 %last.1 = f32[64,1536]{1,0:T(8,128)} custom-call(s32[1]{0:T(128)} %bitcast.me, s32[10,24]{1,0:T(8,128)} %remote.5, f32[32,24,256]{2,1,0:T(8,128)} %copy-done, f32[24,256]{1,0:T(8,128)} %copy-done.2, f32[24,256]{1,0:T(8,128)} %copy-done.3, f32[24,256]{1,0:T(8,128)} %copy-done.4, f32[24,256]{1,0:T(8,128)} %copy-done.5, f32[24,256]{1,0:T(8,128)} %copy-done.6, ...), custom_call_target="tpu_custom_call" | custom-call | tf_op jit(solution)/shard_map/last/pallas_call | solution.py:318
  132.1 21.5 %all-to-all-done.2 = f32[32,3,128]{2,1,0:T(4,128)S(1)} async-done(((f32[32,3,128]{2,1,0:T(4,128)}), f32[32,3,128]{2,1,0:T(4,128)S(1)}, u32[]{:S(2)}, u32[]{:S(2)}) %all-to-all-start.2) | async-done | bytes 49184 | tf_op jit(solution)/shard_map/all_to_all | solution.py:379
  153.7 0.6 broadcast_multiply_fusion
  (52 shorter events, 1.5 us)
Async XLA Ops:
  5.1 17.0 %copy-start.16 = (f32[24,384]{1,0:T(8,128)S(1)}, f32[24,384]{1,0:T(8,128)}, u32[]{:S(2)}) copy-start(f32[24,384]{1,0:T(8,128)} %get-tuple-element.19) | copy-start | bytes 110596
  5.1 36.8 %copy-start.15 = (f32[24,384]{1,0:T(8,128)S(1)}, f32[24,384]{1,0:T(8,128)}, u32[]{:S(2)}) copy-start(f32[24,384]{1,0:T(8,128)} %get-tuple-element.20) | copy-start | bytes 110596
  5.1 42.9 %copy-start.14 = (f32[24,384]{1,0:T(8,128)S(1)}, f32[24,384]{1,0:T(8,128)}, u32[]{:S(2)}) copy-start(f32[24,384]{1,0:T(8,128)} %get-tuple-element.21) | copy-start | bytes 110596
  5.1 47.2 %copy-start.13 = (f32[24,384]{1,0:T(8,128)S(1)}, f32[24,384]{1,0:T(8,128)}, u32[]{:S(2)}) copy-start(f32[24,384]{1,0:T(8,128)} %get-tuple-element.22) | copy-start | bytes 110596
  5.1 50.6 %copy-start.12 = (f32[24,384]{1,0:T(8,128)S(1)}, f32[24,384]{1,0:T(8,128)}, u32[]{:S(2)}) copy-start(f32[24,384]{1,0:T(8,128)} %get-tuple-element.23) | copy-start | bytes 110596
  5.1 56.7 %all-to-all-start = ((f32[32,24,384]{2,1,0:T(8,128)}), f32[32,24,384]{2,1,0:T(8,128)S(1)}, u32[]{:S(2)}, u32[]{:S(2)}) async-start(f32[32,24,384]{2,1,0:T(8,128)} %get-tuple-element.18), calls=%async_computation | async-start | bytes 2359296 | tf_op jit(solution)/shard_map/all_to_all | solution.py:348
  22.1 36.6 %collective-permute-start = (f32[24,384]{1,0:T(8,128)S(1)}, f32[24,384]{1,0:T(8,128)S(1)}, u32[]{:S(2)}, u32[]{:S(2)}) collective-permute-start(f32[24,384]{1,0:T(8,128)S(1)} %copy-done.16), channel_id=1, source_target_pairs={{0,512},{32,544},{64,576},{96,608},{128,640},{160,672},{192,704},{... | collective-permute-start | bytes 110600 | tf_op jit(solution)/shard_map/ppermute | solution.py:345
  41.9 19.6 %collective-permute-start.1 = (f32[24,384]{1,0:T(8,128)S(1)}, f32[24,384]{1,0:T(8,128)S(1)}, u32[]{:S(2)}, u32[]{:S(2)}) collective-permute-start(f32[24,384]{1,0:T(8,128)S(1)} %copy-done.15), channel_id=1, source_target_pairs={{0,256},{32,288},{64,320},{96,352},{128,384},{160,416},{192,448},{... | collective-permute-start | bytes 110600 | tf_op jit(solution)/shard_map/ppermute | solution.py:345
  48.0 13.5 %collective-permute-start.2 = (f32[24,384]{1,0:T(8,128)S(1)}, f32[24,384]{1,0:T(8,128)S(1)}, u32[]{:S(2)}, u32[]{:S(2)}) collective-permute-start(f32[24,384]{1,0:T(8,128)S(1)} %copy-done.14), channel_id=1, source_target_pairs={{0,128},{32,160},{64,192},{96,224},{128,0},{160,32},{192,64},{224,... | collective-permute-start | bytes 110600 | tf_op jit(solution)/shard_map/ppermute | solution.py:345
  52.3 9.2 %collective-permute-start.3 = (f32[24,384]{1,0:T(8,128)S(1)}, f32[24,384]{1,0:T(8,128)S(1)}, u32[]{:S(2)}, u32[]{:S(2)}) collective-permute-start(f32[24,384]{1,0:T(8,128)S(1)} %copy-done.13), channel_id=1, source_target_pairs={{0,64},{32,96},{64,0},{96,32},{128,192},{160,224},{192,128},{224,1... | collective-permute-start | bytes 110600 | tf_op jit(solution)/shard_map/ppermute | solution.py:345
  55.7 6.1 %collective-permute-start.4 = (f32[24,384]{1,0:T(8,128)S(1)}, f32[24,384]{1,0:T(8,128)S(1)}, u32[]{:S(2)}, u32[]{:S(2)}) collective-permute-start(f32[24,384]{1,0:T(8,128)S(1)} %copy-done.12), channel_id=1, source_target_pairs={{0,32},{32,0},{64,96},{96,64},{128,160},{160,128},{192,224},{224,1... | collective-permute-start | bytes 110600 | tf_op jit(solution)/shard_map/ppermute | solution.py:345
  58.6 3.2 %copy-start.7 = (f32[24,384]{1,0:T(8,128)}, f32[24,384]{1,0:T(8,128)S(1)}, u32[]{:S(2)}) copy-start(f32[24,384]{1,0:T(8,128)S(1)} %collective-permute-done.refs_1_) | copy-start | bytes 110596
  71.5 7.6 %copy-start.21 = (f32[24,256]{1,0:T(8,128)S(1)}, f32[24,256]{1,0:T(8,128)}, u32[]{:S(2)}) copy-start(f32[24,256]{1,0:T(8,128)} %get-tuple-element.28) | copy-start | bytes 73732
  71.5 18.7 %copy-start.20 = (f32[24,256]{1,0:T(8,128)S(1)}, f32[24,256]{1,0:T(8,128)}, u32[]{:S(2)}) copy-start(f32[24,256]{1,0:T(8,128)} %get-tuple-element.29) | copy-start | bytes 73732
  71.6 21.2 %copy-start.19 = (f32[24,256]{1,0:T(8,128)S(1)}, f32[24,256]{1,0:T(8,128)}, u32[]{:S(2)}) copy-start(f32[24,256]{1,0:T(8,128)} %get-tuple-element.30) | copy-start | bytes 73732
  71.6 26.7 %copy-start.18 = (f32[24,256]{1,0:T(8,128)S(1)}, f32[24,256]{1,0:T(8,128)}, u32[]{:S(2)}) copy-start(f32[24,256]{1,0:T(8,128)} %get-tuple-element.31) | copy-start | bytes 73732
  71.6 32.3 %copy-start.17 = (f32[24,256]{1,0:T(8,128)S(1)}, f32[24,256]{1,0:T(8,128)}, u32[]{:S(2)}) copy-start(f32[24,256]{1,0:T(8,128)} %get-tuple-element.32) | copy-start | bytes 73732
  71.6 38.2 %all-to-all-start.1 = ((f32[32,24,256]{2,1,0:T(8,128)}), f32[32,24,256]{2,1,0:T(8,128)S(1)}, u32[]{:S(2)}, u32[]{:S(2)}) async-start(f32[32,24,256]{2,1,0:T(8,128)} %get-tuple-element.27), calls=%async_computation.1 | async-start | bytes 1572864 | tf_op jit(solution)/shard_map/all_to_all | solution.py:348
  79.1 28.9 %collective-permute-start.5 = (f32[24,256]{1,0:T(8,128)S(1)}, f32[24,256]{1,0:T(8,128)S(1)}, u32[]{:S(2)}, u32[]{:S(2)}) collective-permute-start(f32[24,256]{1,0:T(8,128)S(1)} %copy-done.21), channel_id=1, source_target_pairs={{0,512},{32,544},{64,576},{96,608},{128,640},{160,672},{192,704},{... | collective-permute-start | bytes 73736 | tf_op jit(solution)/shard_map/ppermute | solution.py:345
  90.3 18.6 %collective-permute-start.6 = (f32[24,256]{1,0:T(8,128)S(1)}, f32[24,256]{1,0:T(8,128)S(1)}, u32[]{:S(2)}, u32[]{:S(2)}) collective-permute-start(f32[24,256]{1,0:T(8,128)S(1)} %copy-done.20), channel_id=1, source_target_pairs={{0,256},{32,288},{64,320},{96,352},{128,384},{160,416},{192,448},{... | collective-permute-start | bytes 73736 | tf_op jit(solution)/shard_map/ppermute | solution.py:345
  92.7 16.2 %collective-permute-start.7 = (f32[24,256]{1,0:T(8,128)S(1)}, f32[24,256]{1,0:T(8,128)S(1)}, u32[]{:S(2)}, u32[]{:S(2)}) collective-permute-start(f32[24,256]{1,0:T(8,128)S(1)} %copy-done.19), channel_id=1, source_target_pairs={{0,128},{32,160},{64,192},{96,224},{128,0},{160,32},{192,64},{224,... | collective-permute-start | bytes 73736 | tf_op jit(solution)/shard_map/ppermute | solution.py:345
  98.3 10.7 %collective-permute-start.8 = (f32[24,256]{1,0:T(8,128)S(1)}, f32[24,256]{1,0:T(8,128)S(1)}, u32[]{:S(2)}, u32[]{:S(2)}) collective-permute-start(f32[24,256]{1,0:T(8,128)S(1)} %copy-done.18), channel_id=1, source_target_pairs={{0,64},{32,96},{64,0},{96,32},{128,192},{160,224},{192,128},{224,1... | collective-permute-start | bytes 73736 | tf_op jit(solution)/shard_map/ppermute | solution.py:345
  103.9 5.9 %collective-permute-start.9 = (f32[24,256]{1,0:T(8,128)S(1)}, f32[24,256]{1,0:T(8,128)S(1)}, u32[]{:S(2)}, u32[]{:S(2)}) collective-permute-start(f32[24,256]{1,0:T(8,128)S(1)} %copy-done.17), channel_id=1, source_target_pairs={{0,32},{32,0},{64,96},{96,64},{128,160},{160,128},{192,224},{224,1... | collective-permute-start | bytes 73736 | tf_op jit(solution)/shard_map/ppermute | solution.py:345
  113.1 40.6 %all-to-all-start.2 = ((f32[32,3,128]{2,1,0:T(4,128)}), f32[32,3,128]{2,1,0:T(4,128)S(1)}, u32[]{:S(2)}, u32[]{:S(2)}) async-start(f32[32,3,128]{2,1,0:T(4,128)} %merge.1), calls=%async_computation.2 | async-start | bytes 131072 | tf_op jit(solution)/shard_map/all_to_all | solution.py:379
  (11 other events, 9.5 us)

commit v5 on v3

--- a/solution.py
+++ b/solution.py
@@ -327,6 +327,23 @@
     )(*scalars, *arrays)
 
 
+def hold_kernel(*refs):
+    pass
+
+
+def hold(arrays):
+    n = len(arrays)
+    return pl.pallas_call(
+        hold_kernel,
+        out_shape=[jax.ShapeDtypeStruct(a.shape, a.dtype) for a in arrays],
+        in_specs=[ANY] * n,
+        out_specs=[ANY] * n,
+        input_output_aliases={i: i for i in range(n)},
+        cost_estimate=pl.CostEstimate(flops=40_000_000_000, bytes_accessed=0, transcendentals=0),
+        name="hold",
+    )(*arrays)
+
+
 def on_device(sizes, state, geo, mass, weight, bins, pairs, remote):
     nz, nx, ny, nc = sizes
     group = ("x", "y", "c")
@@ -358,6 +375,7 @@
         [VM((384, 128), F32)] * 3,
     )
     near, far = spread(near), swap(far)
+    far = [*hold(far[:1]), *far[1:]]
     part, near, *far = call(
         functools.partial(middle_kernel, levels, n_far),
         "middle",
@@ -366,19 +384,19 @@
         [shape(192, 512), shape(n_near, K, 256)] + [shape(K, 256)] * n_far,
         [VM((384, 128), F32)] * 4,
     )
-    near, late, early = spread(near), far[:2], swap(far[2:], 2)
+    near, late = spread(near), far[2:]
     sums, *late = pl.pallas_call(
-        functools.partial(merge_kernel, nz, len(early) + len(late)),
+        functools.partial(merge_kernel, nz, len(late)),
         out_shape=[shape(nz, 3, 128)] + [shape(K, 256)] * len(late),
         grid=(1,),
-        in_specs=[pl.BlockSpec((n_near, K, 128), lambda i: (0, 0, 1))] + [ANY] * (len(early) + len(late)),
+        in_specs=[pl.BlockSpec((n_near, K, 128), lambda i: (0, 0, 1))] + [ANY] * len(late),
         out_specs=[pl.BlockSpec((nz, 3, 128), lambda i: (0, 0, 0))] + [ANY] * len(late),
-        input_output_aliases={1 + len(early) + i: 1 + i for i in range(len(late))},
+        input_output_aliases={1 + i: 1 + i for i in range(len(late))},
         compiler_params=PARAMS,
         name="merge",
-    )(near, *early, *late)
+    )(near, *late)
     sums = lax.all_to_all(sums, "z", 0, 0, tiled=True)
-    far = swap(late) + early
+    far = [*hold(swap(far[:2])), *swap(late, 2)]
     (final,) = call(
         functools.partial(last_kernel, levels, n_far),
         "last",

time: 153 us -> 141 us (0.922)
  the two profiles are of different devices: /device:TPU:1 before, /device:TPU:2 now
where the time goes in v5:
time: 141 us
  starting transfers between devices  108 us (77%)
  Pallas kernels  17.8 us (13%)
  waiting for transfers between devices  8.48 us (6%)
  local copies, waits for them, and re-layouts  4.33 us (3%)
    ppermute x10, starting transfers between devices, swap(): lax.ppermute(v, 'z', [(s, s ^ m) for s in range(nz)])  74 us
    all_to_all x1, starting transfers between devices, on_device(): sums = lax.all_to_all(sums, 'z', 0, 0, tiled=True)  19 us
    pallas_call x3, Pallas kernels, call(): pl.pallas_call(kernel, out_shape=outs, grid=(1,), in_specs=[SMEM] * len(s...  16 us
    all_to_all x2, starting transfers between devices, spread(): return lax.all_to_all(near, group, 0, 0, tiled=True)  15.3 us
    all_to_all x1, waiting for transfers between devices, on_device(): sums = lax.all_to_all(sums, 'z', 0, 0, tiled=True)  4.57 us
    unnamed x36, local copies, waits for them, and re-layouts  4.33 us
    ppermute x10, waiting for transfers between devices, swap(): lax.ppermute(v, 'z', [(s, s ^ m) for s in range(nz)])  3.91 us
  transfers between devices with their start and end apart: 13, of which 4 were waited for; matrix products, arithmetic and copies ran while one was open for 0% of the time, Pallas kernels for 3%

profile of v5, /device:TPU:2, one launch (start us, length us, event | category | flops | bytes accessed | tf_op | source)
XLA Modules:
  0.0 140.5 jit_solution(18404093979454908689)
XLA Ops:
  0.6 4.4 %first.1 = (f32[192,512]{1,0:T(8,128)}, f32[384,128]{1,0:T(8,128)}, f32[384,128]{1,0:T(8,128)}, f32[32,24,384]{2,1,0:T(8,128)}, f32[24,384]{1,0:T(8,128)}, /*ind...) custom-call(s32[1]{0:T(128)} %bitcast.me, s32[10,24]{1,0:T(8,128)} %remote.5, ...), custom_call_target="tpu_custom_call" | custom-call | tf_op jit(solution)/shard_map/first/pallas_call | solution.py:318
  5.0 29.0 %collective-permute-start = (f32[24,384]{1,0:T(8,128)}, f32[24,384]{1,0:T(8,128)S(1)}, u32[]{:S(2)}, u32[]{:S(2)}) collective-permute-start(f32[24,384]{1,0:T(8,128)} %get-tuple-element.25), channel_id=1, source_target_pairs={{0,512},{32,544},{64,576},{96,608},{128,640},{160,672},{192,704},{... | collective-permute-start | bytes 110600 | tf_op jit(solution)/shard_map/ppermute | solution.py:362
  34.1 7.8 %all-to-all-start = ((f32[32,24,384]{2,1,0:T(8,128)}), f32[32,24,384]{2,1,0:T(8,128)S(1)}, u32[]{:S(2)}, u32[]{:S(2)}) async-start(f32[32,24,384]{2,1,0:T(8,128)} %get-tuple-element.24), calls=%async_computation | async-start | bytes 2359296 | tf_op jit(solution)/shard_map/all_to_all | solution.py:365
  41.9 6.1 %collective-permute-start.1 = (f32[24,384]{1,0:T(8,128)S(1)}, f32[24,384]{1,0:T(8,128)S(1)}, u32[]{:S(2)}, u32[]{:S(2)}) collective-permute-start(f32[24,384]{1,0:T(8,128)S(1)} %copy-done.15), channel_id=1, source_target_pairs={{0,256},{32,288},{64,320},{96,352},{128,384},{160,416},{192,448},{... | collective-permute-start | bytes 110600 | tf_op jit(solution)/shard_map/ppermute | solution.py:362
  48.0 4.3 %collective-permute-start.2 = (f32[24,384]{1,0:T(8,128)S(1)}, f32[24,384]{1,0:T(8,128)S(1)}, u32[]{:S(2)}, u32[]{:S(2)}) collective-permute-start(f32[24,384]{1,0:T(8,128)S(1)} %copy-done.14), channel_id=1, source_target_pairs={{0,128},{32,160},{64,192},{96,224},{128,0},{160,32},{192,64},{224,... | collective-permute-start | bytes 110600 | tf_op jit(solution)/shard_map/ppermute | solution.py:362
  52.3 3.4 %collective-permute-start.3 = (f32[24,384]{1,0:T(8,128)S(1)}, f32[24,384]{1,0:T(8,128)S(1)}, u32[]{:S(2)}, u32[]{:S(2)}) collective-permute-start(f32[24,384]{1,0:T(8,128)S(1)} %copy-done.13), channel_id=1, source_target_pairs={{0,64},{32,96},{64,0},{96,32},{128,192},{160,224},{192,128},{224,1... | collective-permute-start | bytes 110600 | tf_op jit(solution)/shard_map/ppermute | solution.py:362
  55.7 2.9 %collective-permute-start.4 = (f32[24,384]{1,0:T(8,128)S(1)}, f32[24,384]{1,0:T(8,128)S(1)}, u32[]{:S(2)}, u32[]{:S(2)}) collective-permute-start(f32[24,384]{1,0:T(8,128)S(1)} %copy-done.12), channel_id=1, source_target_pairs={{0,32},{32,0},{64,96},{96,64},{128,160},{160,128},{192,224},{224,1... | collective-permute-start | bytes 110600 | tf_op jit(solution)/shard_map/ppermute | solution.py:362
  58.6 0.6 copy-done.6
  59.2 2.5 %collective-permute-done.1.refs_2_ = f32[24,384]{1,0:T(8,128)S(1)} collective-permute-done((f32[24,384]{1,0:T(8,128)S(1)}, f32[24,384]{1,0:T(8,128)S(1)}, u32[]{:S(2)}, u32[]{:S(2)}) %collective-permute-start.1) | collective-permute-done | bytes 36896 | tf_op jit(solution)/shard_map/ppermute | solution.py:362
  62.9 8.6 %middle.1 = (f32[192,512]{1,0:T(8,128)}, f32[32,24,256]{2,1,0:T(8,128)}, f32[24,256]{1,0:T(8,128)}, f32[24,256]{1,0:T(8,128)}, f32[24,256]{1,0:T(8,128)}, /*index=5*/f32[24,256]{1,0:T(8,128)}, f32[24,256]{1,0:T(8,128)}) custom-call(s32[1]{0:T(128)} %bitcast.me, s32[10,24]{1,0:T(8,128)} %remote.5, s32[2,40]{1,0:T(2,128)} %bitcast.3, ...), custom_call_target="tpu_custom_call" | custom-call | tf_op jit(solution)/shard_map/middle/pallas_call | solution.py:318
  71.5 7.5 %all-to-all-start.1 = ((f32[32,24,256]{2,1,0:T(8,128)}), f32[32,24,256]{2,1,0:T(8,128)S(1)}, u32[]{:S(2)}, u32[]{:S(2)}) async-start(f32[32,24,256]{2,1,0:T(8,128)} %get-tuple-element.33), calls=%async_computation.1 | async-start | bytes 1572864 | tf_op jit(solution)/shard_map/all_to_all | solution.py:365
  79.1 11.1 %collective-permute-start.5 = (f32[24,256]{1,0:T(8,128)S(1)}, f32[24,256]{1,0:T(8,128)S(1)}, u32[]{:S(2)}, u32[]{:S(2)}) collective-permute-start(f32[24,256]{1,0:T(8,128)S(1)} %copy-done.17), channel_id=1, source_target_pairs={{0,512},{32,544},{64,576},{96,608},{128,640},{160,672},{192,704},{... | collective-permute-start | bytes 73736 | tf_op jit(solution)/shard_map/ppermute | solution.py:362
  90.2 1.9 %collective-permute-start.6 = (f32[24,256]{1,0:T(8,128)S(1)}, f32[24,256]{1,0:T(8,128)S(1)}, u32[]{:S(2)}, u32[]{:S(2)}) collective-permute-start(f32[24,256]{1,0:T(8,128)S(1)} %copy-done.16), channel_id=1, source_target_pairs={{0,256},{32,288},{64,320},{96,352},{128,384},{160,416},{192,448},{... | collective-permute-start | bytes 73736 | tf_op jit(solution)/shard_map/ppermute | solution.py:362
  92.2 0.9 copy-done
  93.0 1.8 %merge.1 = (f32[32,3,128]{2,1,0:T(4,128)}, f32[24,256]{1,0:T(8,128)}, f32[24,256]{1,0:T(8,128)}, f32[24,256]{1,0:T(8,128)}) custom-call(f32[32,24,256]{2,1,0:T(8,128)} %copy-done, f32[24,256]{1,0:T(8,128)} %get-tuple-element.38.refs_0_, f32[24,256]{1,0:T(8,128)} %get-tuple-element.39.refs_1_, ...), custom_call_target="tpu_custom_call", output_to_operand_aliasing={{1}: (1, {}), {2}: (2, {}), {3}: (3, {})} | custom-call | tf_op jit(solution)/shard_map/merge/pallas_call | solution.py:388
  94.9 19.0 %all-to-all-start.2 = ((f32[32,3,128]{2,1,0:T(4,128)}), f32[32,3,128]{2,1,0:T(4,128)S(1)}, u32[]{:S(2)}, u32[]{:S(2)}) async-start(f32[32,3,128]{2,1,0:T(4,128)} %get-tuple-element.45), calls=%async_computation.2 | async-start | bytes 131072 | tf_op jit(solution)/shard_map/all_to_all | solution.py:398
  113.9 7.6 %collective-permute-start.7 = (f32[24,256]{1,0:T(8,128)}, f32[24,256]{1,0:T(8,128)S(1)}, u32[]{:S(2)}, u32[]{:S(2)}) collective-permute-start(f32[24,256]{1,0:T(8,128)} %get-tuple-element.41), channel_id=1, source_target_pairs={{0,128},{32,160},{64,192},{96,224},{128,0},{160,32},{192,64},{224,... | collective-permute-start | bytes 73736 | tf_op jit(solution)/shard_map/ppermute | solution.py:362
  121.5 4.3 %collective-permute-start.8 = (f32[24,256]{1,0:T(8,128)}, f32[24,256]{1,0:T(8,128)S(1)}, u32[]{:S(2)}, u32[]{:S(2)}) collective-permute-start(f32[24,256]{1,0:T(8,128)} %get-tuple-element.42), channel_id=1, source_target_pairs={{0,64},{32,96},{64,0},{96,32},{128,192},{160,224},{192,128},{224,1... | collective-permute-start | bytes 73736 | tf_op jit(solution)/shard_map/ppermute | solution.py:362
  125.8 3.4 %collective-permute-start.9 = (f32[24,256]{1,0:T(8,128)}, f32[24,256]{1,0:T(8,128)S(1)}, u32[]{:S(2)}, u32[]{:S(2)}) collective-permute-start(f32[24,256]{1,0:T(8,128)} %get-tuple-element.43), channel_id=1, source_target_pairs={{0,32},{32,0},{64,96},{96,64},{128,160},{160,128},{192,224},{224,1... | collective-permute-start | bytes 73736 | tf_op jit(solution)/shard_map/ppermute | solution.py:362
  129.8 0.6 copy-done.8
  130.4 1.3 collective-permute-done.9.refs_5_
  131.7 0.6 copy-done.11
  132.3 3.0 %last.1 = f32[64,1536]{1,0:T(8,128)} custom-call(s32[1]{0:T(128)} %bitcast.me, s32[10,24]{1,0:T(8,128)} %remote.5, f32[32,24,256]{2,1,0:T(8,128)} %copy-done, f32[24,256]{1,0:T(8,128)} %get-tuple-element.36.refs_1_, f32[24,256]{1,0:T(8,128)} %get-tuple-element.37.refs_2_, f32[24,256]{1,0:T(8,128)} %copy-done.9, f32[24,256]{1,0:T(8,128)} %copy-done.10, ...), custom_call_target="tpu_custom_call" | custom-call | tf_op jit(solution)/shard_map/last/pallas_call | solution.py:318
  135.3 4.6 %all-to-all-done.2 = f32[32,3,128]{2,1,0:T(4,128)S(1)} async-done(((f32[32,3,128]{2,1,0:T(4,128)}), f32[32,3,128]{2,1,0:T(4,128)S(1)}, u32[]{:S(2)}, u32[]{:S(2)}) %all-to-all-start.2) | async-done | bytes 49184 | tf_op jit(solution)/shard_map/all_to_all | solution.py:398
  (46 shorter events, 2.4 us)
Async XLA Ops:
  5.0 53.6 %collective-permute-start = (f32[24,384]{1,0:T(8,128)}, f32[24,384]{1,0:T(8,128)S(1)}, u32[]{:S(2)}, u32[]{:S(2)}) collective-permute-start(f32[24,384]{1,0:T(8,128)} %get-tuple-element.25), channel_id=1, source_target_pairs={{0,512},{32,544},{64,576},{96,608},{128,640},{160,672},{192,704},{... | collective-permute-start | bytes 110600 | tf_op jit(solution)/shard_map/ppermute | solution.py:362
  34.0 7.8 %copy-start.15 = (f32[24,384]{1,0:T(8,128)S(1)}, f32[24,384]{1,0:T(8,128)}, u32[]{:S(2)}) copy-start(f32[24,384]{1,0:T(8,128)} %get-tuple-element.26) | copy-start | bytes 110596
  34.0 13.9 %copy-start.14 = (f32[24,384]{1,0:T(8,128)S(1)}, f32[24,384]{1,0:T(8,128)}, u32[]{:S(2)}) copy-start(f32[24,384]{1,0:T(8,128)} %get-tuple-element.27) | copy-start | bytes 110596
  34.0 18.2 %copy-start.13 = (f32[24,384]{1,0:T(8,128)S(1)}, f32[24,384]{1,0:T(8,128)}, u32[]{:S(2)}) copy-start(f32[24,384]{1,0:T(8,128)} %get-tuple-element.28) | copy-start | bytes 110596
  34.1 21.6 %copy-start.12 = (f32[24,384]{1,0:T(8,128)S(1)}, f32[24,384]{1,0:T(8,128)}, u32[]{:S(2)}) copy-start(f32[24,384]{1,0:T(8,128)} %get-tuple-element.29) | copy-start | bytes 110596
  34.1 27.8 %all-to-all-start = ((f32[32,24,384]{2,1,0:T(8,128)}), f32[32,24,384]{2,1,0:T(8,128)S(1)}, u32[]{:S(2)}, u32[]{:S(2)}) async-start(f32[32,24,384]{2,1,0:T(8,128)} %get-tuple-element.24), calls=%async_computation | async-start | bytes 2359296 | tf_op jit(solution)/shard_map/all_to_all | solution.py:365
  41.9 19.9 %collective-permute-start.1 = (f32[24,384]{1,0:T(8,128)S(1)}, f32[24,384]{1,0:T(8,128)S(1)}, u32[]{:S(2)}, u32[]{:S(2)}) collective-permute-start(f32[24,384]{1,0:T(8,128)S(1)} %copy-done.15), channel_id=1, source_target_pairs={{0,256},{32,288},{64,320},{96,352},{128,384},{160,416},{192,448},{... | collective-permute-start | bytes 110600 | tf_op jit(solution)/shard_map/ppermute | solution.py:362
  48.0 13.8 %collective-permute-start.2 = (f32[24,384]{1,0:T(8,128)S(1)}, f32[24,384]{1,0:T(8,128)S(1)}, u32[]{:S(2)}, u32[]{:S(2)}) collective-permute-start(f32[24,384]{1,0:T(8,128)S(1)} %copy-done.14), channel_id=1, source_target_pairs={{0,128},{32,160},{64,192},{96,224},{128,0},{160,32},{192,64},{224,... | collective-permute-start | bytes 110600 | tf_op jit(solution)/shard_map/ppermute | solution.py:362
  52.3 9.5 %collective-permute-start.3 = (f32[24,384]{1,0:T(8,128)S(1)}, f32[24,384]{1,0:T(8,128)S(1)}, u32[]{:S(2)}, u32[]{:S(2)}) collective-permute-start(f32[24,384]{1,0:T(8,128)S(1)} %copy-done.13), channel_id=1, source_target_pairs={{0,64},{32,96},{64,0},{96,32},{128,192},{160,224},{192,128},{224,1... | collective-permute-start | bytes 110600 | tf_op jit(solution)/shard_map/ppermute | solution.py:362
  55.7 6.1 %collective-permute-start.4 = (f32[24,384]{1,0:T(8,128)S(1)}, f32[24,384]{1,0:T(8,128)S(1)}, u32[]{:S(2)}, u32[]{:S(2)}) collective-permute-start(f32[24,384]{1,0:T(8,128)S(1)} %copy-done.12), channel_id=1, source_target_pairs={{0,32},{32,0},{64,96},{96,64},{128,160},{160,128},{192,224},{224,1... | collective-permute-start | bytes 110600 | tf_op jit(solution)/shard_map/ppermute | solution.py:362
  61.8 0.6 copy-start.4
  61.8 1.0 copy-start.1
  71.5 7.6 %copy-start.17 = (f32[24,256]{1,0:T(8,128)S(1)}, f32[24,256]{1,0:T(8,128)}, u32[]{:S(2)}) copy-start(f32[24,256]{1,0:T(8,128)} %get-tuple-element.34) | copy-start | bytes 73732
  71.5 18.7 %copy-start.16 = (f32[24,256]{1,0:T(8,128)S(1)}, f32[24,256]{1,0:T(8,128)}, u32[]{:S(2)}) copy-start(f32[24,256]{1,0:T(8,128)} %get-tuple-element.35) | copy-start | bytes 73732
  71.5 20.6 %all-to-all-start.1 = ((f32[32,24,256]{2,1,0:T(8,128)}), f32[32,24,256]{2,1,0:T(8,128)S(1)}, u32[]{:S(2)}, u32[]{:S(2)}) async-start(f32[32,24,256]{2,1,0:T(8,128)} %get-tuple-element.33), calls=%async_computation.1 | async-start | bytes 1572864 | tf_op jit(solution)/shard_map/all_to_all | solution.py:365
  79.1 50.1 %collective-permute-start.5 = (f32[24,256]{1,0:T(8,128)S(1)}, f32[24,256]{1,0:T(8,128)S(1)}, u32[]{:S(2)}, u32[]{:S(2)}) collective-permute-start(f32[24,256]{1,0:T(8,128)S(1)} %copy-done.17), channel_id=1, source_target_pairs={{0,512},{32,544},{64,576},{96,608},{128,640},{160,672},{192,704},{... | collective-permute-start | bytes 73736 | tf_op jit(solution)/shard_map/ppermute | solution.py:362
  90.2 39.0 %collective-permute-start.6 = (f32[24,256]{1,0:T(8,128)S(1)}, f32[24,256]{1,0:T(8,128)S(1)}, u32[]{:S(2)}, u32[]{:S(2)}) collective-permute-start(f32[24,256]{1,0:T(8,128)S(1)} %copy-done.16), channel_id=1, source_target_pairs={{0,256},{32,288},{64,320},{96,352},{128,384},{160,416},{192,448},{... | collective-permute-start | bytes 73736 | tf_op jit(solution)/shard_map/ppermute | solution.py:362
  92.2 0.9 copy-start
  94.9 45.0 %all-to-all-start.2 = ((f32[32,3,128]{2,1,0:T(4,128)}), f32[32,3,128]{2,1,0:T(4,128)S(1)}, u32[]{:S(2)}, u32[]{:S(2)}) async-start(f32[32,3,128]{2,1,0:T(4,128)} %get-tuple-element.45), calls=%async_computation.2 | async-start | bytes 131072 | tf_op jit(solution)/shard_map/all_to_all | solution.py:398
  113.9 16.5 %collective-permute-start.7 = (f32[24,256]{1,0:T(8,128)}, f32[24,256]{1,0:T(8,128)S(1)}, u32[]{:S(2)}, u32[]{:S(2)}) collective-permute-start(f32[24,256]{1,0:T(8,128)} %get-tuple-element.41), channel_id=1, source_target_pairs={{0,128},{32,160},{64,192},{96,224},{128,0},{160,32},{192,64},{224,... | collective-permute-start | bytes 73736 | tf_op jit(solution)/shard_map/ppermute | solution.py:362
  121.5 8.9 %collective-permute-start.8 = (f32[24,256]{1,0:T(8,128)}, f32[24,256]{1,0:T(8,128)S(1)}, u32[]{:S(2)}, u32[]{:S(2)}) collective-permute-start(f32[24,256]{1,0:T(8,128)} %get-tuple-element.42), channel_id=1, source_target_pairs={{0,64},{32,96},{64,0},{96,32},{128,192},{160,224},{192,128},{224,1... | collective-permute-start | bytes 73736 | tf_op jit(solution)/shard_map/ppermute | solution.py:362
  125.8 5.9 %collective-permute-start.9 = (f32[24,256]{1,0:T(8,128)}, f32[24,256]{1,0:T(8,128)S(1)}, u32[]{:S(2)}, u32[]{:S(2)}) collective-permute-start(f32[24,256]{1,0:T(8,128)} %get-tuple-element.43), channel_id=1, source_target_pairs={{0,32},{32,0},{64,96},{96,64},{128,160},{160,128},{192,224},{224,1... | collective-permute-start | bytes 73736 | tf_op jit(solution)/shard_map/ppermute | solution.py:362
  130.4 1.3 copy-start.9
  130.4 1.3 copy-start.10
  (7 other events, 4.2 us)

commit v6 on v5

--- a/solution.py
+++ b/solution.py
@@ -278,7 +278,7 @@
         out_near[j, 0:12, 192:256] = sums[:, 64:128]
 
 
-def merge_kernel(copies, n_in, near, *refs):
+def merge_kernel(n_in, near, *refs):
     out = refs[n_in]
     sums = jnp.sum(near[:, :, :], axis=0)
     row = lax.broadcasted_iota(jnp.int32, (K, 128), 0)
@@ -290,8 +290,20 @@
     full = jnp.dot(sums, spread, precision=lax.Precision.HIGHEST, preferred_element_type=F32)
     full = jnp.where((row & 3) == (col >> 5), full, 0.0)
     done = jnp.concatenate([jnp.sum(full[4 * i : 4 * i + 4], axis=0, keepdims=True) for i in range(3)], axis=0)
-    for j in range(copies):
-        out[j] = done
+    out[...] = done
+
+
+def copies_kernel(n_in, sums, *refs):
+    out = refs[n_in]
+    for j in range(out.shape[0]):
+        out[j] = sums[...]
+
+
+def total_kernel(planes, scale, z, parts, out):
+    acc = parts[z[0]]
+    for plane in range(1, planes):
+        acc = acc + parts[lax.rem(z[0] + (planes - plane), planes)]
+    out[...] = acc * scale
 
 
 def last_kernel(levels, n_far, me, remote, *refs):
@@ -386,17 +398,32 @@
     )
     near, late = spread(near), far[2:]
     sums, *late = pl.pallas_call(
-        functools.partial(merge_kernel, nz, len(late)),
-        out_shape=[shape(nz, 3, 128)] + [shape(K, 256)] * len(late),
+        functools.partial(merge_kernel, len(late)),
+        out_shape=[shape(3, 128)] + [shape(K, 256)] * len(late),
         grid=(1,),
         in_specs=[pl.BlockSpec((n_near, K, 128), lambda i: (0, 0, 1))] + [ANY] * len(late),
-        out_specs=[pl.BlockSpec((nz, 3, 128), lambda i: (0, 0, 0))] + [ANY] * len(late),
+        out_specs=[pl.BlockSpec((3, 128), lambda i: (0, 0))] + [ANY] * len(late),
         input_output_aliases={1 + i: 1 + i for i in range(len(late))},
         compiler_params=PARAMS,
         name="merge",
     )(near, *late)
-    sums = lax.all_to_all(sums, "z", 0, 0, tiled=True)
-    far = [*hold(swap(far[:2])), *swap(late, 2)]
+    hop = [(z * n_near + m, (z + m) % nz * n_near + m) for z in range(nz) for m in range(n_near)]
+    sums = lax.ppermute(sums, ("z", *group), hop)
+    mids, tail = swap(late[:2], 2), late[2:]
+    held = hold(swap(far[:2]))
+    gone = [*held, *mids]
+    sums, *tail = pl.pallas_call(
+        functools.partial(copies_kernel, len(gone) + len(tail)),
+        out_shape=[shape(n_near, 3, 128)] + [shape(K, 256)] * len(tail),
+        grid=(1,),
+        in_specs=[whole(sums)] + [ANY] * (len(gone) + len(tail)),
+        out_specs=[pl.BlockSpec((n_near, 3, 128), lambda i: (0, 0, 0))] + [ANY] * len(tail),
+        input_output_aliases={1 + len(gone) + i: 1 + i for i in range(len(tail))},
+        compiler_params=PARAMS,
+        name="copies",
+    )(sums, *gone, *tail)
+    sums = spread(sums)
+    far = [*gone, *swap(tail, 4)]
     (final,) = call(
         functools.partial(last_kernel, levels, n_far),
         "last",
@@ -406,7 +433,15 @@
         [VM((384, 128), F32)] * 2,
     )
     points = nz * n_near * E * 512
-    return final, jnp.sum(sums, axis=0) * (1.0 / math.sqrt(points / NBIN))
+    (gradient,) = call(
+        functools.partial(total_kernel, nz, 1.0 / math.sqrt(points / NBIN)),
+        "total",
+        [lax.axis_index("z").astype(jnp.int32).reshape(1)],
+        [sums],
+        [shape(3, 128)],
+        [],
+    )
+    return final, gradient
 
 
 def solution(mesh):

time: 141 us -> 146 us (1.035)
  the two profiles are of different devices: /device:TPU:2 before, /device:TPU:1 now
where the time goes in v6:
time: 146 us; the launch traced here: 145 us
  starting transfers between devices  110 us (75%)
  Pallas kernels  20.6 us (14%)
  waiting for transfers between devices  8.25 us (6%)
  local copies, waits for them, and re-layouts  4.96 us (3%)
    ppermute x10, starting transfers between devices, swap(): lax.ppermute(v, 'z', [(s, s ^ m) for s in range(nz)])  69.2 us
    all_to_all x3, starting transfers between devices, spread(): return lax.all_to_all(near, group, 0, 0, tiled=True)  38.7 us
    pallas_call x4, Pallas kernels, call(): pl.pallas_call(kernel, out_shape=outs, grid=(1,), in_specs=[SMEM] * len(s...  17.5 us
    ppermute x10, waiting for transfers between devices, swap(): lax.ppermute(v, 'z', [(s, s ^ m) for s in range(nz)])  6.81 us
    unnamed x40, local copies, waits for them, and re-layouts  4.96 us
  transfers between devices with their start and end apart: 14, of which 6 were waited for; matrix products, arithmetic and copies ran while one was open for 0% of the time, Pallas kernels for 3%

profile of v6, /device:TPU:1, one launch (start us, length us, event | category | flops | bytes accessed | tf_op | source)
XLA Modules:
  0.0 145.0 jit_solution(4549218584127202650)
XLA Ops:
  0.6 4.4 %first.1 = (f32[192,512]{1,0:T(8,128)}, f32[384,128]{1,0:T(8,128)}, f32[384,128]{1,0:T(8,128)}, f32[32,24,384]{2,1,0:T(8,128)}, f32[24,384]{1,0:T(8,128)}, /*ind...) custom-call(s32[1]{0:T(128)} %bitcast.me, s32[10,24]{1,0:T(8,128)} %remote.5, ...), custom_call_target="tpu_custom_call" | custom-call | tf_op jit(solution)/shard_map/first/pallas_call | solution.py:330
  5.1 29.5 %collective-permute-start = (f32[24,384]{1,0:T(8,128)}, f32[24,384]{1,0:T(8,128)S(1)}, u32[]{:S(2)}, u32[]{:S(2)}) collective-permute-start(f32[24,384]{1,0:T(8,128)} %get-tuple-element.27), channel_id=1, source_target_pairs={{0,512},{32,544},{64,576},{96,608},{128,640},{160,672},{192,704},{... | collective-permute-start | bytes 110600 | tf_op jit(solution)/shard_map/ppermute | solution.py:374
  34.6 8.2 %all-to-all-start = ((f32[32,24,384]{2,1,0:T(8,128)}), f32[32,24,384]{2,1,0:T(8,128)S(1)}, u32[]{:S(2)}, u32[]{:S(2)}) async-start(f32[32,24,384]{2,1,0:T(8,128)} %get-tuple-element.26), calls=%async_computation | async-start | bytes 2359296 | tf_op jit(solution)/shard_map/all_to_all | solution.py:377
  42.8 5.8 %collective-permute-start.1 = (f32[24,384]{1,0:T(8,128)S(1)}, f32[24,384]{1,0:T(8,128)S(1)}, u32[]{:S(2)}, u32[]{:S(2)}) collective-permute-start(f32[24,384]{1,0:T(8,128)S(1)} %copy-done.17), channel_id=1, source_target_pairs={{0,256},{32,288},{64,320},{96,352},{128,384},{160,416},{192,448},{... | collective-permute-start | bytes 110600 | tf_op jit(solution)/shard_map/ppermute | solution.py:374
  48.7 4.0 %collective-permute-start.2 = (f32[24,384]{1,0:T(8,128)S(1)}, f32[24,384]{1,0:T(8,128)S(1)}, u32[]{:S(2)}, u32[]{:S(2)}) collective-permute-start(f32[24,384]{1,0:T(8,128)S(1)} %copy-done.16), channel_id=1, source_target_pairs={{0,128},{32,160},{64,192},{96,224},{128,0},{160,32},{192,64},{224,... | collective-permute-start | bytes 110600 | tf_op jit(solution)/shard_map/ppermute | solution.py:374
  52.7 3.1 %collective-permute-start.3 = (f32[24,384]{1,0:T(8,128)S(1)}, f32[24,384]{1,0:T(8,128)S(1)}, u32[]{:S(2)}, u32[]{:S(2)}) collective-permute-start(f32[24,384]{1,0:T(8,128)S(1)} %copy-done.15), channel_id=1, source_target_pairs={{0,64},{32,96},{64,0},{96,32},{128,192},{160,224},{192,128},{224,1... | collective-permute-start | bytes 110600 | tf_op jit(solution)/shard_map/ppermute | solution.py:374
  55.8 2.6 %collective-permute-start.4 = (f32[24,384]{1,0:T(8,128)S(1)}, f32[24,384]{1,0:T(8,128)S(1)}, u32[]{:S(2)}, u32[]{:S(2)}) collective-permute-start(f32[24,384]{1,0:T(8,128)S(1)} %copy-done.14), channel_id=1, source_target_pairs={{0,32},{32,0},{64,96},{96,64},{128,160},{160,128},{192,224},{224,1... | collective-permute-start | bytes 110600 | tf_op jit(solution)/shard_map/ppermute | solution.py:374
  59.1 2.1 %collective-permute-done.2.refs_3_ = f32[24,384]{1,0:T(8,128)S(1)} collective-permute-done((f32[24,384]{1,0:T(8,128)S(1)}, f32[24,384]{1,0:T(8,128)S(1)}, u32[]{:S(2)}, u32[]{:S(2)}) %collective-permute-start.2) | collective-permute-done | bytes 36896 | tf_op jit(solution)/shard_map/ppermute | solution.py:374
  62.3 8.7 %middle.1 = (f32[192,512]{1,0:T(8,128)}, f32[32,24,256]{2,1,0:T(8,128)}, f32[24,256]{1,0:T(8,128)}, f32[24,256]{1,0:T(8,128)}, f32[24,256]{1,0:T(8,128)}, /*index=5*/f32[24,256]{1,0:T(8,128)}, f32[24,256]{1,0:T(8,128)}) custom-call(s32[1]{0:T(128)} %bitcast.me, s32[10,24]{1,0:T(8,128)} %remote.5, s32[2,40]{1,0:T(2,128)} %bitcast.4, ...), custom_call_target="tpu_custom_call" | custom-call | tf_op jit(solution)/shard_map/middle/pallas_call | solution.py:330
  71.0 9.1 %all-to-all-start.1 = ((f32[32,24,256]{2,1,0:T(8,128)}), f32[32,24,256]{2,1,0:T(8,128)S(1)}, u32[]{:S(2)}, u32[]{:S(2)}) async-start(f32[32,24,256]{2,1,0:T(8,128)} %get-tuple-element.35), calls=%async_computation.1 | async-start | bytes 1572864 | tf_op jit(solution)/shard_map/all_to_all | solution.py:377
  80.1 10.8 %collective-permute-start.5 = (f32[24,256]{1,0:T(8,128)S(1)}, f32[24,256]{1,0:T(8,128)S(1)}, u32[]{:S(2)}, u32[]{:S(2)}) collective-permute-start(f32[24,256]{1,0:T(8,128)S(1)} %copy-done.19), channel_id=1, source_target_pairs={{0,512},{32,544},{64,576},{96,608},{128,640},{160,672},{192,704},{... | collective-permute-start | bytes 73736 | tf_op jit(solution)/shard_map/ppermute | solution.py:374
  90.9 1.9 %collective-permute-start.6 = (f32[24,256]{1,0:T(8,128)S(1)}, f32[24,256]{1,0:T(8,128)S(1)}, u32[]{:S(2)}, u32[]{:S(2)}) collective-permute-start(f32[24,256]{1,0:T(8,128)S(1)} %copy-done.18), channel_id=1, source_target_pairs={{0,256},{32,288},{64,320},{96,352},{128,384},{160,416},{192,448},{... | collective-permute-start | bytes 73736 | tf_op jit(solution)/shard_map/ppermute | solution.py:374
  92.9 1.4 all-to-all-done.1.near.refs_0_
  95.2 1.8 %merge.1 = (f32[3,128]{1,0:T(4,128)}, f32[24,256]{1,0:T(8,128)}, f32[24,256]{1,0:T(8,128)}, f32[24,256]{1,0:T(8,128)}) custom-call(f32[32,24,256]{2,1,0:T(8,128)} %copy-done, f32[24,256]{1,0:T(8,128)} %get-tuple-element.40.refs_0_, f32[24,256]{1,0:T(8,128)} %get-tuple-element.41.refs_1_, ...), custom_call_target="tpu_custom_call", output_to_operand_aliasing={{1}: (1, {}), {2}: (2, {}), {3}: (3, {})} | custom-call | tf_op jit(solution)/shard_map/merge/pallas_call | solution.py:400
  97.0 2.3 %collective-permute-start.9 = (f32[3,128]{1,0:T(4,128)}, f32[3,128]{1,0:T(4,128)S(1)}, u32[]{:S(2)}, u32[]{:S(2)}) collective-permute-start(f32[3,128]{1,0:T(4,128)} %get-tuple-element.45), channel_id=1, source_target_pairs={{0,0},{1,33},{2,66},{3,99},{4,132},{5,165},{6,198},{7,231},{8,264}... | collective-permute-start | bytes 4616 | tf_op jit(solution)/shard_map/ppermute | solution.py:411
  99.3 5.2 %collective-permute-start.7 = (f32[24,256]{1,0:T(8,128)}, f32[24,256]{1,0:T(8,128)S(1)}, u32[]{:S(2)}, u32[]{:S(2)}) collective-permute-start(f32[24,256]{1,0:T(8,128)} %get-tuple-element.43), channel_id=1, source_target_pairs={{0,128},{32,160},{64,192},{96,224},{128,0},{160,32},{192,64},{224,... | collective-permute-start | bytes 73736 | tf_op jit(solution)/shard_map/ppermute | solution.py:374
  104.5 3.5 %collective-permute-start.8 = (f32[24,256]{1,0:T(8,128)}, f32[24,256]{1,0:T(8,128)S(1)}, u32[]{:S(2)}, u32[]{:S(2)}) collective-permute-start(f32[24,256]{1,0:T(8,128)} %get-tuple-element.44), channel_id=1, source_target_pairs={{0,64},{32,96},{64,0},{96,32},{128,192},{160,224},{192,128},{224,1... | collective-permute-start | bytes 73736 | tf_op jit(solution)/shard_map/ppermute | solution.py:374
  108.1 1.3 collective-permute-done.6.refs_1_
  111.5 1.3 copies.1
  112.8 21.5 %all-to-all-start.2 = ((f32[32,3,128]{2,1,0:T(4,128)}), f32[32,3,128]{2,1,0:T(4,128)S(1)}, u32[]{:S(2)}, u32[]{:S(2)}) async-start(f32[32,3,128]{2,1,0:T(4,128)} %get-tuple-element.49), calls=%async_computation.2 | async-start | bytes 131072 | tf_op jit(solution)/shard_map/all_to_all | solution.py:377
  134.3 2.6 %collective-permute-start.10 = (f32[24,256]{1,0:T(8,128)}, f32[24,256]{1,0:T(8,128)S(1)}, u32[]{:S(2)}, u32[]{:S(2)}) collective-permute-start(f32[24,256]{1,0:T(8,128)} %get-tuple-element.47), channel_id=1, source_target_pairs={{0,32},{32,0},{64,96},{96,64},{128,160},{160,128},{192,224},{224,1... | collective-permute-start | bytes 73736 | tf_op jit(solution)/shard_map/ppermute | solution.py:374
  136.9 2.4 %collective-permute-done.10.refs_5_ = f32[24,256]{1,0:T(8,128)S(1)} collective-permute-done((f32[24,256]{1,0:T(8,128)}, f32[24,256]{1,0:T(8,128)S(1)}, u32[]{:S(2)}, u32[]{:S(2)}) %collective-permute-start.10) | collective-permute-done | bytes 24608 | tf_op jit(solution)/shard_map/ppermute | solution.py:374
  139.9 3.0 %last.1 = f32[64,1536]{1,0:T(8,128)} custom-call(s32[1]{0:T(128)} %bitcast.me, s32[10,24]{1,0:T(8,128)} %remote.5, f32[32,24,256]{2,1,0:T(8,128)} %copy-done, f32[24,256]{1,0:T(8,128)} %get-tuple-element.38.refs_0_.refs_1_, f32[24,256]{1,0:T(8,128)} %get-tuple-element.39.refs_1_.refs_2_, f32[24,256]{1,0:T(8,128)} %copy-done.3, f32[24,256]{1,0:T(8,128)} %copy-done.4, ...), custom_call_target="tpu_custom_call" | custom-call | tf_op jit(solution)/shard_map/last/pallas_call | solution.py:330
  143.6 1.5 %total.1 = f32[3,128]{1,0:T(4,128)} custom-call(s32[1]{0:T(128)} %bitcast.2.z, f32[32,3,128]{2,1,0:T(4,128)} %copy-done.2), custom_call_target="tpu_custom_call" | custom-call | tf_op jit(solution)/shard_map/total/pallas_call | solution.py:330
  (52 shorter events, 5.9 us)
Async XLA Ops:
  5.1 53.4 %collective-permute-start = (f32[24,384]{1,0:T(8,128)}, f32[24,384]{1,0:T(8,128)S(1)}, u32[]{:S(2)}, u32[]{:S(2)}) collective-permute-start(f32[24,384]{1,0:T(8,128)} %get-tuple-element.27), channel_id=1, source_target_pairs={{0,512},{32,544},{64,576},{96,608},{128,640},{160,672},{192,704},{... | collective-permute-start | bytes 110600 | tf_op jit(solution)/shard_map/ppermute | solution.py:374
  34.6 8.2 %copy-start.17 = (f32[24,384]{1,0:T(8,128)S(1)}, f32[24,384]{1,0:T(8,128)}, u32[]{:S(2)}) copy-start(f32[24,384]{1,0:T(8,128)} %get-tuple-element.28) | copy-start | bytes 110596
  34.6 14.1 %copy-start.16 = (f32[24,384]{1,0:T(8,128)S(1)}, f32[24,384]{1,0:T(8,128)}, u32[]{:S(2)}) copy-start(f32[24,384]{1,0:T(8,128)} %get-tuple-element.29) | copy-start | bytes 110596
  34.6 18.1 %copy-start.15 = (f32[24,384]{1,0:T(8,128)S(1)}, f32[24,384]{1,0:T(8,128)}, u32[]{:S(2)}) copy-start(f32[24,384]{1,0:T(8,128)} %get-tuple-element.30) | copy-start | bytes 110596
  34.6 21.2 %copy-start.14 = (f32[24,384]{1,0:T(8,128)S(1)}, f32[24,384]{1,0:T(8,128)}, u32[]{:S(2)}) copy-start(f32[24,384]{1,0:T(8,128)} %get-tuple-element.31) | copy-start | bytes 110596
  34.6 26.6 %all-to-all-start = ((f32[32,24,384]{2,1,0:T(8,128)}), f32[32,24,384]{2,1,0:T(8,128)S(1)}, u32[]{:S(2)}, u32[]{:S(2)}) async-start(f32[32,24,384]{2,1,0:T(8,128)} %get-tuple-element.26), calls=%async_computation | async-start | bytes 2359296 | tf_op jit(solution)/shard_map/all_to_all | solution.py:377
  42.8 16.3 %collective-permute-start.1 = (f32[24,384]{1,0:T(8,128)S(1)}, f32[24,384]{1,0:T(8,128)S(1)}, u32[]{:S(2)}, u32[]{:S(2)}) collective-permute-start(f32[24,384]{1,0:T(8,128)S(1)} %copy-done.17), channel_id=1, source_target_pairs={{0,256},{32,288},{64,320},{96,352},{128,384},{160,416},{192,448},{... | collective-permute-start | bytes 110600 | tf_op jit(solution)/shard_map/ppermute | solution.py:374
  48.7 12.6 %collective-permute-start.2 = (f32[24,384]{1,0:T(8,128)S(1)}, f32[24,384]{1,0:T(8,128)S(1)}, u32[]{:S(2)}, u32[]{:S(2)}) collective-permute-start(f32[24,384]{1,0:T(8,128)S(1)} %copy-done.16), channel_id=1, source_target_pairs={{0,128},{32,160},{64,192},{96,224},{128,0},{160,32},{192,64},{224,... | collective-permute-start | bytes 110600 | tf_op jit(solution)/shard_map/ppermute | solution.py:374
  52.7 8.5 %collective-permute-start.3 = (f32[24,384]{1,0:T(8,128)S(1)}, f32[24,384]{1,0:T(8,128)S(1)}, u32[]{:S(2)}, u32[]{:S(2)}) collective-permute-start(f32[24,384]{1,0:T(8,128)S(1)} %copy-done.15), channel_id=1, source_target_pairs={{0,64},{32,96},{64,0},{96,32},{128,192},{160,224},{192,128},{224,1... | collective-permute-start | bytes 110600 | tf_op jit(solution)/shard_map/ppermute | solution.py:374
  55.8 5.4 %collective-permute-start.4 = (f32[24,384]{1,0:T(8,128)S(1)}, f32[24,384]{1,0:T(8,128)S(1)}, u32[]{:S(2)}, u32[]{:S(2)}) collective-permute-start(f32[24,384]{1,0:T(8,128)S(1)} %copy-done.14), channel_id=1, source_target_pairs={{0,32},{32,0},{64,96},{96,64},{128,160},{160,128},{192,224},{224,1... | collective-permute-start | bytes 110600 | tf_op jit(solution)/shard_map/ppermute | solution.py:374
  59.1 2.2 %copy-start.7 = (f32[24,384]{1,0:T(8,128)}, f32[24,384]{1,0:T(8,128)S(1)}, u32[]{:S(2)}) copy-start(f32[24,384]{1,0:T(8,128)S(1)} %collective-permute-done.1.refs_2_) | copy-start | bytes 110596
  61.3 1.0 copy-start.1
  71.0 9.1 %copy-start.19 = (f32[24,256]{1,0:T(8,128)S(1)}, f32[24,256]{1,0:T(8,128)}, u32[]{:S(2)}) copy-start(f32[24,256]{1,0:T(8,128)} %get-tuple-element.36) | copy-start | bytes 73732
  71.0 19.9 %copy-start.18 = (f32[24,256]{1,0:T(8,128)S(1)}, f32[24,256]{1,0:T(8,128)}, u32[]{:S(2)}) copy-start(f32[24,256]{1,0:T(8,128)} %get-tuple-element.37) | copy-start | bytes 73732
  71.0 23.3 %all-to-all-start.1 = ((f32[32,24,256]{2,1,0:T(8,128)}), f32[32,24,256]{2,1,0:T(8,128)S(1)}, u32[]{:S(2)}, u32[]{:S(2)}) async-start(f32[32,24,256]{2,1,0:T(8,128)} %get-tuple-element.35), calls=%async_computation.1 | async-start | bytes 1572864 | tf_op jit(solution)/shard_map/all_to_all | solution.py:377
  80.1 28.0 %collective-permute-start.5 = (f32[24,256]{1,0:T(8,128)S(1)}, f32[24,256]{1,0:T(8,128)S(1)}, u32[]{:S(2)}, u32[]{:S(2)}) collective-permute-start(f32[24,256]{1,0:T(8,128)S(1)} %copy-done.19), channel_id=1, source_target_pairs={{0,512},{32,544},{64,576},{96,608},{128,640},{160,672},{192,704},{... | collective-permute-start | bytes 73736 | tf_op jit(solution)/shard_map/ppermute | solution.py:374
  90.9 18.5 %collective-permute-start.6 = (f32[24,256]{1,0:T(8,128)S(1)}, f32[24,256]{1,0:T(8,128)S(1)}, u32[]{:S(2)}, u32[]{:S(2)}) collective-permute-start(f32[24,256]{1,0:T(8,128)S(1)} %copy-done.18), channel_id=1, source_target_pairs={{0,256},{32,288},{64,320},{96,352},{128,384},{160,416},{192,448},{... | collective-permute-start | bytes 73736 | tf_op jit(solution)/shard_map/ppermute | solution.py:374
  97.0 13.0 %collective-permute-start.9 = (f32[3,128]{1,0:T(4,128)}, f32[3,128]{1,0:T(4,128)S(1)}, u32[]{:S(2)}, u32[]{:S(2)}) collective-permute-start(f32[3,128]{1,0:T(4,128)} %get-tuple-element.45), channel_id=1, source_target_pairs={{0,0},{1,33},{2,66},{3,99},{4,132},{5,165},{6,198},{7,231},{8,264}... | collective-permute-start | bytes 4616 | tf_op jit(solution)/shard_map/ppermute | solution.py:411
  99.3 11.3 %collective-permute-start.7 = (f32[24,256]{1,0:T(8,128)}, f32[24,256]{1,0:T(8,128)S(1)}, u32[]{:S(2)}, u32[]{:S(2)}) collective-permute-start(f32[24,256]{1,0:T(8,128)} %get-tuple-element.43), channel_id=1, source_target_pairs={{0,128},{32,160},{64,192},{96,224},{128,0},{160,32},{192,64},{224,... | collective-permute-start | bytes 73736 | tf_op jit(solution)/shard_map/ppermute | solution.py:374
  104.5 6.4 %collective-permute-start.8 = (f32[24,256]{1,0:T(8,128)}, f32[24,256]{1,0:T(8,128)S(1)}, u32[]{:S(2)}, u32[]{:S(2)}) collective-permute-start(f32[24,256]{1,0:T(8,128)} %get-tuple-element.44), channel_id=1, source_target_pairs={{0,64},{32,96},{64,0},{96,32},{128,192},{160,224},{192,128},{224,1... | collective-permute-start | bytes 73736 | tf_op jit(solution)/shard_map/ppermute | solution.py:374
  108.1 1.3 copy-start.5
  110.0 0.9 copy-start.13
  112.8 30.1 %all-to-all-start.2 = ((f32[32,3,128]{2,1,0:T(4,128)}), f32[32,3,128]{2,1,0:T(4,128)S(1)}, u32[]{:S(2)}, u32[]{:S(2)}) async-start(f32[32,3,128]{2,1,0:T(4,128)} %get-tuple-element.49), calls=%async_computation.2 | async-start | bytes 131072 | tf_op jit(solution)/shard_map/all_to_all | solution.py:377
  134.3 5.1 %collective-permute-start.10 = (f32[24,256]{1,0:T(8,128)}, f32[24,256]{1,0:T(8,128)S(1)}, u32[]{:S(2)}, u32[]{:S(2)}) collective-permute-start(f32[24,256]{1,0:T(8,128)} %get-tuple-element.47), channel_id=1, source_target_pairs={{0,32},{32,0},{64,96},{96,64},{128,160},{160,128},{192,224},{224,1... | collective-permute-start | bytes 73736 | tf_op jit(solution)/shard_map/ppermute | solution.py:374
  (10 other events, 6.4 us)

commit v7 on v5

--- a/solution.py
+++ b/solution.py
@@ -289,7 +289,7 @@
     sums = jnp.where((row < 12) & (col >= 64) & (col < 96), sums, 0.0)
     full = jnp.dot(sums, spread, precision=lax.Precision.HIGHEST, preferred_element_type=F32)
     full = jnp.where((row & 3) == (col >> 5), full, 0.0)
-    done = jnp.concatenate([jnp.sum(full[4 * i : 4 * i + 4], axis=0, keepdims=True) for i in range(3)], axis=0)
+    done = jnp.concatenate([jnp.sum(full[4 * i : 4 * i + 4], axis=0, keepdims=True) for i in range(3)], axis=1)
     for j in range(copies):
         out[j] = done
 
@@ -387,10 +387,10 @@
     near, late = spread(near), far[2:]
     sums, *late = pl.pallas_call(
         functools.partial(merge_kernel, nz, len(late)),
-        out_shape=[shape(nz, 3, 128)] + [shape(K, 256)] * len(late),
+        out_shape=[shape(nz, 1, 384)] + [shape(K, 256)] * len(late),
         grid=(1,),
         in_specs=[pl.BlockSpec((n_near, K, 128), lambda i: (0, 0, 1))] + [ANY] * len(late),
-        out_specs=[pl.BlockSpec((nz, 3, 128), lambda i: (0, 0, 0))] + [ANY] * len(late),
+        out_specs=[pl.BlockSpec((nz, 1, 384), lambda i: (0, 0, 0))] + [ANY] * len(late),
         input_output_aliases={1 + i: 1 + i for i in range(len(late))},
         compiler_params=PARAMS,
         name="merge",
@@ -406,7 +406,7 @@
         [VM((384, 128), F32)] * 2,
     )
     points = nz * n_near * E * 512
-    return final, jnp.sum(sums, axis=0) * (1.0 / math.sqrt(points / NBIN))
+    return final, jnp.sum(sums, axis=0).reshape(3, 128) * (1.0 / math.sqrt(points / NBIN))
 
 
 def solution(mesh):

time: 141 us -> 140 us (level)
  the two profiles are of different devices: /device:TPU:2 before, /device:TPU:1 now
where the time goes in v7:
time: 140 us; the launch traced here: 137 us
  starting transfers between devices  106 us (76%)
  Pallas kernels  17.8 us (13%)
  waiting for transfers between devices  7.26 us (5%)
  local copies, waits for them, and re-layouts  4.32 us (3%)
    ppermute x10, starting transfers between devices, swap(): lax.ppermute(v, 'z', [(s, s ^ m) for s in range(nz)])  72 us
    all_to_all x2, starting transfers between devices, spread(): return lax.all_to_all(near, group, 0, 0, tiled=True)  17.3 us
    all_to_all x1, starting transfers between devices, on_device(): sums = lax.all_to_all(sums, 'z', 0, 0, tiled=True)  17.1 us
    pallas_call x3, Pallas kernels, call(): pl.pallas_call(kernel, out_shape=outs, grid=(1,), in_specs=[SMEM] * len(s...  16 us
    unnamed x36, local copies, waits for them, and re-layouts  4.32 us
    all_to_all x1, waiting for transfers between devices, on_device(): sums = lax.all_to_all(sums, 'z', 0, 0, tiled=True)  2.92 us
    ppermute x10, waiting for transfers between devices, swap(): lax.ppermute(v, 'z', [(s, s ^ m) for s in range(nz)])  2.91 us
  transfers between devices with their start and end apart: 13, of which 4 were waited for; matrix products, arithmetic and copies ran while one was open for 0% of the time, Pallas kernels for 3%

profile of v7, /device:TPU:1, one launch (start us, length us, event | category | flops | bytes accessed | tf_op | source)
XLA Modules:
  0.0 137.3 jit_solution(18016430030951107832)
XLA Ops:
  0.6 4.4 %first.1 = (f32[192,512]{1,0:T(8,128)}, f32[384,128]{1,0:T(8,128)}, f32[384,128]{1,0:T(8,128)}, f32[32,24,384]{2,1,0:T(8,128)}, f32[24,384]{1,0:T(8,128)}, /*ind...) custom-call(s32[1]{0:T(128)} %bitcast.me, s32[10,24]{1,0:T(8,128)} %remote.5, ...), custom_call_target="tpu_custom_call" | custom-call | tf_op jit(solution)/shard_map/first/pallas_call | solution.py:318
  5.1 29.5 %collective-permute-start = (f32[24,384]{1,0:T(8,128)}, f32[24,384]{1,0:T(8,128)S(1)}, u32[]{:S(2)}, u32[]{:S(2)}) collective-permute-start(f32[24,384]{1,0:T(8,128)} %get-tuple-element.25), channel_id=1, source_target_pairs={{0,512},{32,544},{64,576},{96,608},{128,640},{160,672},{192,704},{... | collective-permute-start | bytes 110600 | tf_op jit(solution)/shard_map/ppermute | solution.py:362
  34.6 8.2 %all-to-all-start = ((f32[32,24,384]{2,1,0:T(8,128)}), f32[32,24,384]{2,1,0:T(8,128)S(1)}, u32[]{:S(2)}, u32[]{:S(2)}) async-start(f32[32,24,384]{2,1,0:T(8,128)} %get-tuple-element.24), calls=%async_computation | async-start | bytes 2359296 | tf_op jit(solution)/shard_map/all_to_all | solution.py:365
  42.8 5.8 %collective-permute-start.1 = (f32[24,384]{1,0:T(8,128)S(1)}, f32[24,384]{1,0:T(8,128)S(1)}, u32[]{:S(2)}, u32[]{:S(2)}) collective-permute-start(f32[24,384]{1,0:T(8,128)S(1)} %copy-done.15), channel_id=1, source_target_pairs={{0,256},{32,288},{64,320},{96,352},{128,384},{160,416},{192,448},{... | collective-permute-start | bytes 110600 | tf_op jit(solution)/shard_map/ppermute | solution.py:362
  48.7 4.0 %collective-permute-start.2 = (f32[24,384]{1,0:T(8,128)S(1)}, f32[24,384]{1,0:T(8,128)S(1)}, u32[]{:S(2)}, u32[]{:S(2)}) collective-permute-start(f32[24,384]{1,0:T(8,128)S(1)} %copy-done.14), channel_id=1, source_target_pairs={{0,128},{32,160},{64,192},{96,224},{128,0},{160,32},{192,64},{224,... | collective-permute-start | bytes 110600 | tf_op jit(solution)/shard_map/ppermute | solution.py:362
  52.7 3.1 %collective-permute-start.3 = (f32[24,384]{1,0:T(8,128)S(1)}, f32[24,384]{1,0:T(8,128)S(1)}, u32[]{:S(2)}, u32[]{:S(2)}) collective-permute-start(f32[24,384]{1,0:T(8,128)S(1)} %copy-done.13), channel_id=1, source_target_pairs={{0,64},{32,96},{64,0},{96,32},{128,192},{160,224},{192,128},{224,1... | collective-permute-start | bytes 110600 | tf_op jit(solution)/shard_map/ppermute | solution.py:362
  55.8 2.6 %collective-permute-start.4 = (f32[24,384]{1,0:T(8,128)S(1)}, f32[24,384]{1,0:T(8,128)S(1)}, u32[]{:S(2)}, u32[]{:S(2)}) collective-permute-start(f32[24,384]{1,0:T(8,128)S(1)} %copy-done.12), channel_id=1, source_target_pairs={{0,32},{32,0},{64,96},{96,64},{128,160},{160,128},{192,224},{224,1... | collective-permute-start | bytes 110600 | tf_op jit(solution)/shard_map/ppermute | solution.py:362
  59.1 2.1 %collective-permute-done.2.refs_3_ = f32[24,384]{1,0:T(8,128)S(1)} collective-permute-done((f32[24,384]{1,0:T(8,128)S(1)}, f32[24,384]{1,0:T(8,128)S(1)}, u32[]{:S(2)}, u32[]{:S(2)}) %collective-permute-start.2) | collective-permute-done | bytes 36896 | tf_op jit(solution)/shard_map/ppermute | solution.py:362
  62.3 8.6 %middle.1 = (f32[192,512]{1,0:T(8,128)}, f32[32,24,256]{2,1,0:T(8,128)}, f32[24,256]{1,0:T(8,128)}, f32[24,256]{1,0:T(8,128)}, f32[24,256]{1,0:T(8,128)}, /*index=5*/f32[24,256]{1,0:T(8,128)}, f32[24,256]{1,0:T(8,128)}) custom-call(s32[1]{0:T(128)} %bitcast.me, s32[10,24]{1,0:T(8,128)} %remote.5, s32[2,40]{1,0:T(2,128)} %bitcast.5, ...), custom_call_target="tpu_custom_call" | custom-call | tf_op jit(solution)/shard_map/middle/pallas_call | solution.py:318
  71.0 9.1 %all-to-all-start.1 = ((f32[32,24,256]{2,1,0:T(8,128)}), f32[32,24,256]{2,1,0:T(8,128)S(1)}, u32[]{:S(2)}, u32[]{:S(2)}) async-start(f32[32,24,256]{2,1,0:T(8,128)} %get-tuple-element.33), calls=%async_computation.1 | async-start | bytes 1572864 | tf_op jit(solution)/shard_map/all_to_all | solution.py:365
  80.0 10.8 %collective-permute-start.5 = (f32[24,256]{1,0:T(8,128)S(1)}, f32[24,256]{1,0:T(8,128)S(1)}, u32[]{:S(2)}, u32[]{:S(2)}) collective-permute-start(f32[24,256]{1,0:T(8,128)S(1)} %copy-done.17), channel_id=1, source_target_pairs={{0,512},{32,544},{64,576},{96,608},{128,640},{160,672},{192,704},{... | collective-permute-start | bytes 73736 | tf_op jit(solution)/shard_map/ppermute | solution.py:362
  90.9 1.9 %collective-permute-start.6 = (f32[24,256]{1,0:T(8,128)S(1)}, f32[24,256]{1,0:T(8,128)S(1)}, u32[]{:S(2)}, u32[]{:S(2)}) collective-permute-start(f32[24,256]{1,0:T(8,128)S(1)} %copy-done.16), channel_id=1, source_target_pairs={{0,256},{32,288},{64,320},{96,352},{128,384},{160,416},{192,448},{... | collective-permute-start | bytes 73736 | tf_op jit(solution)/shard_map/ppermute | solution.py:362
  92.8 1.4 %all-to-all-done.1.near.refs_0_ = f32[32,24,256]{2,1,0:T(8,128)S(1)} async-done(((f32[32,24,256]{2,1,0:T(8,128)}), f32[32,24,256]{2,1,0:T(8,128)S(1)}, u32[]{:S(2)}, u32[]{:S(2)}) %all-to-all-start.1) | async-done | bytes 786464 | tf_op jit(solution)/shard_map/all_to_all | solution.py:365
  94.3 0.9 copy-done
  95.2 1.8 %merge.1 = (f32[32,1,384]{2,1,0:T(1,128)}, f32[24,256]{1,0:T(8,128)}, f32[24,256]{1,0:T(8,128)}, f32[24,256]{1,0:T(8,128)}) custom-call(f32[32,24,256]{2,1,0:T(8,128)} %copy-done, f32[24,256]{1,0:T(8,128)} %get-tuple-element.38.refs_0_, f32[24,256]{1,0:T(8,128)} %get-tuple-element.39.refs_1_, ...), custom_call_target="tpu_custom_call", output_to_operand_aliasing={{1}: (1, {}), {2}: (2, {}), {3}: (3, {})} | custom-call | tf_op jit(solution)/shard_map/merge/pallas_call | solution.py:388
  97.0 17.1 %all-to-all-start.2 = ((f32[32,1,384]{2,1,0:T(1,128)}), f32[32,1,384]{2,1,0:T(1,128)S(1)}, u32[]{:S(2)}, u32[]{:S(2)}) async-start(f32[32,1,384]{2,1,0:T(1,128)} %get-tuple-element.45), calls=%async_computation.2 | async-start | bytes 98304 | tf_op jit(solution)/shard_map/all_to_all | solution.py:398
  114.0 7.0 %collective-permute-start.7 = (f32[24,256]{1,0:T(8,128)}, f32[24,256]{1,0:T(8,128)S(1)}, u32[]{:S(2)}, u32[]{:S(2)}) collective-permute-start(f32[24,256]{1,0:T(8,128)} %get-tuple-element.41), channel_id=1, source_target_pairs={{0,128},{32,160},{64,192},{96,224},{128,0},{160,32},{192,64},{224,... | collective-permute-start | bytes 73736 | tf_op jit(solution)/shard_map/ppermute | solution.py:362
  121.1 4.0 %collective-permute-start.8 = (f32[24,256]{1,0:T(8,128)}, f32[24,256]{1,0:T(8,128)S(1)}, u32[]{:S(2)}, u32[]{:S(2)}) collective-permute-start(f32[24,256]{1,0:T(8,128)} %get-tuple-element.42), channel_id=1, source_target_pairs={{0,64},{32,96},{64,0},{96,32},{128,192},{160,224},{192,128},{224,1... | collective-permute-start | bytes 73736 | tf_op jit(solution)/shard_map/ppermute | solution.py:362
  125.1 3.1 %collective-permute-start.9 = (f32[24,256]{1,0:T(8,128)}, f32[24,256]{1,0:T(8,128)S(1)}, u32[]{:S(2)}, u32[]{:S(2)}) collective-permute-start(f32[24,256]{1,0:T(8,128)} %get-tuple-element.43), channel_id=1, source_target_pairs={{0,32},{32,0},{64,96},{96,64},{128,160},{160,128},{192,224},{224,1... | collective-permute-start | bytes 73736 | tf_op jit(solution)/shard_map/ppermute | solution.py:362
  128.8 0.6 copy-done.8
  129.4 0.7 collective-permute-done.9.refs_5_
  130.2 0.6 copy-done.11
  130.8 3.0 %last.1 = f32[64,1536]{1,0:T(8,128)} custom-call(s32[1]{0:T(128)} %bitcast.me, s32[10,24]{1,0:T(8,128)} %remote.5, f32[32,24,256]{2,1,0:T(8,128)} %copy-done, f32[24,256]{1,0:T(8,128)} %get-tuple-element.36.refs_1_, f32[24,256]{1,0:T(8,128)} %get-tuple-element.37.refs_2_, f32[24,256]{1,0:T(8,128)} %copy-done.9, f32[24,256]{1,0:T(8,128)} %copy-done.10, ...), custom_call_target="tpu_custom_call" | custom-call | tf_op jit(solution)/shard_map/last/pallas_call | solution.py:318
  133.7 2.9 %all-to-all-done.2 = f32[32,1,384]{2,1,0:T(1,128)S(1)} async-done(((f32[32,1,384]{2,1,0:T(1,128)}), f32[32,1,384]{2,1,0:T(1,128)S(1)}, u32[]{:S(2)}, u32[]{:S(2)}) %all-to-all-start.2) | async-done | bytes 49184 | tf_op jit(solution)/shard_map/all_to_all | solution.py:398
  (46 shorter events, 2.9 us)
Async XLA Ops:
  5.1 53.4 %collective-permute-start = (f32[24,384]{1,0:T(8,128)}, f32[24,384]{1,0:T(8,128)S(1)}, u32[]{:S(2)}, u32[]{:S(2)}) collective-permute-start(f32[24,384]{1,0:T(8,128)} %get-tuple-element.25), channel_id=1, source_target_pairs={{0,512},{32,544},{64,576},{96,608},{128,640},{160,672},{192,704},{... | collective-permute-start | bytes 110600 | tf_op jit(solution)/shard_map/ppermute | solution.py:362
  34.6 8.2 %copy-start.15 = (f32[24,384]{1,0:T(8,128)S(1)}, f32[24,384]{1,0:T(8,128)}, u32[]{:S(2)}) copy-start(f32[24,384]{1,0:T(8,128)} %get-tuple-element.26) | copy-start | bytes 110596
  34.6 14.1 %copy-start.14 = (f32[24,384]{1,0:T(8,128)S(1)}, f32[24,384]{1,0:T(8,128)}, u32[]{:S(2)}) copy-start(f32[24,384]{1,0:T(8,128)} %get-tuple-element.27) | copy-start | bytes 110596
  34.6 18.1 %copy-start.13 = (f32[24,384]{1,0:T(8,128)S(1)}, f32[24,384]{1,0:T(8,128)}, u32[]{:S(2)}) copy-start(f32[24,384]{1,0:T(8,128)} %get-tuple-element.28) | copy-start | bytes 110596
  34.6 21.2 %copy-start.12 = (f32[24,384]{1,0:T(8,128)S(1)}, f32[24,384]{1,0:T(8,128)}, u32[]{:S(2)}) copy-start(f32[24,384]{1,0:T(8,128)} %get-tuple-element.29) | copy-start | bytes 110596
  34.6 26.6 %all-to-all-start = ((f32[32,24,384]{2,1,0:T(8,128)}), f32[32,24,384]{2,1,0:T(8,128)S(1)}, u32[]{:S(2)}, u32[]{:S(2)}) async-start(f32[32,24,384]{2,1,0:T(8,128)} %get-tuple-element.24), calls=%async_computation | async-start | bytes 2359296 | tf_op jit(solution)/shard_map/all_to_all | solution.py:365
  42.8 16.3 %collective-permute-start.1 = (f32[24,384]{1,0:T(8,128)S(1)}, f32[24,384]{1,0:T(8,128)S(1)}, u32[]{:S(2)}, u32[]{:S(2)}) collective-permute-start(f32[24,384]{1,0:T(8,128)S(1)} %copy-done.15), channel_id=1, source_target_pairs={{0,256},{32,288},{64,320},{96,352},{128,384},{160,416},{192,448},{... | collective-permute-start | bytes 110600 | tf_op jit(solution)/shard_map/ppermute | solution.py:362
  48.7 12.6 %collective-permute-start.2 = (f32[24,384]{1,0:T(8,128)S(1)}, f32[24,384]{1,0:T(8,128)S(1)}, u32[]{:S(2)}, u32[]{:S(2)}) collective-permute-start(f32[24,384]{1,0:T(8,128)S(1)} %copy-done.14), channel_id=1, source_target_pairs={{0,128},{32,160},{64,192},{96,224},{128,0},{160,32},{192,64},{224,... | collective-permute-start | bytes 110600 | tf_op jit(solution)/shard_map/ppermute | solution.py:362
  52.7 8.5 %collective-permute-start.3 = (f32[24,384]{1,0:T(8,128)S(1)}, f32[24,384]{1,0:T(8,128)S(1)}, u32[]{:S(2)}, u32[]{:S(2)}) collective-permute-start(f32[24,384]{1,0:T(8,128)S(1)} %copy-done.13), channel_id=1, source_target_pairs={{0,64},{32,96},{64,0},{96,32},{128,192},{160,224},{192,128},{224,1... | collective-permute-start | bytes 110600 | tf_op jit(solution)/shard_map/ppermute | solution.py:362
  55.8 5.4 %collective-permute-start.4 = (f32[24,384]{1,0:T(8,128)S(1)}, f32[24,384]{1,0:T(8,128)S(1)}, u32[]{:S(2)}, u32[]{:S(2)}) collective-permute-start(f32[24,384]{1,0:T(8,128)S(1)} %copy-done.12), channel_id=1, source_target_pairs={{0,32},{32,0},{64,96},{96,64},{128,160},{160,128},{192,224},{224,1... | collective-permute-start | bytes 110600 | tf_op jit(solution)/shard_map/ppermute | solution.py:362
  59.1 2.2 %copy-start.2 = (f32[24,384]{1,0:T(8,128)}, f32[24,384]{1,0:T(8,128)S(1)}, u32[]{:S(2)}) copy-start(f32[24,384]{1,0:T(8,128)S(1)} %collective-permute-done.1.refs_2_) | copy-start | bytes 110596
  61.3 1.0 copy-start.1
  70.9 9.1 %copy-start.17 = (f32[24,256]{1,0:T(8,128)S(1)}, f32[24,256]{1,0:T(8,128)}, u32[]{:S(2)}) copy-start(f32[24,256]{1,0:T(8,128)} %get-tuple-element.34) | copy-start | bytes 73732
  70.9 19.9 %copy-start.16 = (f32[24,256]{1,0:T(8,128)S(1)}, f32[24,256]{1,0:T(8,128)}, u32[]{:S(2)}) copy-start(f32[24,256]{1,0:T(8,128)} %get-tuple-element.35) | copy-start | bytes 73732
  71.0 23.3 %all-to-all-start.1 = ((f32[32,24,256]{2,1,0:T(8,128)}), f32[32,24,256]{2,1,0:T(8,128)S(1)}, u32[]{:S(2)}, u32[]{:S(2)}) async-start(f32[32,24,256]{2,1,0:T(8,128)} %get-tuple-element.33), calls=%async_computation.1 | async-start | bytes 1572864 | tf_op jit(solution)/shard_map/all_to_all | solution.py:365
  80.0 48.1 %collective-permute-start.5 = (f32[24,256]{1,0:T(8,128)S(1)}, f32[24,256]{1,0:T(8,128)S(1)}, u32[]{:S(2)}, u32[]{:S(2)}) collective-permute-start(f32[24,256]{1,0:T(8,128)S(1)} %copy-done.17), channel_id=1, source_target_pairs={{0,512},{32,544},{64,576},{96,608},{128,640},{160,672},{192,704},{... | collective-permute-start | bytes 73736 | tf_op jit(solution)/shard_map/ppermute | solution.py:362
  90.9 37.3 %collective-permute-start.6 = (f32[24,256]{1,0:T(8,128)S(1)}, f32[24,256]{1,0:T(8,128)S(1)}, u32[]{:S(2)}, u32[]{:S(2)}) collective-permute-start(f32[24,256]{1,0:T(8,128)S(1)} %copy-done.16), channel_id=1, source_target_pairs={{0,256},{32,288},{64,320},{96,352},{128,384},{160,416},{192,448},{... | collective-permute-start | bytes 73736 | tf_op jit(solution)/shard_map/ppermute | solution.py:362
  94.3 0.9 copy-start
  97.0 39.7 %all-to-all-start.2 = ((f32[32,1,384]{2,1,0:T(1,128)}), f32[32,1,384]{2,1,0:T(1,128)S(1)}, u32[]{:S(2)}, u32[]{:S(2)}) async-start(f32[32,1,384]{2,1,0:T(1,128)} %get-tuple-element.45), calls=%async_computation.2 | async-start | bytes 98304 | tf_op jit(solution)/shard_map/all_to_all | solution.py:398
  114.0 15.4 %collective-permute-start.7 = (f32[24,256]{1,0:T(8,128)}, f32[24,256]{1,0:T(8,128)S(1)}, u32[]{:S(2)}, u32[]{:S(2)}) collective-permute-start(f32[24,256]{1,0:T(8,128)} %get-tuple-element.41), channel_id=1, source_target_pairs={{0,128},{32,160},{64,192},{96,224},{128,0},{160,32},{192,64},{224,... | collective-permute-start | bytes 73736 | tf_op jit(solution)/shard_map/ppermute | solution.py:362
  121.1 8.3 %collective-permute-start.8 = (f32[24,256]{1,0:T(8,128)}, f32[24,256]{1,0:T(8,128)S(1)}, u32[]{:S(2)}, u32[]{:S(2)}) collective-permute-start(f32[24,256]{1,0:T(8,128)} %get-tuple-element.42), channel_id=1, source_target_pairs={{0,64},{32,96},{64,0},{96,32},{128,192},{160,224},{192,128},{224,1... | collective-permute-start | bytes 73736 | tf_op jit(solution)/shard_map/ppermute | solution.py:362
  125.1 5.1 %collective-permute-start.9 = (f32[24,256]{1,0:T(8,128)}, f32[24,256]{1,0:T(8,128)S(1)}, u32[]{:S(2)}, u32[]{:S(2)}) collective-permute-start(f32[24,256]{1,0:T(8,128)} %get-tuple-element.43), channel_id=1, source_target_pairs={{0,32},{32,0},{64,96},{96,64},{128,160},{160,128},{192,224},{224,1... | collective-permute-start | bytes 73736 | tf_op jit(solution)/shard_map/ppermute | solution.py:362
  129.4 0.8 copy-start.9
  129.4 0.8 copy-start.10
  (7 other events, 4.3 us)
